TPU v7x, 32 devices: a whole 2x2x4 slice. The times are simulated.
32 devices in a mesh: seq: 8 (over z, x), grp: 4 (over y, core).
Axes of the slice: x: 2, y: 2, z: 4, core: 2. Of those that a mesh axis runs over, the one named last changes fastest.
Arguments:
- tokens: bfloat16 [8, 4096, 768], P('grp', 'seq')
- seq_lengths: int32 [8], P('grp'), may hold values from 2048 to 4096, as said below
- answer_mask: int32 [8, 4096], P('grp', 'seq'), may hold values from 0 to 1, as said below
- out_grad: bfloat16 [8, 4096, 768], P('grp', 'seq'), may hold values from -6 to 6
- qkv_weight: float32 [768, 2304], P(('seq', 'grp')), may hold values from -0.21875 to 0.21875
- merge_weight: float32 [768, 768], P(('seq', 'grp')), may hold values from -0.875 to 0.875
- expand_weight: float32 [768, 3072], P(('seq', 'grp')), may hold values from -0.21875 to 0.21875
- shrink_weight: float32 [3072, 768], P(('seq', 'grp')), may hold values from -0.109375 to 0.109375
- small_params: float32 [768, 14], P(('seq', 'grp'))
- qkv_rows: float32 [768], P(('seq', 'grp')), may hold values from 3.5267696e-08 to 1.4107079e-07
- qkv_cols: float32 [2304], replicated, may hold values from 3.5267696e-08 to 1.4107079e-07
- merge_rows: float32 [768], P(('seq', 'grp')), may hold values from 3.5267696e-08 to 1.4107079e-07
- merge_cols: float32 [768], replicated, may hold values from 3.5267696e-08 to 1.4107079e-07
- expand_rows: float32 [768], P(('seq', 'grp')), may hold values from 3.5267696e-08 to 1.4107079e-07
- expand_cols: float32 [3072], replicated, may hold values from 3.5267696e-08 to 1.4107079e-07
- shrink_rows: float32 [3072], P(('seq', 'grp')), may hold values from 3.5267696e-08 to 1.4107079e-07
- shrink_cols: float32 [768], replicated, may hold values from 3.5267696e-08 to 1.4107079e-07
- small_moment: float32 [768, 14], P(('seq', 'grp')), may hold values from 3.5267696e-08 to 1.4107079e-07
Outputs:
- block_out: bfloat16 [8, 4096, 768], P('grp', 'seq')
- input_grad: float32 [8, 4096, 768], P('grp', 'seq')
- grad_norm: float32 [], replicated
- qkv_grad: float32 [768, 2304], P(('seq', 'grp'))
- qkv_rows_new: float32 [768], P(('seq', 'grp'))
- qkv_cols_new: float32 [2304], replicated
- qkv_new: float32 [768, 2304], P(('seq', 'grp'))
- qkv_low: bfloat16 [768, 2304], P(('seq', 'grp'))
- merge_grad: float32 [768, 768], P(('seq', 'grp'))
- merge_rows_new: float32 [768], P(('seq', 'grp'))
- merge_cols_new: float32 [768], replicated
- merge_new: float32 [768, 768], P(('seq', 'grp'))
- merge_low: bfloat16 [768, 768], P(('seq', 'grp'))
- expand_grad: float32 [768, 3072], P(('seq', 'grp'))
- expand_rows_new: float32 [768], P(('seq', 'grp'))
- expand_cols_new: float32 [3072], replicated
- expand_new: float32 [768, 3072], P(('seq', 'grp'))
- expand_low: bfloat16 [768, 3072], P(('seq', 'grp'))
- shrink_grad: float32 [3072, 768], P(('seq', 'grp'))
- shrink_rows_new: float32 [3072], P(('seq', 'grp'))
- shrink_cols_new: float32 [768], replicated
- shrink_new: float32 [3072, 768], P(('seq', 'grp'))
- shrink_low: bfloat16 [3072, 768], P(('seq', 'grp'))
- small_grad: float32 [768, 14], P(('seq', 'grp'))
- small_moment_new: float32 [768, 14], P(('seq', 'grp'))
- small_new: float32 [768, 14], P(('seq', 'grp'))
- small_low: bfloat16 [768, 14], P(('seq', 'grp'))
Inputs may be any that keep to these rules, and one draw needn't show every extreme that they name: `seq_lengths`: each group of 2 consecutive sequences holds one of length 4096. `answer_mask`: 1 on the positions of answer spans, 0 elsewhere.
All inputs are finite; a program needn't handle non-finite values.
Results may differ from a plain program's by a relative error of at most 0.015.
The roundings to bfloat16 on the way count: a program that leaves them out, or rounds other values in their place, can miss the bound.
Values may be sent and summed in bfloat16 or wider, within the bound.
No kernel may reach another device: no remote copies, remote signals or barrier semaphores. Data moves between devices by JAX's collectives and lax.ppermute only.
A program may use at most 256 MiB of HBM per device.

v0:
```python
import functools

import jax
import jax.numpy as jnp
from jax import lax
from jax.experimental import pallas as pl
from jax.experimental.pallas import tpu as pltpu
from jax.sharding import PartitionSpec as P

D = 768
HEAD_DIM = 64
FF = 3072
WIN = 64
PWIN = 64
TILE = 128
LANES = 128
NEAR = TILE + 2 * WIN
FAR = TILE // 4 + 2 * PWIN
GROUPS = D // LANES

EPS_NORM = 1e-05
EPS_FACTOR = 1e-30
DECAY = 0.5
RATE = 0.08
CLIP = 1.0
NEG = -1e30
BIG = 3e38
SCALE = HEAD_DIM ** (-0.5)

TAIL_STEP = 0.31
TAIL = (
    0.12367211422929353,
    0.12367030785161068,
    0.11185922254891491,
    0.08691510254396204,
    0.06423540557821411,
    -0.014525970624111314,
    0.08814037010576171,
    -0.154963171944524,
    0.08860162861073731,
    -0.017604979368020673,
)
INV_ROOT = 0.3989422804014327

F32 = jnp.float32
BF16 = jnp.bfloat16
CUT = 1280
TOGETHER = 3
BACK_TOGETHER = 2
VMEM_LIMIT = 60 * 1024 * 1024


def nn(left, right):
    return jnp.dot(left, right, preferred_element_type=F32)


def nt(left, right):
    return lax.dot_general(left, right, (((1,), (1,)), ((), ())), preferred_element_type=F32)


def outer(left, right):
    return lax.dot_general(left, right, (((0,), (0,)), ((), ())), preferred_element_type=F32)


def from_behind(value, axis, by):
    size = lax.axis_size(axis)
    pairs = [(i, i + by) for i in range(size) if 0 <= i + by < size]
    return lax.ppermute(value, axis, pairs)


def params(**extra):
    return pltpu.CompilerParams(vmem_limit_bytes=VMEM_LIMIT, **extra)


def cost(micros):
    return pl.CostEstimate(flops=int(micros * 8e8), bytes_accessed=0, transcendentals=0)


def fixed(shape):
    zeros = (0,) * len(shape)
    return pl.BlockSpec(shape, lambda *_: zeros, pipeline_mode=pl.Buffered(1))


def lanes_of(index, width=LANES):
    return slice(index * width, (index + 1) * width)


def near_cap(start, total, length, first):
    key = start - WIN + first + lax.broadcasted_iota(jnp.int32, (NEAR, TILE), 0)
    query = start + first + lax.broadcasted_iota(jnp.int32, (NEAR, TILE), 1)
    near = (jnp.abs(query - key) <= WIN) & (key >= 0) & (key < total)
    return jnp.where(near & ((key < length) | (key == query)), BIG, NEG)


def far_cap(start, total, length, first):
    pooled = start // 4 - PWIN + first // 4 + lax.broadcasted_iota(jnp.int32, (FAR, TILE), 0)
    coarse = (start + first + lax.broadcasted_iota(jnp.int32, (FAR, TILE), 1)) // 4
    far = (jnp.abs(coarse - pooled) <= PWIN) & (pooled >= 0) & (pooled < total // 4)
    return jnp.where(far & ((4 * pooled < length) | (pooled == coarse)), BIG, NEG)


def split_pair(pair):
    lane = lax.broadcasted_iota(jnp.int32, pair.shape, 1)
    zero = jnp.zeros_like(pair)
    return jnp.concatenate(
        [jnp.where(lane < HEAD_DIM, pair, zero), jnp.where(lane < HEAD_DIM, zero, pair)], axis=0
    )


LEVELS = ((0, NEAR), (NEAR, NEAR + FAR))


def join_pair(stacked):
    row = lax.broadcasted_iota(jnp.int32, (LANES, TILE), 0)
    return jnp.where(row < HEAD_DIM, stacked[:, :TILE], stacked[:, TILE:])


def project_kernel(
    info, beside, own, across, weight_a, weight_b, query, key, value, pool, rim_near, rim_across,
    vectors, wide,
):
    piece = own.shape[1]
    pools = piece // 4
    even = (info[0] // piece) % 2 == 0
    low = jnp.where(even, across[0], beside[0])
    high = jnp.where(even, beside[0], across[0])
    small = weight_b[:, 3 * D - CUT :].astype(F32).T
    vectors[...] = small[:16]
    taps = small[4:14]

    def weight_chunk(chunk):
        if chunk < CUT // 256:
            return weight_a[:, lanes_of(chunk, 256)]
        return weight_b[:, lanes_of(chunk - CUT // 256, 256)]

    for chunk in range(3):
        cols = lanes_of(chunk, 256)
        query[0, :, cols] = (nn(own[0], weight_chunk(chunk)) * SCALE).astype(BF16)
    for chunk in range(6):
        target = key if chunk < 3 else value
        cols = lanes_of(chunk % 3, 256)
        block = weight_chunk(3 + chunk)
        for source, base, count in ((low, 0, WIN), (own[0], WIN, piece), (high, WIN + piece, WIN)):
            rounded = nn(source, block).astype(BF16)
            held = rounded.astype(F32)
            wide[2 * chunk, base : base + count, :] = held[:, :LANES]
            wide[2 * chunk + 1, base : base + count, :] = held[:, LANES:]
            target[0, base : base + count, cols] = rounded
    for group in range(2 * GROUPS):
        part = group // GROUPS
        cols = lanes_of(group % GROUPS)
        pooled = None
        for tap in range(5):
            term = taps[5 * part + tap : 5 * part + tap + 1, cols] * wide[
                group, pl.ds(WIN - 2 + tap, pools, stride=4), :
            ]
            pooled = term if pooled is None else pooled + term
        pooled = pooled.astype(BF16)
        pool[0, part, :, cols] = pooled
        first, last = (pooled[:PWIN], pooled[pools - PWIN :])
        rim_near[0, part, :, cols] = jnp.where(even, last, first)
        rim_across[0, part, :, cols] = jnp.where(even, first, last)


def level_mixed(queries, keys, values, cap, lse, tile, pairs):
    heads = [(at, head) for at in range(len(pairs)) for head in range(2)]
    scores = [nt(keys[at], queries[at][head * TILE : (head + 1) * TILE]) for at, head in heads]
    scores = [jnp.minimum(entry, cap[...]) for entry in scores]
    tops = [jnp.max(entry, axis=0, keepdims=True) for entry in scores]
    raised = [jnp.exp(entry - top) for entry, top in zip(scores, tops)]
    norms = [jnp.sum(entry, axis=0, keepdims=True) for entry in raised]
    for (at, head), top, norm in zip(heads, tops, norms):
        lse[0, tile, pairs[at] : pairs[at] + 1, lanes_of(head)] = top + jnp.log(norm)
    probs = [(entry * (1.0 / norm)).astype(BF16) for entry, norm in zip(raised, norms)]
    turned = [entry.T for entry in values]
    mixed = [
        nn(entry, jnp.concatenate(probs[2 * at : 2 * at + 2], axis=1)) for at, entry in enumerate(turned)
    ]
    return [join_pair(entry).T for entry in mixed]


def near_kernel(info, query, key, value, mixed, lse, cap):
    piece = query.shape[1]
    which = pl.program_id(0)
    start, total, length = (info[0], info[1], info[2 + which])

    def tile_step(tile, carry):
        first = pl.multiple_of(tile * TILE, TILE)
        cap[...] = near_cap(start, total, length, first)
        for begin in range(0, GROUPS, TOGETHER):
            pairs = range(begin, begin + TOGETHER)
            queries = [split_pair(query[0, pl.ds(first, TILE), lanes_of(pair)]) for pair in pairs]
            keys = [key[0, pl.ds(first, NEAR), lanes_of(pair)] for pair in pairs]
            values = [value[0, pl.ds(first, NEAR), lanes_of(pair)] for pair in pairs]
            parts = level_mixed(queries, keys, values, cap, lse, tile, pairs)
            for pair, part in zip(pairs, parts):
                mixed[0, pl.ds(first, TILE), lanes_of(pair)] = part
        return carry

    lax.fori_loop(0, piece // TILE, tile_step, 0)


def far_kernel(info, query, pool, beside, across, mixed, att, pkey, pvalue, lse, cap):
    piece = query.shape[1]
    pools = piece // 4
    which = pl.program_id(0)
    start, total, length = (info[0], info[1], info[2 + which])
    even = (start // piece) % 2 == 0
    for part, target in enumerate((pkey, pvalue)):
        target[0, :PWIN, :] = jnp.where(even, across[0, part], beside[0, part])
        target[0, PWIN : PWIN + pools, :] = pool[0, part]
        target[0, PWIN + pools :, :] = jnp.where(even, beside[0, part], across[0, part])

    def tile_step(tile, carry):
        first = pl.multiple_of(tile * TILE, TILE)
        coarse = pl.multiple_of(tile * (TILE // 4), TILE // 4)
        cap[...] = far_cap(start, total, length, first)
        for begin in range(0, GROUPS, TOGETHER):
            pairs = range(begin, begin + TOGETHER)
            queries = [split_pair(query[0, pl.ds(first, TILE), lanes_of(pair)]) for pair in pairs]
            keys = [pkey[0, pl.ds(coarse, FAR), lanes_of(pair)] for pair in pairs]
            values = [pvalue[0, pl.ds(coarse, FAR), lanes_of(pair)] for pair in pairs]
            parts = level_mixed(queries, keys, values, cap, lse, tile, pairs)
            for pair, part in zip(pairs, parts):
                place = (0, pl.ds(first, TILE), lanes_of(pair))
                att[place] = (mixed[place] + part).astype(BF16)
        return carry

    lax.fori_loop(0, piece // TILE, tile_step, 0)


def per_seq(body, operands, shapes, micros, name, shared=0, common=(), scratch=()):
    info, *rest = operands
    seqs = rest[0].shape[0]
    split = len(rest) - shared

    def seq_block(shape):
        return pl.BlockSpec((1,) + tuple(shape), lambda s: (s,) + (0,) * len(shape))

    return pl.pallas_call(
        body,
        grid=(seqs,),
        in_specs=[pl.BlockSpec(memory_space=pltpu.SMEM)]
        + [seq_block(entry.shape[1:]) for entry in rest[:split]]
        + [fixed(entry.shape) for entry in rest[split:]],
        out_specs=[seq_block(shape) for shape, _ in shapes]
        + [pl.BlockSpec(shape, lambda s: (0,) * len(shape)) for shape, _ in common],
        out_shape=[jax.ShapeDtypeStruct((seqs,) + shape, dtype) for shape, dtype in shapes]
        + [jax.ShapeDtypeStruct(shape, dtype) for shape, dtype in common],
        scratch_shapes=list(scratch),
        compiler_params=params(),
        cost_estimate=cost(micros),
        name=name,
    )(*operands)


def project(info, beside, own, across, weight_a, weight_b):
    _, piece, width = own.shape
    extent, pools = (piece + 2 * WIN, piece // 4)
    return per_seq(
        project_kernel,
        (info, beside, own, across, weight_a, weight_b),
        [
            ((piece, width), BF16),
            ((extent, width), BF16),
            ((extent, width), BF16),
            ((2, pools, width), BF16),
            ((2, PWIN, width), BF16),
            ((2, PWIN, width), BF16),
        ],
        10,
        "project",
        shared=2,
        common=[((16, width), F32)],
        scratch=[pltpu.VMEM((2 * GROUPS, extent, LANES), F32)],
    )


def near_attend(info, query, key, value):
    _, piece, width = query.shape
    return per_seq(
        near_kernel,
        (info, query, key, value),
        [((piece, width), F32), ((piece // TILE, 8, 2 * TILE), F32)],
        30,
        "near",
        scratch=[pltpu.VMEM((NEAR, TILE), F32)],
    )


def far_attend(info, query, pool, beside, across, mixed):
    _, piece, width = query.shape
    pools = piece // 4 + 2 * PWIN
    return per_seq(
        far_kernel,
        (info, query, pool, beside, across, mixed),
        [
            ((piece, width), BF16),
            ((pools, width), BF16),
            ((pools, width), BF16),
            ((piece // TILE, 8, 2 * TILE), F32),
        ],
        12,
        "far",
        scratch=[pltpu.VMEM((FAR, TILE), F32)],
    )


def layer_stats(values):
    centred = values - jnp.mean(values, axis=-1, keepdims=True)
    inverse = lax.rsqrt(jnp.mean(centred * centred, axis=-1, keepdims=True) + EPS_NORM)
    return (centred * inverse, inverse)


def layer_back(grad, normed, inverse):
    return inverse * (
        grad
        - jnp.mean(grad, axis=-1, keepdims=True)
        - normed * jnp.mean(grad * normed, axis=-1, keepdims=True)
    )


def gelu_parts(up):
    size = jnp.abs(up)
    bell = jnp.exp(-0.5 * (up * up))
    near = 1.0 / (1.0 + TAIL_STEP * size)
    poly = jnp.full_like(up, TAIL[-1])
    for factor in TAIL[-2::-1]:
        poly = poly * near + factor
    tail = bell * (near * poly)
    phi = jnp.where(up >= 0.0, 1.0 - tail, tail)
    return (up * phi, phi + up * (bell * INV_ROOT))


def feed_kernel(
    tokens, att, cot, packed, vectors, block_out, first_grad, hidden_low, active,
    up_grad, branch_grad, mixed_grad, att_grad, sums, slope,
):
    step = pl.program_id(0)
    gain_one, bias_one, gain_two, bias_two = [vectors[i : i + 1, :] for i in range(4)]
    def merge():
        return packed[:, :D]

    def expand(chunk):
        return packed[:, lanes_of(1 + chunk, D)]

    def shrink(chunk):
        return packed[:, lanes_of(1 + FF // D + chunk, D)]

    first_norm, first_inv = layer_stats(tokens[...].astype(F32) + nn(att[...], merge()))
    hidden = first_norm * gain_one + bias_one
    low = hidden.astype(BF16)
    hidden_low[...] = low
    branch = None
    for chunk in range(FF // D):
        cols = lanes_of(chunk, D)
        wide, steep = gelu_parts(nn(low, expand(chunk)))
        narrow = wide.astype(BF16)
        active[:, cols] = narrow
        slope[:, cols] = steep
        term = nn(narrow, shrink(chunk))
        branch = term if branch is None else branch + term
    second_norm, second_inv = layer_stats(hidden + branch)
    block_out[...] = (second_norm * gain_two + bias_two).astype(BF16)
    cotangent = cot[...].astype(F32)

    @pl.when(step == 0)
    def clear():
        sums[...] = jnp.zeros_like(sums)

    def add_sum(row, value):
        sums[row : row + 1, :] += jnp.sum(value, axis=0, keepdims=True)

    add_sum(2, cotangent * second_norm)
    add_sum(3, cotangent)
    second_grad = layer_back(cotangent * gain_two, second_norm, second_inv)
    second_low = second_grad.astype(BF16)
    branch_grad[...] = second_low
    feed = None
    for chunk in range(FF // D):
        cols = lanes_of(chunk, D)
        narrow = (nt(second_low, shrink(chunk)) * slope[:, cols]).astype(BF16)
        up_grad[:, cols] = narrow
        term = nt(narrow, expand(chunk))
        feed = term if feed is None else feed + term
    hidden_grad = second_grad + feed.astype(BF16).astype(F32)
    add_sum(0, hidden_grad * first_norm)
    add_sum(1, hidden_grad)
    grad = layer_back(hidden_grad * gain_one, first_norm, first_inv)
    first_grad[...] = grad
    grad_low = grad.astype(BF16)
    mixed_grad[...] = grad_low
    att_grad[...] = nt(grad_low, merge()).astype(BF16)


def feed(tokens, att, cot, packed, vectors):
    rows, width = tokens.shape
    block = 256
    ff = FF

    def row_block(cols):
        return pl.BlockSpec((block, cols), lambda i: (i, 0))

    outs = [
        (width, BF16),
        (width, F32),
        (width, BF16),
        (ff, BF16),
        (ff, BF16),
        (width, BF16),
        (width, BF16),
        (width, BF16),
    ]
    return pl.pallas_call(
        feed_kernel,
        grid=(rows // block,),
        in_specs=[row_block(width)] * 3
        + [fixed(packed.shape), fixed(vectors.shape)],
        out_specs=[row_block(cols) for cols, _ in outs] + [pl.BlockSpec((8, width), lambda i: (0, 0))],
        out_shape=[jax.ShapeDtypeStruct((rows, cols), dtype) for cols, dtype in outs]
        + [jax.ShapeDtypeStruct((8, width), F32)],
        scratch_shapes=[pltpu.VMEM((block, ff), F32)],
        compiler_params=params(),
        cost_estimate=cost(48),
        name="feed",
    )(tokens, att, cot, packed, vectors)


def back_kernel(
    which, info, query, key, value, pkey, pvalue, grad, near_lse, far_lse, query_grad, near_grad,
    far_grad, rim_near, rim_across, caps,
):
    piece = query.shape[1]
    even = (info[0] // piece) % 2 == 0
    start, total, length = (info[0], info[1], info[2 + which])
    near_grad[...] = jnp.zeros_like(near_grad)
    far_grad[...] = jnp.zeros_like(far_grad)

    def tile_step(tile, carry):
        first = pl.multiple_of(tile * TILE, TILE)
        coarse = pl.multiple_of(tile * (TILE // 4), TILE // 4)
        for cap, (begin, end) in zip((near_cap, far_cap), LEVELS):
            block = cap(start, total, length, first)
            caps[begin:end, :TILE] = block
            caps[begin:end, TILE:] = block
        near_rows, far_rows = (pl.ds(first, NEAR), pl.ds(coarse, FAR))
        place = pl.ds(first, TILE)
        for start_pair in range(0, GROUPS, BACK_TOGETHER):
            pairs = range(start_pair, start_pair + BACK_TOGETHER)
            many = range(BACK_TOGETHER)
            spans = [lanes_of(pair) for pair in pairs]
            queries = [split_pair(query[0, place, cols]) for cols in spans]
            grads = [split_pair(grad[0, place, cols]) for cols in spans]
            keys = [
                jnp.concatenate([key[0, near_rows, cols], pkey[0, far_rows, cols]], axis=0)
                for cols in spans
            ]
            values = [
                jnp.concatenate([value[0, near_rows, cols], pvalue[0, far_rows, cols]], axis=0)
                for cols in spans
            ]
            scores = [nt(keys[at], queries[at]) for at in many]
            prob_grads = [nt(values[at], grads[at]) for at in many]
            probs = [[] for _ in many]
            score_grads = [[] for _ in many]
            for level, (begin, end) in enumerate(LEVELS):
                lse = (near_lse, far_lse)[level]
                exact_probs = [
                    jnp.exp(
                        jnp.minimum(scores[at][begin:end], caps[begin:end, :])
                        - lse[0, tile, pairs[at] : pairs[at] + 1, :]
                    )
                    for at in many
                ]
                weighted = [exact_probs[at] * prob_grads[at][begin:end] for at in many]
                inner = [jnp.sum(entry, axis=0, keepdims=True) for entry in weighted]
                for at in many:
                    score_grads[at].append((weighted[at] - exact_probs[at] * inner[at]).astype(BF16))
                    probs[at].append(exact_probs[at].astype(BF16))
            score_grads = [jnp.concatenate(entry, axis=0) for entry in score_grads]
            key_parts = [nn(score_grads[at], queries[at]) for at in many]
            value_parts = [nn(jnp.concatenate(probs[at], axis=0), grads[at]) for at in many]
            turned = [entry.T for entry in keys]
            query_parts = [nn(turned[at], score_grads[at]) for at in many]
            for at, cols in enumerate(spans):
                near_grad[0, 0, near_rows, cols] += key_parts[at][:NEAR]
                far_grad[0, 0, far_rows, cols] += key_parts[at][NEAR:]
                near_grad[0, 1, near_rows, cols] += value_parts[at][:NEAR]
                far_grad[0, 1, far_rows, cols] += value_parts[at][NEAR:]
                query_grad[0, place, cols] = (join_pair(query_parts[at]) * SCALE).T.astype(BF16)
        return carry

    lax.fori_loop(0, piece // TILE, tile_step, 0)
    pools = far_grad.shape[2]
    blank = jnp.zeros((16, far_grad.shape[3]), BF16)
    for part in range(2):
        low = [near_grad[0, part, :WIN, :], far_grad[0, part, : PWIN + 16, :]]
        low = [entry.astype(BF16) for entry in low]
        high = [near_grad[0, part, WIN + piece :, :], far_grad[0, part, pools - PWIN :, :]]
        high = [entry.astype(BF16) for entry in high]

        @pl.when(even)
        def even_side():
            rim_near[0, part, :WIN, :] = high[0]
            rim_near[0, part, WIN : WIN + PWIN, :] = high[1]
            rim_near[0, part, WIN + PWIN :, :] = blank
            rim_across[0, part, :WIN, :] = low[0]
            rim_across[0, part, WIN:, :] = low[1]

        @pl.when(jnp.logical_not(even))
        def odd_side():
            rim_across[0, part, :WIN, :] = high[0]
            rim_across[0, part, WIN : WIN + PWIN, :] = high[1]
            rim_across[0, part, WIN + PWIN :, :] = blank
            rim_near[0, part, :WIN, :] = low[0]
            rim_near[0, part, WIN:, :] = low[1]


def seq_slice(shape, which):
    return pl.BlockSpec((1,) + tuple(shape[1:]), lambda _: (which,) + (0,) * (len(shape) - 1))


def back(which, info, query, key, value, pkey, pvalue, grad, near_lse, far_lse):
    _, piece, width = query.shape
    extent, pools = (key.shape[1], pkey.shape[1])
    operands = (query, key, value, pkey, pvalue, grad, near_lse, far_lse)
    shapes = [
        ((1, piece, width), BF16),
        ((1, 2, extent, width), F32),
        ((1, 2, pools, width), F32),
        ((1, 2, WIN + PWIN + 16, width), BF16),
        ((1, 2, WIN + PWIN + 16, width), BF16),
    ]
    return pl.pallas_call(
        functools.partial(back_kernel, which),
        grid=(1,),
        in_specs=[pl.BlockSpec(memory_space=pltpu.SMEM)]
        + [seq_slice(entry.shape, which) for entry in operands],
        out_specs=[seq_slice(shape, 0) for shape, _ in shapes],
        out_shape=[jax.ShapeDtypeStruct(shape, dtype) for shape, dtype in shapes],
        scratch_shapes=[pltpu.VMEM((NEAR + FAR, 2 * TILE), F32)],
        compiler_params=params(),
        cost_estimate=cost(0.01 if which else 30),
        name="back",
    )(info, *operands)


def pool_back_kernel(
    first, last, info, query_grad, near_grad, far_grad, beside, across, key, value, taps, turned, *rest
):
    rest = list(rest)
    before, taps_before = (None, None) if first else (rest.pop(0), rest.pop(0))
    sums = rest.pop(0) if last else None
    full_grad = rest.pop(0)
    outs = [rest.pop(0), rest.pop(0)]
    held, spread, window, taps_grad = rest
    piece = full_grad.shape[1]
    pools = piece // 4
    even = (info[0] // piece) % 2 == 0
    full_grad[0, :, :D] = query_grad[0]
    if first:
        taps_grad[...] = jnp.zeros_like(taps_grad)
    else:
        taps_grad[...] = taps_before[...]

    def product(chunk):
        cols = lanes_of(chunk, 256)
        total = nn(turned[...], full_grad[0, :, cols])
        if not first:
            total = total + before[:, cols]
        if not last:
            outs[0][:, cols] = total
        elif chunk < CUT // 256:
            outs[0][:, cols] = total.astype(BF16)
        else:
            outs[1][:, lanes_of(chunk - CUT // 256, 256)] = total.astype(BF16)

    for group in range(2 * GROUPS):
        if group % 4 == 0:
            product(group // 4)
        part = group // GROUPS
        cols = lanes_of(group % GROUPS)
        source = key if part == 0 else value
        pair = [entry[0, part, :, cols].astype(F32) for entry in (beside, across)]
        from_high = jnp.where(even, pair[0], pair[1])
        from_low = jnp.where(even, pair[1], pair[0])
        tap = [taps[4 + 5 * part + t : 5 + 5 * part + t, cols] for t in range(5)]
        held[0:pools, :] = far_grad[0, part, PWIN : PWIN + pools, cols]
        held[0:PWIN, :] += from_low[WIN : WIN + PWIN]
        held[pools - PWIN : pools, :] += from_high[WIN : WIN + PWIN]
        held[pools : pools + 16, :] = (
            far_grad[0, part, PWIN + pools : PWIN + pools + 16, cols] + from_high[WIN + PWIN :]
        )
        now = held[0:pools, :]
        later = held[1 : pools + 1, :]
        spread[pl.ds(0, pools, stride=4), :] = tap[2] * now
        spread[pl.ds(1, pools, stride=4), :] = tap[3] * now
        spread[pl.ds(2, pools, stride=4), :] = tap[4] * now + tap[0] * later
        spread[pl.ds(3, pools, stride=4), :] = tap[1] * later
        spread[0:WIN, :] += from_low[:WIN]
        spread[piece - WIN : piece, :] += from_high[:WIN]
        total = near_grad[0, part, WIN : WIN + piece, cols] + spread[...]
        full_grad[0, :, lanes_of(GROUPS + group)] = total.astype(BF16)
        window[...] = source[0, WIN - 16 : WIN + piece + 16, cols].astype(F32)
        for t in range(5):
            row = 5 * part + t
            taps_grad[row : row + 1, cols] += jnp.sum(
                now * window[pl.ds(14 + t, pools, stride=4), :], axis=0, keepdims=True
            )
        if group % 2 == 1:
            product((GROUPS + group) // 2)
    if last:
        zeros = jnp.zeros((LANES - 14, D), F32)
        small = jnp.concatenate([sums[0:4, :], taps_grad[0:10, :], zeros], axis=0)
        outs[1][:, 3 * D - CUT :] = small.T.astype(BF16)
    else:
        outs[1][...] = taps_grad[...]


def pool_back(which, seqs, info, entries, key, value, taps, turned, before, sums):
    near_grad = entries[1]
    _, _, extent, width = near_grad.shape
    piece = extent - 2 * WIN
    pools = piece // 4
    first, last = (which == 0, which == seqs - 1)
    extra = (() if first else tuple(before)) + ((sums,) if last else ())
    if last:
        outs = [((width, CUT), BF16), ((width, 3 * width + LANES - CUT), BF16)]
    else:
        outs = [((width, 3 * width), F32), ((16, width), F32)]
    return pl.pallas_call(
        functools.partial(pool_back_kernel, first, last),
        grid=(1,),
        in_specs=[pl.BlockSpec(memory_space=pltpu.SMEM)]
        + [seq_slice(entry.shape, 0) for entry in entries]
        + [seq_slice(entry.shape, which) for entry in (key, value)]
        + [fixed(taps.shape), pl.BlockSpec((width, piece), lambda _: (0, which))]
        + [fixed(entry.shape) for entry in extra],
        out_specs=[seq_slice((1, piece, 3 * width), 0)] + [fixed(shape) for shape, _ in outs],
        out_shape=[jax.ShapeDtypeStruct((1, piece, 3 * width), BF16)]
        + [jax.ShapeDtypeStruct(shape, dtype) for shape, dtype in outs],
        scratch_shapes=[
            pltpu.VMEM((pools + 16, LANES), F32),
            pltpu.VMEM((piece, LANES), F32),
            pltpu.VMEM((piece + 32, LANES), F32),
            pltpu.VMEM((16, width), F32),
        ],
        compiler_params=params(),
        cost_estimate=cost(0.01 if which else 30),
        name="pool_back",
    )(info, *entries, key, value, taps, turned, *extra)


def unmix(width):
    row = lax.broadcasted_iota(jnp.int32, (4 * width, 4 * width), 0)
    col = lax.broadcasted_iota(jnp.int32, (4 * width, 4 * width), 1)
    return jnp.where(row == 4 * (col % width) + col // width, 1.0, 0.0)


def exact(left, right):
    return jnp.dot(left, right, precision=lax.Precision.HIGHEST, preferred_element_type=F32)


def exact_nt(left, right):
    return lax.dot_general(
        left, right, (((1,), (1,)), ((), ())), precision=lax.Precision.HIGHEST, preferred_element_type=F32
    )


def pack_kernel(merge, expand, shrink, out, held):
    rows = merge.shape[0]
    mixer = unmix(LANES).astype(BF16)
    out[:, :D] = merge[...].astype(BF16)
    for group in range(FF // (4 * LANES)):
        block = nn(expand[:, lanes_of(group, 4 * LANES)].astype(BF16), mixer).astype(BF16)
        for j in range(4):
            first = D + j * D + group * LANES
            out[:, first : first + LANES] = block[:, lanes_of(j)]
    for group in range(GROUPS):
        held[group] = shrink[:, lanes_of(group)]
        for j in range(4):
            first = (5 + j) * D + group * LANES
            out[:, first : first + LANES] = held[group, pl.ds(j, rows, stride=4), :].astype(BF16)


def squares(block):
    return jnp.sum(block * block, axis=0, keepdims=True)


def late_kernel(late, *rest):
    olds, (out, expand, shrink, held) = (rest[:4], rest[4:])
    rows = late.shape[0]
    mixer = unmix(LANES).astype(BF16)
    for group in range(FF // (4 * LANES)):
        pieces = []
        for j in range(4):
            first = (5 + j) * D + group * LANES
            pieces.append(late[:, first : first + LANES])
        left = jnp.concatenate(pieces, axis=1)
        total = None
        for _ in range(3):
            top = left.astype(BF16)
            left = left - top.astype(F32)
            term = nt(top, mixer)
            total = term if total is None else total + term
        expand[:, lanes_of(group, 4 * LANES)] = total
    for group in range(GROUPS):
        for j in range(4):
            held[group, pl.ds(j, rows, stride=4), :] = late[:, lanes_of(j * GROUPS + group)]
        shrink[:, lanes_of(group)] = held[group]
    out[:, : 3 * D] = jnp.zeros((1, 3 * D), F32)
    out[:, 3 * D : 4 * D] = squares(late[:, 4 * D : 5 * D])
    for j in range(FF // D):
        out[:, (4 + j) * D : (5 + j) * D] = squares(expand[:, lanes_of(j, D)])
    out[:, 8 * D : 9 * D] = squares(shrink[...])
    lane = lax.broadcasted_iota(jnp.int32, (1, LANES), 1)
    tail = jnp.zeros((1, LANES), F32)
    for slot, entry in enumerate(olds):
        tail = jnp.where(lane == slot + 1, jnp.sum(entry[...], axis=1, keepdims=True), tail)
    out[:, 9 * D :] = tail


def stats_kernel(early, base, out):
    out[:, : 3 * D] = squares(early[:, : 3 * D])
    out[:, 3 * D : 9 * D] = base[:, 3 * D : 9 * D]
    lane = lax.broadcasted_iota(jnp.int32, (1, LANES), 1)
    small = jnp.sum(squares(early[:, 3 * D :]), axis=1, keepdims=True)
    out[:, 9 * D :] = base[:, 9 * D :] + jnp.where(lane == 0, small, 0.0)


def update_kernel(
    total, early, late, expand, shrink, rows_0, rows_1, rows_2, rows_3, cols_0, cols_1,
    cols_2, cols_3, weight_0, weight_1, weight_2, weight_3, small, moment,
    norm_out, grad_0, rows_new_0, cols_new_0, new_0, low_0, grad_1, rows_new_1, cols_new_1, new_1,
    low_1, grad_2, rows_new_2, cols_new_2, new_2, low_2, grad_3, rows_new_3, cols_new_3, new_3,
    low_3, small_grad, moment_new, small_new, small_low,
):
    smalls = small.shape[0]
    tail = total[:, 9 * D :]
    spans = ((0, 3 * D), (3 * D, 4 * D), (4 * D, 8 * D), (8 * D, 9 * D))
    matrix_sums = [jnp.sum(total[:, a:b], axis=1, keepdims=True) for a, b in spans]
    norm = jnp.sqrt(matrix_sums[0] + matrix_sums[1] + matrix_sums[2] + matrix_sums[3] + tail[:, 0:1])
    clip = CLIP / jnp.maximum(norm, CLIP)
    norm_out[...] = norm
    parts = (
        [early[:, lanes_of(j, D)] for j in range(3)],
        [late[:, 4 * D : 5 * D]],
        [expand[:, lanes_of(j, D)] for j in range(FF // D)],
        [shrink[...]],
    )
    heights = (D, D, D, FF)
    olds = (
        (rows_0, cols_0, weight_0, grad_0, rows_new_0, cols_new_0, new_0, low_0),
        (rows_1, cols_1, weight_1, grad_1, rows_new_1, cols_new_1, new_1, low_1),
        (rows_2, cols_2, weight_2, grad_2, rows_new_2, cols_new_2, new_2, low_2),
        (rows_3, cols_3, weight_3, grad_3, rows_new_3, cols_new_3, new_3, low_3),
    )
    for index in range(4):
        old_rows, old_cols, weight, grad, rows_new, cols_new, new, low = olds[index]
        begin, end = spans[index]
        width, height = (end - begin, heights[index])
        mean_cols = (total[:, begin:end] * clip) * clip / height + EPS_FACTOR
        fresh_cols = DECAY * old_cols[...] + (1.0 - DECAY) * mean_cols
        for group in range(width // LANES):
            cols_new[group : group + 1, :] = fresh_cols[:, lanes_of(group)]
        squared = sum(part * part for part in parts[index])
        row_sum = exact_nt(jnp.ones((8, D), F32), squared)[:1]
        mean_rows = (row_sum * clip) * clip / width + EPS_FACTOR
        fresh_rows = DECAY * old_rows[...] + (1.0 - DECAY) * mean_rows
        rows_new[...] = fresh_rows
        row = lax.broadcasted_iota(jnp.int32, (weight.shape[0], weight.shape[0]), 0)
        col = lax.broadcasted_iota(jnp.int32, (weight.shape[0], weight.shape[0]), 1)
        down = jnp.sum(jnp.where(row == col, fresh_rows, 0.0), axis=1, keepdims=True)
        mean_all = (matrix_sums[index] * clip) * clip / (width * height) + EPS_FACTOR
        row_mean = DECAY * (tail[:, 1 + index : 2 + index] / height) + (1.0 - DECAY) * mean_all
        for j, part in enumerate(parts[index]):
            cols = lanes_of(j, D)
            clipped = part * clip
            grad[:, cols] = clipped
            estimate = down * fresh_cols[:, cols] / row_mean
            fresh = weight[:, cols] - RATE * clipped * lax.rsqrt(estimate)
            new[:, cols] = fresh
            low[:, cols] = fresh.astype(BF16)
    row = lax.broadcasted_iota(jnp.int32, (16, LANES), 0)
    col = lax.broadcasted_iota(jnp.int32, (16, LANES), 1)
    turned = exact_nt(jnp.where(row == col, 1.0, 0.0), early[:, 3 * D :])
    clipped = turned[:smalls] * clip
    small_grad[...] = clipped
    fresh_moment = DECAY * moment[...] + (1.0 - DECAY) * (clipped * clipped + EPS_FACTOR)
    moment_new[...] = fresh_moment
    fresh = small[...] - RATE * clipped * lax.rsqrt(fresh_moment)
    small_new[...] = fresh
    small_low[...] = fresh.astype(BF16)


def whole_call(body, outs, operands, name, micros, scratch=()):
    return pl.pallas_call(
        body,
        out_shape=[jax.ShapeDtypeStruct(shape, dtype) for shape, dtype in outs],
        in_specs=[pl.BlockSpec(memory_space=pltpu.VMEM)] * len(operands),
        out_specs=[pl.BlockSpec(memory_space=pltpu.VMEM)] * len(outs),
        scratch_shapes=list(scratch),
        compiler_params=params(),
        cost_estimate=cost(micros),
        name=name,
    )(*operands)


def swap(value, axis, bit):
    size = lax.axis_size(axis)
    return lax.ppermute(value, axis, [(i, i ^ (1 << bit)) for i in range(size)])


def bits_of(axis):
    return lax.axis_size(axis).bit_length() - 1


def side(axis, bit):
    return (lax.axis_index(axis) >> bit) & 1


def doubled(value, axis, bit, dim):
    other = swap(value, axis, bit)
    mine = side(axis, bit)
    return jnp.where(
        mine == 0, jnp.stack([value, other], axis=dim), jnp.stack([other, value], axis=dim)
    )


def halves(value, axis, bit, dim):
    mine = side(axis, bit)
    away = lax.dynamic_index_in_dim(value, 1 - mine, dim, keepdims=False)
    return [lax.dynamic_index_in_dim(value, mine, dim, keepdims=False), swap(away, axis, bit)]


def quarters(value, axis, bit, dim):
    size = lax.axis_size(axis)
    mine = (lax.axis_index(axis) >> bit) & 3
    value = value.reshape(value.shape[:dim] + (4,) + value.shape[dim + 2 :])
    blocks = [lax.dynamic_index_in_dim(value, mine, dim, keepdims=False)]
    for step in range(1, 4):
        away = lax.dynamic_index_in_dim(value, mine ^ step, dim, keepdims=False)
        blocks.append(lax.ppermute(away, axis, [(i, i ^ (step << bit)) for i in range(size)]))
    return blocks


def added(blocks, dtype):
    return sum(block.astype(F32) for block in blocks).astype(dtype)


def place_of(done, step):
    return sum(1 for other in done if other > step)


def order_key(axis, bit):
    return (1 if axis == "seq" else 0, bit)


def gather_pairs(value, steps):
    done = []
    for axis, bit in steps:
        at = order_key(axis, bit)
        value = doubled(value, axis, bit, place_of(done, at))
        done.append(at)
    return (value, done)


def scatter_begin(value, steps, lead=0):
    left = [(axis, bit + k) for axis, bit, count in steps for k in range(count)]
    left = sorted((order_key(axis, bit) for axis, bit in left), reverse=True)
    value = value.reshape(value.shape[:lead] + (2,) * len(left) + value.shape[lead + 1 :])
    return (value, left, list(steps), lead)


def scatter_step(state, gate=None):
    value, left, steps, lead = state
    axis, bit, count = steps[0]
    gone = [order_key(axis, bit + k) for k in range(count)]
    dtype = F32 if len(steps) == 1 else BF16
    dim = lead + min(left.index(entry) for entry in gone)
    blocks = (halves if count == 1 else quarters)(value, axis, bit, dim)
    if gate is not None:
        blocks, _ = lax.optimization_barrier((blocks, gate))
    value = added(blocks, dtype)
    return (value, [other for other in left if other not in gone], steps[1:], lead)


def scatter_end(state, gate=None):
    while state[2]:
        state = scatter_step(state, gate)
    return state[0]


def after(states, values):
    blocks, values = lax.optimization_barrier(([state[0] for state in states], values))
    return ([(block,) + tuple(state[1:]) for block, state in zip(blocks, states)], values)


def gather_far(shard):
    steps = [("seq", bit) for bit in reversed(range(1, bits_of("seq")))]
    return gather_pairs(shard, steps)


def gather_near(part, done, first):
    side_bits = [("grp", bit) for bit in range(1, bits_of("grp"))]
    middle = [("seq", 0)] + side_bits if first == "seq" else side_bits + [("seq", 0)]
    done = list(done)
    for axis, bit in middle + [("grp", 0)]:
        at = order_key(axis, bit)
        part = doubled(part, axis, bit, place_of(done, at))
        done.append(at)
    return part.reshape(-1, part.shape[-1])


def near_swap(even, odd):
    mine = side("seq", 0)
    return swap(jnp.where(mine == 0, even, odd), "seq", 0)


def across_swap(value):
    size = lax.axis_size("seq")
    pairs = [(i, i - 1 if i % 2 == 0 else i + 1) for i in range(size)]
    return lax.ppermute(value, "seq", [(i, j) for i, j in pairs if 0 <= j < size])


def diagonal_swap(even, odd):
    return across_swap(jnp.where(side("seq", 0) == 0, even, odd))


def late_steps(side_first):
    side_bits = [("grp", bit, 1) for bit in range(1, bits_of("grp"))]
    far_bits = [("seq", bit, 1) for bit in range(1, bits_of("seq"))]
    start = side_bits + far_bits[:1] if side_first else far_bits[:1] + side_bits
    return [("grp", 0, 1)] + start + [("seq", 0, 1)] + far_bits[1:]


def scatter_steps(first, most=2):
    count = bits_of("seq")
    far_bits = [("seq", bit, min(most, count - bit)) for bit in range(1, count, most)]
    side_bits = [("grp", bit, 1) for bit in range(1, bits_of("grp"))]
    middle = [("seq", 0, 1)] + side_bits if first == "seq" else side_bits + [("seq", 0, 1)]
    return [("grp", 0, 1)] + middle + far_bits


def summed_all(value):
    for axis in ("grp", "seq"):
        count, size = (bits_of(axis), lax.axis_size(axis))
        for bit in range(0, count, 2):
            others = [
                lax.ppermute(value, axis, [(i, i ^ (step << bit)) for i in range(size)])
                for step in range(1, 4 if bit + 1 < count else 2)
            ]
            value = value + others[0]
            if len(others) == 3:
                value = value + (others[1] + others[2])
    return value


def local(
    tokens,
    seq_lengths,
    answer_mask,
    out_grad,
    qkv_weight,
    merge_weight,
    expand_weight,
    shrink_weight,
    small_params,
    qkv_rows,
    qkv_cols,
    merge_rows,
    merge_cols,
    expand_rows,
    expand_cols,
    shrink_rows,
    shrink_cols,
    small_moment,
):
    seqs, piece, width = tokens.shape
    axes = ("seq", "grp")
    devices = lax.axis_size("seq") * lax.axis_size("grp")
    rows = qkv_weight.shape[0]
    ff_rows = shrink_weight.shape[0]
    chunks = FF // D
    total = piece * lax.axis_size("seq")
    start = lax.axis_index("seq") * piece
    info = jnp.concatenate(
        [jnp.stack([start, jnp.int32(total)]).astype(jnp.int32), seq_lengths.astype(jnp.int32)]
    )
    smalls = small_params.shape[1]

    packed = whole_call(
        pack_kernel,
        [((rows, 9 * D), BF16)],
        (merge_weight, expand_weight, shrink_weight),
        "pack",
        2,
        [pltpu.VMEM((GROUPS, ff_rows, LANES), F32)],
    )[0]
    packed = lax.all_gather(packed, axes, axis=0, tiled=True)
    early = jnp.concatenate(
        [qkv_weight.astype(BF16), jnp.pad(small_params.astype(BF16), ((0, 0), (0, LANES - smalls)))],
        axis=1,
    )
    last, ahead = (tokens[:, piece - WIN :], tokens[:, :WIN])
    beside = near_swap(last, ahead)
    across = diagonal_swap(ahead, last)
    early, done = gather_far(early)
    weight_a = gather_near(early[..., :CUT], done, "grp")
    weight_b = gather_near(early[..., CUT:], done, "seq")
    flat = tokens.reshape(seqs * piece, width)
    cot = (out_grad * answer_mask[:, :, None].astype(BF16)).reshape(seqs * piece, width)

    turned = flat.T
    old_rows = [entry[None, :] for entry in (qkv_rows, merge_rows, expand_rows, shrink_rows)]
    old_cols = [entry[None, :] for entry in (qkv_cols, merge_cols, expand_cols, shrink_cols)]
    turned, old_rows, old_cols, info = lax.optimization_barrier((turned, old_rows, old_cols, info))
    query, key, value, pool, rim_near, rim_across, vectors = project(
        info, beside, tokens, across, weight_a, weight_b
    )
    mixed, near_lse = near_attend(info, query, key, value)
    att, pkey, pvalue, far_lse = far_attend(
        info, query, pool, swap(rim_near, "seq", 0), across_swap(rim_across), mixed
    )
    att_flat = att.reshape(seqs * piece, width)
    (
        block_out, first_grad, hidden_low, active, up_grad, branch_grad, mixed_grad, att_grad, sums,
    ) = feed(flat, att_flat, cot, packed, vectors)

    shrink_local = outer(active, branch_grad).astype(BF16).reshape(chunks, devices, rows, D)
    merge_local = outer(att_flat, mixed_grad).astype(BF16).reshape(1, devices, rows, D)
    shrink_local, merge_local, up_grad = lax.optimization_barrier((shrink_local, merge_local, up_grad))
    shrink_chain = scatter_step(scatter_begin(shrink_local, late_steps(True), 1))
    merge_chain = scatter_step(scatter_begin(merge_local, late_steps(True), 1))
    late_chain = (jnp.concatenate([shrink_chain[0], merge_chain[0]], axis=0),) + shrink_chain[1:]
    expand_local = outer(hidden_low, up_grad).astype(BF16).reshape(devices, rows, FF)
    expand_chain = scatter_begin(expand_local, late_steps(False))
    chains = [late_chain, scatter_step(expand_chain)]

    def seq_rows(value, which):
        return value[which * piece : (which + 1) * piece]

    def advance(states, gate):
        return [scatter_step(state, gate) if len(state[2]) > 1 else state for state in states]

    att_grad = att_grad.reshape(seqs, piece, width)
    chains, info = after(chains, info)
    full_parts, parts, rims = ([], [], [])
    for which in range(seqs):
        parts.append(back(which, info, query, key, value, pkey, pvalue, att_grad, near_lse, far_lse))
        info, _ = lax.optimization_barrier((info, parts[which][0]))
    for which in range(seqs):
        query_part, near_grad, far_grad, rim_near, rim_across = parts[which]
        if which:
            rim_near, rim_across, _ = lax.optimization_barrier((rim_near, rim_across, rims[which - 1][3:]))
        rims.append((query_part, near_grad, far_grad, swap(rim_near, "seq", 0), across_swap(rim_across)))
    chains = advance(chains, (parts[-1][0], rims[0][3:]))
    chains, vectors = after(chains, vectors)
    before = None
    for which in range(seqs):
        full_part, *before = pool_back(
            which, seqs, info, rims[which], key, value, vectors, turned, before, sums
        )
        full_parts.append(full_part.reshape(piece, 3 * width))
        if which == 0:
            while len(chains[0][2]) > bits_of("seq") - 1:
                chains = advance(chains, (full_part, rims[-1][3:]))
            chains, vectors = after(chains, vectors)
    late_parts = [chains[0][0][j] for j in range(chunks + 1)] + [chains[1][0]]
    late_chain = (jnp.concatenate(late_parts, axis=-1),) + chains[1][1:]
    late_chain = advance([late_chain], None)[0]
    (late_chain,), before = after([late_chain], before)
    early_chains = [
        scatter_step(scatter_begin(entry.reshape(devices, rows, -1), scatter_steps(first)))
        for entry, first in zip(before, ("seq", "grp"))
    ]
    for _ in range(bits_of("grp")):
        early_chains = [scatter_step(state) for state in early_chains]
    early_chain = (
        jnp.concatenate([state[0] for state in early_chains], axis=-1),
    ) + early_chains[0][1:]
    late_sum = scatter_end(late_chain, early_chain[0])
    early_sum = scatter_end(early_chain)
    full_parts, _ = lax.optimization_barrier((full_parts, early_chain[0]))
    input_grad = jnp.stack(
        [
            seq_rows(first_grad, which)
            + nt(full_parts[which][:, :CUT], weight_a)
            + nt(full_parts[which][:, CUT:], weight_b[:, : 3 * D - CUT])
            for which in range(seqs)
        ]
    )

    masters = (qkv_weight, merge_weight, expand_weight, shrink_weight)
    base, expand_sum, shrink_sum = whole_call(
        late_kernel,
        [((1, 9 * D + LANES), F32), ((rows, FF), F32), ((ff_rows, D), F32)],
        (late_sum,) + tuple(old_rows),
        "late_stats",
        3,
        [pltpu.VMEM((GROUPS, ff_rows, LANES), F32)],
    )
    payload = whole_call(
        stats_kernel, [((1, 9 * D + LANES), F32)], (early_sum, base), "stats", 1
    )[0]
    payload = summed_all(payload)
    outs = [((1, 1), F32)]
    for master in masters:
        high, wide = master.shape
        outs += [((high, wide), F32), ((1, high), F32), ((wide // LANES, LANES), F32), ((high, wide), F32)]
        outs += [((high, wide), BF16)]
    outs += [((smalls, rows), F32)] * 3 + [((smalls, rows), BF16)]
    fresh = whole_call(
        update_kernel,
        outs,
        (payload, early_sum, late_sum, expand_sum, shrink_sum)
        + tuple(old_rows)
        + tuple(old_cols)
        + masters
        + (small_params.T, small_moment.T),
        "update",
        5,
    )
    results = []
    for index in range(4):
        grad, rows_new, cols_new, new, low_new = fresh[1 + 5 * index : 6 + 5 * index]
        results += [grad, rows_new.reshape(-1), cols_new.reshape(-1), new, low_new]
    return (
        block_out.reshape(seqs, piece, width),
        input_grad,
        fresh[0].reshape(()),
        *results,
        *[entry.T for entry in fresh[21:]],
    )


def solution(mesh):
    whole = ("seq", "grp")
    matrix = P(whole, None)
    vector = P(whole)
    in_specs = (
        P("grp", "seq", None),
        P("grp"),
        P("grp", "seq"),
        P("grp", "seq", None),
        *[matrix] * 5,
        *[vector, P()] * 4,
        matrix,
    )
    out_specs = (
        P("grp", "seq", None),
        P("grp", "seq", None),
        P(),
        *[matrix, vector, P(), matrix, matrix] * 4,
        *[matrix] * 4,
    )
    return jax.shard_map(local, mesh=mesh, in_specs=in_specs, out_specs=out_specs, check_vma=False)
```

profile of v0, /device:TPU:0, one launch (start us, length us, event | category | flops | bytes accessed | tf_op | source)
XLA Modules:
  0.0 367.4 jit_solution(13675073267820813509)
XLA Ops:
  7.3 2.6 pack.1
  10.7 4.0 %collective-permute-start.2 = (bf16[24,2432]{1,0:T(8,128)(2,1)}, bf16[24,2432]{1,0:T(8,128)(2,1)S(1)}, u32[]{:S(2)}, u32[]{:S(2)}) collective-permute-start(bf16[24,2432]{1,0:T(8,128)(2,1)} %get-tuple-element.270), channel_id=1, source_target_pairs={{0,16},{4,20},{8,24},{12,28},{16,0},{20,4},{24,8},{28,12},{1,17},{... | collective-permute-start | bytes 350216 | tf_op jit(solution)/shard_map/ppermute | solution.py:811
  15.5 1.5 collective-permute-start
  17.0 1.3 collective-permute-start.1
  18.4 1.4 broadcast_multiply_fusion
  19.8 1.7 copy.85
  23.9 2.6 collective-permute-start.3
  26.7 9.9 %collective-permute-done.3 = bf16[2,24,2432]{2,1,0:T(8,128)(2,1)S(1)} collective-permute-done((bf16[2,24,2432]{2,1,0:T(8,128)(2,1)S(1)}, bf16[2,24,2432]{2,1,0:T(8,128)(2,1)S(1)}, u32[]{:S(2)}, u32[]{:S(2)}) %collective-permute-start.3) | collective-permute-done | bytes 233504 | tf_op jit(solution)/shard_map/ppermute | solution.py:811
  36.7 2.2 collective-permute-start.7
  38.9 1.5 collective-permute-start.4
  40.4 2.6 collective-permute-done.7
  43.1 1.5 collective-permute-start.8
  44.8 2.5 collective-permute-done.4
  47.6 11.8 %collective-permute-done.8 = bf16[2,2,2,24,1152]{4,3,0,1,2:T(8,128)(2,1)S(1)} collective-permute-done((bf16[2,2,2,24,1152]{4,3,0,1,2:T(8,128)(2,1)S(1)}, bf16[2,2,2,24,1152]{4,3,0,1,2:T(8,128)(2,1)S(1)}, u32[]{:S(2)}, u32[]{:S(2)}) %collective-permute-start.8) | collective-permute-done | bytes 442400 | tf_op jit(solution)/shard_map/ppermute | solution.py:811
  59.6 5.6 %collective-permute-done.5 = bf16[2,2,2,24,1280]{4,3,0,1,2:T(8,128)(2,1)S(1)} collective-permute-done((bf16[2,2,2,24,1280]{4,3,0,1,2:T(8,128)(2,1)S(1)}, bf16[2,2,2,24,1280]{4,3,0,1,2:T(8,128)(2,1)S(1)}, u32[]{:S(2)}, u32[]{:S(2)}) %collective-permute-start.5) | collective-permute-done | bytes 491552 | tf_op jit(solution)/shard_map/ppermute | solution.py:811
  66.2 1.3 copy.74
  68.3 1.5 copy.73
  69.9 10.0 %project.1 = (bf16[2,512,768]{2,1,0:T(8,128)(2,1)}, bf16[2,640,768]{2,1,0:T(8,128)(2,1)}, bf16[2,640,768]{2,1,0:T(8,128)(2,1)}, bf16[2,2,128,768]{3,2,1,0:T(8,12...) custom-call(s32[4]{0:T(128)} %pad_add_fusion.info, ...), custom_call_target="tpu_custom_call" | custom-call | flops 8000000000 | tf_op jit(solution)/shard_map/project/pallas_call | solution.py:240
  81.7 11.5 %near.1 = (f32[2,512,768]{2,1,0:T(8,128)}, f32[2,4,8,256]{3,2,1,0:T(8,128)}) custom-call(s32[4]{0:T(128)} %pad_add_fusion.info, bf16[2,512,768]{2,1,0:T(8,128)(2,1)} %get-tuple-element.135.query, bf16[2,640,768]{2,1,0:T(8,128)(2,1)} %get-tuple-element.139.key, bf16[2,640,768]{2,1,0:T(8,128)(2,1)} %get-tuple-element.140.value), custom_call_target="tpu_custom_call" | custom-call | flops 24000000000 | tf_op jit(solution)/shard_map/near/pallas_call | solution.py:240
  93.2 13.9 %collective-permute-done.10.beside = bf16[2,2,64,768]{3,2,1,0:T(8,128)(2,1)S(1)} collective-permute-done((bf16[2,2,64,768]{3,2,1,0:T(8,128)(2,1)}, bf16[2,2,64,768]{3,2,1,0:T(8,128)(2,1)S(1)}, u32[]{:S(2)}, u32[]{:S(2)}) %collective-permute-start.10) | collective-permute-done | bytes 393248 | tf_op jit(solution)/shard_map/ppermute | solution.py:811
  108.1 10.8 %far.1 = (bf16[2,512,768]{2,1,0:T(8,128)(2,1)}, bf16[2,256,768]{2,1,0:T(8,128)(2,1)}, bf16[2,256,768]{2,1,0:T(8,128)(2,1)}, f32[2,4,8,256]{3,2,1,0:T(8,128)}) custom-call(s32[4]{0:T(128)} %pad_add_fusion.info, bf16[2,512,768]{2,1,0:T(8,128)(2,1)} %get-tuple-element.135.query, bf16[2,2,128,768]{3,2,1,0:T(8,128)(2,1)} %get-tuple-element.136.pool, ...), custom_call_target="tpu_custom_call" | custom-call | flops 9600000000 | tf_op jit(solution)/shard_map/far/pallas_call | solution.py:240
  118.8 9.3 %all-gather.2.cloned.1.call-done.packed = bf16[768,6912]{1,0:T(8,128)(2,1)} async-done(((bf16[24,6912]{1,0:T(8,128)(2,1)}), bf16[768,6912]{1,0:T(8,128)(2,1)}) %all-gather.2.cloned.1.call-update) | async-done | bytes 10616848 | tf_op jit(solution)/shard_map/all_gather | solution.py:1000
  128.2 48.2 %feed.1 = (bf16[1024,768]{1,0:T(8,128)(2,1)}, f32[1024,768]{1,0:T(8,128)}, bf16[1024,768]{1,0:T(8,128)(2,1)}, bf16[1024,3072]{1,0:T(8,128)(2,1)}, bf16[1024,3072...) custom-call(bf16[1024,768]{1,0:T(8,128)(2,1)} %bitcast.191, ...), custom_call_target="tpu_custom_call" | custom-call | flops 38400000000 | tf_op jit(solution)/shard_map/feed/pallas_call | solution.py:414
  176.4 3.0 convolution_convert_fusion.2
  179.4 8.7 %convolution_convert_fusion.1 = bf16[3072,768]{1,0:T(8,128)(2,1)S(1)} fusion(bf16[1024,3072]{1,0:T(8,128)(2,1)} %get-tuple-element.146, bf16[1024,768]{1,0:T(8,128)(2,1)S(1)} %copy-done.22), kind=kOutput, calls=%fused_computation.1 | convolution fusion | flops 4834197504 | bytes 12582912 | tf_op jit(solution)/shard_map/dot_general | solution.py:62
  188.1 1.7 dynamic-slice_bitcast_fusion
  190.6 5.4 %convolution_convert_fusion = bf16[768,3072]{1,0:T(8,128)(2,1)S(1)} fusion(bf16[1024,768]{1,0:T(8,128)(2,1)S(1)} %copy-done.21, bf16[1024,3072]{1,0:T(8,128)(2,1)S(1)} %bitcast.253), kind=kOutput, calls=%fused_computation | convolution fusion | flops 4834197504 | bytes 12582912 | tf_op jit(solution)/shard_map/dot_general | solution.py:62
  196.4 1.6 copy.105
  199.4 4.3 %collective-permute-done.13 = bf16[1,2,2,2,2,24,768]{6,5,4,3,2,1,0:T(8,128)(2,1)} collective-permute-done((bf16[1,2,2,2,2,24,768]{6,5,4,3,2,1,0:T(8,128)(2,1)}, bf16[1,2,2,2,2,24,768]{6,5,4,3,2,1,0:T(8,128)(2,1)}, u32[]{:S(2)}, u32[]{:S(2)}) %collective-permute-start.13) | collective-permute-done | bytes 589856 | tf_op jit(solution)/shard_map/ppermute | solution.py:811
  204.9 3.1 fusion.1
  208.3 2.6 fusion
  212.1 1.3 collective-permute-start.18
  213.6 1.3 copy.106
  214.9 1.5 collective-permute-start.17
  216.3 15.0 %back.2 = (bf16[1,512,768]{2,1,0:T(8,128)(2,1)}, f32[1,2,640,768]{3,2,1,0:T(8,128)}, f32[1,2,256,768]{3,2,1,0:T(8,128)}, bf16[1,2,144,768]{3,2,1,0:T(8,128)(2,1)}, bf16[1,2,144,768]{3,2,1,0:T(8,128)(2,1)}) custom-call(s32[4]{0:T(128)} %pad_add_fusion.info, bf16[2,512,768]{2,1,0:T(8,128)(2,1)} %get-tuple-element.135.query, ...), custom_call_target="tpu_custom_call" | custom-call | flops 24000000000 | tf_op jit(solution)/shard_map/back/pallas_call | solution.py:534
  231.3 1.4 collective-permute-start.16
  232.9 15.0 %back.3 = (bf16[1,512,768]{2,1,0:T(8,128)(2,1)}, f32[1,2,640,768]{3,2,1,0:T(8,128)}, f32[1,2,256,768]{3,2,1,0:T(8,128)}, bf16[1,2,144,768]{3,2,1,0:T(8,128)(2,1)}, bf16[1,2,144,768]{3,2,1,0:T(8,128)(2,1)}) custom-call(s32[4]{0:T(128)} %pad_add_fusion.info, bf16[2,512,768]{2,1,0:T(8,128)(2,1)} %get-tuple-element.135.query, ...), custom_call_target="tpu_custom_call" | custom-call | flops 8000000 | tf_op jit(solution)/shard_map/back/pallas_call | solution.py:534
  247.9 2.8 collective-permute-done.15.beside
  250.7 2.5 collective-permute-start.19
  253.2 1.6 collective-permute-start.20
  254.8 1.7 add_convert_fusion.1
  256.5 1.7 add_convert_fusion
  259.1 2.0 collective-permute-start.21
  261.1 9.8 %pool_back.2 = (bf16[1,512,2304]{2,1,0:T(8,128)(2,1)}, f32[768,2304]{1,0:T(8,128)}, f32[16,768]{1,0:T(8,128)}) custom-call(s32[4]{0:T(128)} %pad_add_fusion.info, bf16[1,512,768]{2,1,0:T(8,128)(2,1)} %get-tuple-element.160.query_grad, f32[1,2,640,768]{3,2,1,0:T(8,128)} %get-tuple-element.164.near_grad, f32[1,2,256,768]{3,2,1,0:T(8,128)} %get-tuple-element.165.far_grad, ...), custom_call_target="tpu_custom_call" | custom-call | flops 24000000000 | tf_op jit(solution)/shard_map/pool_back/pallas_call | solution.py:631
  272.7 9.1 %collective-permute-done.21 = bf16[5,2,2,24,768]{4,3,2,1,0:T(8,128)(2,1)S(1)} collective-permute-done((bf16[5,2,2,24,768]{4,3,2,1,0:T(8,128)(2,1)S(1)}, bf16[5,2,2,24,768]{4,3,2,1,0:T(8,128)(2,1)S(1)}, u32[]{:S(2)}, u32[]{:S(2)}) %collective-permute-start.21) | collective-permute-done | bytes 737312 | tf_op jit(solution)/shard_map/ppermute | solution.py:811
  282.3 10.5 %pool_back.3 = (bf16[1,512,2304]{2,1,0:T(8,128)(2,1)}, bf16[768,1280]{1,0:T(8,128)(2,1)}, bf16[768,1152]{1,0:T(8,128)(2,1)}) custom-call(s32[4]{0:T(128)} %pad_add_fusion.info, bf16[1,512,768]{2,1,0:T(8,128)(2,1)} %get-tuple-element.162.query_grad, f32[1,2,640,768]{3,2,1,0:T(8,128)} %get-tuple-element.177.near_grad, ...), custom_call_target="tpu_custom_call" | custom-call | flops 8000000 | tf_op jit(solution)/shard_map/pool_back/pallas_call | solution.py:631
  292.8 4.5 %collective-permute-done.23 = bf16[2,24,6912]{2,1,0:T(8,128)(2,1)S(1)} collective-permute-done((bf16[2,24,6912]{2,1,0:T(8,128)(2,1)S(1)}, bf16[2,24,6912]{2,1,0:T(8,128)(2,1)S(1)}, u32[]{:S(2)}, u32[]{:S(2)}) %collective-permute-start.23) | collective-permute-done | bytes 663584 | tf_op jit(solution)/shard_map/ppermute | solution.py:811
  299.5 1.8 collective-permute-start.33
  302.8 11.1 %collective-permute-done.28 = bf16[2,2,2,24,1152]{4,3,1,0,2:T(8,128)(2,1)S(1)} collective-permute-done((bf16[2,2,2,24,1152]{4,3,1,0,2:T(8,128)(2,1)S(1)}, bf16[2,2,2,24,1152]{4,3,1,0,2:T(8,128)(2,1)S(1)}, u32[]{:S(2)}, u32[]{:S(2)}) %collective-permute-start.28) | collective-permute-done | bytes 442400 | tf_op jit(solution)/shard_map/ppermute | solution.py:811
  315.8 2.0 collective-permute-start.26
  317.7 3.1 collective-permute-done.29
  320.9 1.9 collective-permute-done.26
  324.1 1.7 collective-permute-start.31
  325.7 2.3 collective-permute-start.32
  331.7 5.1 %late_stats.1 = (f32[1,7040]{1,0:T(1,128)}, f32[24,3072]{1,0:T(8,128)}, f32[96,768]{1,0:T(8,128)}) custom-call(f32[24,6912]{1,0:T(8,128)} %convert_add_fusion.8.late, f32[1,24]{1,0:T(1,128)} %bitcast.229, f32[1,24]{1,0:T(1,128)} %bitcast.231, f32[1,24]{1,0:T(1,128)} %bitcast.233, f32[1,96]{1,0:T(1,128)} %bitcast.235), custom_call_target="tpu_custom_call" | custom-call | flops 2400000000 | tf_op jit(solution)/shard_map/late_stats/pallas_call | solution.py:797
  336.8 1.7 fusion.25.early
  338.5 1.7 stats.1
  340.2 1.5 collective-permute-start.35
  342.1 3.2 fusion.13
  346.3 2.5 collective-permute-start.39
  348.9 2.3 add_bitcast_fusion
  351.3 2.9 collective-permute-start.40
  354.1 2.0 pad_maximum_fusion
  356.8 3.5 update.1
  (171 shorter events, 30.6 us)
Async XLA Ops:
  7.2 2.7 copy-start.10
  7.2 2.7 copy-start.13
  7.2 7.5 %copy-start.4 = (bf16[2,512,768]{2,1,0:T(8,128)(2,1)S(1)}, bf16[2,512,768]{2,1,0:T(8,128)(2,1)}, u32[]{:S(2)}) copy-start(bf16[2,512,768]{2,1,0:T(8,128)(2,1)} %own.1) | copy-start | bytes 4718596
  7.2 120.9 %all-gather.2.cloned.1.call-start = ((), (), s32[]{:S(2)}) async-start(), calls=%async_computation | async-start | bytes 10948608 | tf_op jit(solution)/shard_map/all_gather | solution.py:1000
  9.9 8.5 %copy-start.16 = (s32[2,512]{1,0:T(2,128)S(1)}, s32[2,512]{1,0:T(2,128)}, u32[]{:S(2)}) copy-start(s32[2,512]{1,0:T(2,128)} %param.20) | copy-start | bytes 12292
  9.9 8.5 %copy-start.8 = (bf16[2,512,768]{2,1,0:T(8,128)(2,1)S(1)}, bf16[2,512,768]{2,1,0:T(8,128)(2,1)}, u32[]{:S(2)}) copy-start(bf16[2,512,768]{2,1,0:T(8,128)(2,1)} %param.21) | copy-start | bytes 4718596
  10.7 13.1 %collective-permute-start.2 = (bf16[24,2432]{1,0:T(8,128)(2,1)}, bf16[24,2432]{1,0:T(8,128)(2,1)S(1)}, u32[]{:S(2)}, u32[]{:S(2)}) collective-permute-start(bf16[24,2432]{1,0:T(8,128)(2,1)} %get-tuple-element.270), channel_id=1, source_target_pairs={{0,16},{4,20},{8,24},{12,28},{16,0},{20,4},{24,8},{28,12},{1,17},{... | collective-permute-start | bytes 350216 | tf_op jit(solution)/shard_map/ppermute | solution.py:811
  15.5 54.3 %collective-permute-start = (bf16[2,64,768]{2,1,0:T(8,128)(2,1)}, bf16[2,64,768]{2,1,0:T(8,128)(2,1)}, u32[]{:S(2)}, u32[]{:S(2)}) collective-permute-start(bf16[2,64,768]{2,1,0:T(8,128)(2,1)} %get-tuple-element.252), channel_id=1, source_target_pairs={{0,4},{4,0},{8,12},{12,8},{16,20},{20,16},{24,28},{28,24},{1,5},{5... | collective-permute-start | bytes 589832 | tf_op jit(solution)/shard_map/ppermute | solution.py:811
  17.0 52.9 %collective-permute-start.1 = (bf16[2,64,768]{2,1,0:T(8,128)(2,1)}, bf16[2,64,768]{2,1,0:T(8,128)(2,1)}, u32[]{:S(2)}, u32[]{:S(2)}) collective-permute-start(bf16[2,64,768]{2,1,0:T(8,128)(2,1)} %get-tuple-element.251), channel_id=1, source_target_pairs={{4,8},{8,4},{12,16},{16,12},{20,24},{24,20},{5,9},{9,5},{13,17},{1... | collective-permute-start | bytes 589832 | tf_op jit(solution)/shard_map/ppermute | solution.py:923
  19.8 1.7 copy-start.12
  19.8 2.3 copy-start.14
  19.8 2.9 copy-start.15
  19.8 3.5 copy-start.17
  23.9 12.6 %collective-permute-start.3 = (bf16[2,24,2432]{2,1,0:T(8,128)(2,1)S(1)}, bf16[2,24,2432]{2,1,0:T(8,128)(2,1)S(1)}, u32[]{:S(2)}, u32[]{:S(2)}) collective-permute-start(bf16[2,24,2432]{2,1,0:T(8,128)(2,1)S(1)} %maximum_select_fusion.12), channel_id=1, source_target_pairs={{0,8},{4,12},{8,0},{12,4},{16,24},{20,28},{24,16},{28,20},{1,9},{5... | collective-permute-start | bytes 700424 | tf_op jit(solution)/shard_map/ppermute | solution.py:811
  36.7 6.4 %collective-permute-start.7 = (bf16[2,2,24,1152]{3,2,0,1:T(8,128)(2,1)S(1)}, bf16[2,2,24,1152]{3,2,0,1:T(8,128)(2,1)S(1)}, u32[]{:S(2)}, u32[]{:S(2)}) collective-permute-start(bf16[2,2,24,1152]{3,2,0,1:T(8,128)(2,1)S(1)} %get-tuple-element.264), channel_id=1, source_target_pairs={{0,4},{4,0},{8,12},{12,8},{16,20},{20,16},{24,28},{28,24},{1,5},{5... | collective-permute-start | bytes 663560 | tf_op jit(solution)/shard_map/ppermute | solution.py:811
  38.9 8.4 %collective-permute-start.4 = (bf16[2,2,24,1280]{3,2,0,1:T(8,128)(2,1)S(1)}, bf16[2,2,24,1280]{3,2,0,1:T(8,128)(2,1)S(1)}, u32[]{:S(2)}, u32[]{:S(2)}) collective-permute-start(bf16[2,2,24,1280]{3,2,0,1:T(8,128)(2,1)S(1)} %get-tuple-element.267), channel_id=1, source_target_pairs={{0,2},{1,3},{2,0},{3,1},{4,6},{5,7},{6,4},{7,5},{8,10},{9,11},{10,... | collective-permute-start | bytes 737288 | tf_op jit(solution)/shard_map/ppermute | solution.py:811
  43.1 16.2 %collective-permute-start.8 = (bf16[2,2,2,24,1152]{4,3,0,1,2:T(8,128)(2,1)S(1)}, bf16[2,2,2,24,1152]{4,3,0,1,2:T(8,128)(2,1)S(1)}, u32[]{:S(2)}, u32[]{:S(2)}) collective-permute-start(bf16[2,2,2,24,1152]{4,3,0,1,2:T(8,128)(2,1)S(1)} %maximum_select_fusion.10), channel_id=1, source_target_pairs={{0,2},{1,3},{2,0},{3,1},{4,6},{5,7},{6,4},{7,5},{8,10},{9,11},{10,... | collective-permute-start | bytes 1327112 | tf_op jit(solution)/shard_map/ppermute | solution.py:811
  47.4 17.8 %collective-permute-start.5 = (bf16[2,2,2,24,1280]{4,3,0,1,2:T(8,128)(2,1)S(1)}, bf16[2,2,2,24,1280]{4,3,0,1,2:T(8,128)(2,1)S(1)}, u32[]{:S(2)}, u32[]{:S(2)}) collective-permute-start(bf16[2,2,2,24,1280]{4,3,0,1,2:T(8,128)(2,1)S(1)} %maximum_select_fusion.7), channel_id=1, source_target_pairs={{0,4},{4,0},{8,12},{12,8},{16,20},{20,16},{24,28},{28,24},{1,5},{5... | collective-permute-start | bytes 1474568 | tf_op jit(solution)/shard_map/ppermute | solution.py:811
  59.5 6.4 %collective-permute-start.9 = (bf16[2,2,2,2,24,1152]{5,4,0,1,2,3:T(8,128)(2,1)S(1)}, bf16[2,2,2,2,24,1152]{5,4,0,1,2,3:T(8,128)(2,1)S(1)}, u32[]{:S(2)}, u32[]{:S(2)}) collective-permute-start(bf16[2,2,2,2,24,1152]{5,4,0,1,2,3:T(8,128)(2,1)S(1)} %maximum_select_fusion.5), channel_id=1, source_target_pairs={{0,1},{1,0},{2,3},{3,2},{4,5},{5,4},{6,7},{7,6},{8,9},{9,8},{10,11... | collective-permute-start | bytes 2654216 | tf_op jit(solution)/shard_map/ppermute | solution.py:811
  65.4 2.6 collective-permute-start.6
  79.9 27.3 %collective-permute-start.10 = (bf16[2,2,64,768]{3,2,1,0:T(8,128)(2,1)}, bf16[2,2,64,768]{3,2,1,0:T(8,128)(2,1)S(1)}, u32[]{:S(2)}, u32[]{:S(2)}) collective-permute-start(bf16[2,2,64,768]{3,2,1,0:T(8,128)(2,1)} %get-tuple-element.137), channel_id=1, source_target_pairs={{0,4},{4,0},{8,12},{12,8},{16,20},{20,16},{24,28},{28,24},{1,5},{5... | collective-permute-start | bytes 1179656 | tf_op jit(solution)/shard_map/ppermute | solution.py:811
  80.8 26.4 %collective-permute-start.11 = (bf16[2,2,64,768]{3,2,1,0:T(8,128)(2,1)}, bf16[2,2,64,768]{3,2,1,0:T(8,128)(2,1)S(1)}, u32[]{:S(2)}, u32[]{:S(2)}) collective-permute-start(bf16[2,2,64,768]{3,2,1,0:T(8,128)(2,1)} %get-tuple-element.138), channel_id=1, source_target_pairs={{4,8},{8,4},{12,16},{16,12},{20,24},{24,20},{5,9},{9,5},{13,17},{1... | collective-permute-start | bytes 1179656 | tf_op jit(solution)/shard_map/ppermute | solution.py:923
  128.2 48.2 %copy-start.20 = (bf16[2,512,768]{2,1,0:T(8,128)(2,1)S(1)}, bf16[2,512,768]{2,1,0:T(8,128)(2,1)}, u32[]{:S(2)}) copy-start(bf16[2,512,768]{2,1,0:T(8,128)(2,1)} %get-tuple-element.142) | copy-start | bytes 4718596
  176.4 3.0 copy-start.22
  176.4 13.7 %slice-start = ((s8[6291456]{0:T(1024)(128)(4,1)}), s8[4194304]{0:T(1024)(128)(4,1)S(1)}, s32[]{:S(2)}) async-start(s8[6291456]{0:T(1024)(128)(4,1)} %bitcast.252), calls=%async_computation.1 | async-start | bytes 8388608
  179.4 10.7 %slice-start.1 = ((s8[6291456]{0:T(1024)(128)(4,1)}), s8[2097152]{0:T(1024)(128)(4,1)S(1)}, s32[]{:S(2)}) async-start(s8[6291456]{0:T(1024)(128)(4,1)} %bitcast.252), calls=%async_computation.2 | async-start | bytes 4194304
  188.1 7.9 %copy-start.1 = (bf16[3072,768]{1,0:T(8,128)(2,1)}, bf16[3072,768]{1,0:T(8,128)(2,1)S(1)}, u32[]{:S(2)}) copy-start(bf16[3072,768]{1,0:T(8,128)(2,1)S(1)} %convolution_convert_fusion.1) | copy-start | bytes 14155780
  188.1 2.5 copy-start.21
  189.8 15.1 %collective-permute-start.12 = (bf16[4,2,2,2,2,24,768]{6,5,4,3,2,1,0:T(8,128)(2,1)}, bf16[4,2,2,2,2,24,768]{6,5,4,3,2,1,0:T(8,128)(2,1)}, u32[]{:S(2)}, u32[]{:S(2)}) collective-permute-start(bf16[4,2,2,2,2,24,768]{6,5,4,3,2,1,0:T(8,128)(2,1)} %dynamic-slice_bitcast_fusion), channel_id=1, source_target_pairs={{0,1},{1,0},{2,3},{3,2},{4,5},{5,4},{6,7},{7,6},{8,9},{9,8},{10,11... | collective-permute-start | bytes 7077896 | tf_op jit(solution)/shard_map/ppermute | solution.py:811
  198.0 10.3 %collective-permute-start.14 = (bf16[2,2,2,2,24,3072]{5,4,3,2,0,1:T(8,128)(2,1)}, bf16[2,2,2,2,24,3072]{5,4,3,2,0,1:T(8,128)(2,1)}, u32[]{:S(2)}, u32[]{:S(2)}) collective-permute-start(bf16[2,2,2,2,24,3072]{5,4,3,2,0,1:T(8,128)(2,1)} %bitcast.177), channel_id=1, source_target_pairs={{0,1},{1,0},{2,3},{3,2},{4,5},{5,4},{6,7},{7,6},{8,9},{9,8},{10,11... | collective-permute-start | bytes 7077896 | tf_op jit(solution)/shard_map/ppermute | solution.py:811
  199.1 4.6 %collective-permute-start.13 = (bf16[1,2,2,2,2,24,768]{6,5,4,3,2,1,0:T(8,128)(2,1)}, bf16[1,2,2,2,2,24,768]{6,5,4,3,2,1,0:T(8,128)(2,1)}, u32[]{:S(2)}, u32[]{:S(2)}) collective-permute-start(bf16[1,2,2,2,2,24,768]{6,5,4,3,2,1,0:T(8,128)(2,1)} %dynamic-slice_bitcast_fusion.8), channel_id=1, source_target_pairs={{0,1},{1,0},{2,3},{3,2},{4,5},{5,4},{6,7},{7,6},{8,9},{9,8},{10,11... | collective-permute-start | bytes 1769480 | tf_op jit(solution)/shard_map/ppermute | solution.py:811
  212.1 42.7 %collective-permute-start.18 = (bf16[2,2,2,24,3072]{4,3,2,1,0:T(8,128)(2,1)}, bf16[2,2,2,24,3072]{4,3,2,1,0:T(8,128)(2,1)}, u32[]{:S(2)}, u32[]{:S(2)}) collective-permute-start(bf16[2,2,2,24,3072]{4,3,2,1,0:T(8,128)(2,1)} %get-tuple-element.245), channel_id=1, source_target_pairs={{0,8},{4,12},{8,0},{12,4},{16,24},{20,28},{24,16},{28,20},{1,9},{5... | collective-permute-start | bytes 3538952 | tf_op jit(solution)/shard_map/ppermute | solution.py:811
  214.9 41.6 %collective-permute-start.17 = (bf16[5,2,2,2,24,768]{5,4,3,1,0,2:T(8,128)(2,1)}, bf16[5,2,2,2,24,768]{5,4,3,1,0,2:T(8,128)(2,1)}, u32[]{:S(2)}, u32[]{:S(2)}) collective-permute-start(bf16[5,2,2,2,24,768]{5,4,3,1,0,2:T(8,128)(2,1)} %bitcast.178), channel_id=1, source_target_pairs={{0,2},{1,3},{2,0},{3,1},{4,6},{5,7},{6,4},{7,5},{8,10},{9,11},{10,... | collective-permute-start | bytes 4423688 | tf_op jit(solution)/shard_map/ppermute | solution.py:811
  231.3 19.4 %collective-permute-start.15 = (bf16[1,2,144,768]{3,2,1,0:T(8,128)(2,1)}, bf16[1,2,144,768]{3,2,1,0:T(8,128)(2,1)}, u32[]{:S(2)}, u32[]{:S(2)}) collective-permute-start(bf16[1,2,144,768]{3,2,1,0:T(8,128)(2,1)} %get-tuple-element.166), channel_id=1, source_target_pairs={{0,4},{4,0},{8,12},{12,8},{16,20},{20,16},{24,28},{28,24},{1,5},{5... | collective-permute-start | bytes 1327112 | tf_op jit(solution)/shard_map/ppermute | solution.py:811
  231.3 19.4 %collective-permute-start.16 = (bf16[1,2,144,768]{3,2,1,0:T(8,128)(2,1)}, bf16[1,2,144,768]{3,2,1,0:T(8,128)(2,1)}, u32[]{:S(2)}, u32[]{:S(2)}) collective-permute-start(bf16[1,2,144,768]{3,2,1,0:T(8,128)(2,1)} %get-tuple-element.167), channel_id=1, source_target_pairs={{4,8},{8,4},{12,16},{16,12},{20,24},{24,20},{5,9},{9,5},{13,17},{1... | collective-permute-start | bytes 1327112 | tf_op jit(solution)/shard_map/ppermute | solution.py:923
  250.7 21.0 %collective-permute-start.19 = (bf16[1,2,144,768]{3,2,1,0:T(8,128)(2,1)}, bf16[1,2,144,768]{3,2,1,0:T(8,128)(2,1)}, u32[]{:S(2)}, u32[]{:S(2)}) collective-permute-start(bf16[1,2,144,768]{3,2,1,0:T(8,128)(2,1)} %get-tuple-element.181), channel_id=1, source_target_pairs={{0,4},{4,0},{8,12},{12,8},{16,20},{20,16},{24,28},{28,24},{1,5},{5... | collective-permute-start | bytes 1327112 | tf_op jit(solution)/shard_map/ppermute | solution.py:811
  253.2 18.6 %collective-permute-start.20 = (bf16[1,2,144,768]{3,2,1,0:T(8,128)(2,1)}, bf16[1,2,144,768]{3,2,1,0:T(8,128)(2,1)}, u32[]{:S(2)}, u32[]{:S(2)}) collective-permute-start(bf16[1,2,144,768]{3,2,1,0:T(8,128)(2,1)} %get-tuple-element.182), channel_id=1, source_target_pairs={{4,8},{8,4},{12,16},{16,12},{20,24},{24,20},{5,9},{9,5},{13,17},{1... | collective-permute-start | bytes 1327112 | tf_op jit(solution)/shard_map/ppermute | solution.py:923
  258.3 14.2 %collective-permute-start.22 = (bf16[2,2,24,3072]{3,2,1,0:T(8,128)(2,1)S(1)}, bf16[2,2,24,3072]{3,2,1,0:T(8,128)(2,1)S(1)}, u32[]{:S(2)}, u32[]{:S(2)}) collective-permute-start(bf16[2,2,24,3072]{3,2,1,0:T(8,128)(2,1)S(1)} %get-tuple-element.255), channel_id=1, source_target_pairs={{0,2},{1,3},{2,0},{3,1},{4,6},{5,7},{6,4},{7,5},{8,10},{9,11},{10,... | collective-permute-start | bytes 1769480 | tf_op jit(solution)/shard_map/ppermute | solution.py:811
  259.1 22.7 %collective-permute-start.21 = (bf16[5,2,2,24,768]{4,3,2,1,0:T(8,128)(2,1)S(1)}, bf16[5,2,2,24,768]{4,3,2,1,0:T(8,128)(2,1)S(1)}, u32[]{:S(2)}, u32[]{:S(2)}) collective-permute-start(bf16[5,2,2,24,768]{4,3,2,1,0:T(8,128)(2,1)S(1)} %get-tuple-element.253), channel_id=1, source_target_pairs={{0,8},{4,12},{8,0},{12,4},{16,24},{20,28},{24,16},{28,20},{1,9},{5... | collective-permute-start | bytes 2211848 | tf_op jit(solution)/shard_map/ppermute | solution.py:811
  282.2 15.2 %collective-permute-start.23 = (bf16[2,24,6912]{2,1,0:T(8,128)(2,1)S(1)}, bf16[2,24,6912]{2,1,0:T(8,128)(2,1)S(1)}, u32[]{:S(2)}, u32[]{:S(2)}) collective-permute-start(bf16[2,24,6912]{2,1,0:T(8,128)(2,1)S(1)} %dynamic-slice_bitcast_fusion.5), channel_id=1, source_target_pairs={{0,4},{4,0},{8,12},{12,8},{16,20},{20,16},{24,28},{28,24},{1,5},{5... | collective-permute-start | bytes 1990664 | tf_op jit(solution)/shard_map/ppermute | solution.py:811
  292.8 4.7 %copy-start.7 = (bf16[768,1152]{1,0:T(8,128)(2,1)S(1)}, bf16[768,1152]{1,0:T(8,128)(2,1)}, u32[]{:S(2)}) copy-start(bf16[768,1152]{1,0:T(8,128)(2,1)} %get-tuple-element.199) | copy-start | bytes 5308420
  297.9 3.4 collective-permute-start.27
  299.3 2.8 collective-permute-start.24
  299.5 23.4 %collective-permute-start.33 = (bf16[24,6912]{1,0:T(8,128)(2,1)S(1)}, bf16[24,6912]{1,0:T(8,128)(2,1)S(1)}, u32[]{:S(2)}, u32[]{:S(2)}) collective-permute-start(bf16[24,6912]{1,0:T(8,128)(2,1)S(1)} %get-tuple-element.257), channel_id=1, source_target_pairs={{0,16},{4,20},{8,24},{12,28},{16,0},{20,4},{24,8},{28,12},{1,17},{... | collective-permute-start | bytes 995336 | tf_op jit(solution)/shard_map/ppermute | solution.py:811
  301.5 12.3 %collective-permute-start.28 = (bf16[2,2,2,24,1152]{4,3,1,0,2:T(8,128)(2,1)S(1)}, bf16[2,2,2,24,1152]{4,3,1,0,2:T(8,128)(2,1)S(1)}, u32[]{:S(2)}, u32[]{:S(2)}) collective-permute-start(bf16[2,2,2,24,1152]{4,3,1,0,2:T(8,128)(2,1)S(1)} %dynamic-slice_bitcast_fusion.10), channel_id=1, source_target_pairs={{0,2},{1,3},{2,0},{3,1},{4,6},{5,7},{6,4},{7,5},{8,10},{9,11},{10,... | collective-permute-start | bytes 1327112 | tf_op jit(solution)/shard_map/ppermute | solution.py:811
  302.4 13.2 %collective-permute-start.25 = (bf16[2,2,2,24,1280]{4,3,1,0,2:T(8,128)(2,1)S(1)}, bf16[2,2,2,24,1280]{4,3,1,0,2:T(8,128)(2,1)S(1)}, u32[]{:S(2)}, u32[]{:S(2)}) collective-permute-start(bf16[2,2,2,24,1280]{4,3,1,0,2:T(8,128)(2,1)S(1)} %dynamic-slice_bitcast_fusion.9), channel_id=1, source_target_pairs={{0,4},{4,0},{8,12},{12,8},{16,20},{20,16},{24,28},{28,24},{1,5},{5... | collective-permute-start | bytes 1474568 | tf_op jit(solution)/shard_map/ppermute | solution.py:811
  314.0 6.8 %collective-permute-start.29 = (bf16[2,2,24,1152]{3,2,1,0:T(8,128)(2,1)S(1)}, bf16[2,2,24,1152]{3,2,1,0:T(8,128)(2,1)S(1)}, u32[]{:S(2)}, u32[]{:S(2)}) collective-permute-start(bf16[2,2,24,1152]{3,2,1,0:T(8,128)(2,1)S(1)} %dynamic-slice_bitcast_fusion.14), channel_id=1, source_target_pairs={{0,4},{4,0},{8,12},{12,8},{16,20},{20,16},{24,28},{28,24},{1,5},{5... | collective-permute-start | bytes 663560 | tf_op jit(solution)/shard_map/ppermute | solution.py:811
  315.6 12.5 %copy-start.9 = (bf16[1,512,2304]{2,1,0:T(8,128)(2,1)S(1)}, bf16[1,512,2304]{2,1,0:T(8,128)(2,1)}, u32[]{:S(2)}) copy-start(bf16[1,512,2304]{2,1,0:T(8,128)(2,1)} %get-tuple-element.176) | copy-start | bytes 7077892
  315.7 12.3 %copy-start.5 = (bf16[2,2,2,2,2,24,1280]{6,5,4,3,2,1,0:T(8,128)(2,1)S(1)}, bf16[2,2,2,2,2,24,1280]{6,5,4,3,2,1,0:T(8,128)(2,1)}, u32[]{:S(2)}) copy-start(bf16[2,2,2,2,2,24,1280]{6,5,4,3,2,1,0:T(8,128)(2,1)} %copy.73) | copy-start | bytes 5898244
  315.8 7.0 %collective-permute-start.26 = (bf16[2,2,24,1280]{3,2,1,0:T(8,128)(2,1)S(1)}, bf16[2,2,24,1280]{3,2,1,0:T(8,128)(2,1)S(1)}, u32[]{:S(2)}, u32[]{:S(2)}) collective-permute-start(bf16[2,2,24,1280]{3,2,1,0:T(8,128)(2,1)S(1)} %dynamic-slice_bitcast_fusion.13), channel_id=1, source_target_pairs={{0,2},{1,3},{2,0},{3,1},{4,6},{5,7},{6,4},{7,5},{8,10},{9,11},{10,... | collective-permute-start | bytes 737288 | tf_op jit(solution)/shard_map/ppermute | solution.py:811
  323.6 13.2 %collective-permute-start.30 = (bf16[24,2432]{1,0:T(8,128)(2,1)}, bf16[24,2432]{1,0:T(8,128)(2,1)S(1)}, u32[]{:S(2)}, u32[]{:S(2)}) collective-permute-start(bf16[24,2432]{1,0:T(8,128)(2,1)} %get-tuple-element.259), channel_id=1, source_target_pairs={{0,8},{4,12},{8,0},{12,4},{16,24},{20,28},{24,16},{28,20},{1,9},{5... | collective-permute-start | bytes 350216 | tf_op jit(solution)/shard_map/ppermute | solution.py:843
  324.1 12.8 %collective-permute-start.31 = (bf16[24,2432]{1,0:T(8,128)(2,1)}, bf16[24,2432]{1,0:T(8,128)(2,1)}, u32[]{:S(2)}, u32[]{:S(2)}) collective-permute-start(bf16[24,2432]{1,0:T(8,128)(2,1)} %get-tuple-element.261), channel_id=1, source_target_pairs={{0,16},{4,20},{8,24},{12,28},{16,0},{20,4},{24,8},{28,12},{1,17},{... | collective-permute-start | bytes 350216 | tf_op jit(solution)/shard_map/ppermute | solution.py:843
  325.7 11.1 %collective-permute-start.32 = (bf16[24,2432]{1,0:T(8,128)(2,1)S(1)}, bf16[24,2432]{1,0:T(8,128)(2,1)}, u32[]{:S(2)}, u32[]{:S(2)}) collective-permute-start(bf16[24,2432]{1,0:T(8,128)(2,1)S(1)} %get-tuple-element.260), channel_id=1, source_target_pairs={{0,24},{4,28},{8,16},{12,20},{16,8},{20,12},{24,0},{28,4},{1,25},{... | collective-permute-start | bytes 350216 | tf_op jit(solution)/shard_map/ppermute | solution.py:843
  328.0 2.1 copy-start
  328.0 2.7 copy-start.2
  340.2 5.1 %copy-start.11 = (f32[1,7040]{1,0:T(1,128)S(1)}, f32[1,7040]{1,0:T(1,128)}, u32[]{:S(2)}) copy-start(f32[1,7040]{1,0:T(1,128)} %stats.1) | copy-start | bytes 84484
  340.2 8.7 %copy-start.3 = (f32[1024,768]{1,0:T(8,128)S(1)}, f32[1024,768]{1,0:T(8,128)}, u32[]{:S(2)}) copy-start(f32[1024,768]{1,0:T(8,128)} %get-tuple-element.145) | copy-start | bytes 9437188
  340.2 5.0 %collective-permute-start.34 = (f32[1,7040]{1,0:T(1,128)}, f32[1,7040]{1,0:T(1,128)S(1)}, u32[]{:S(2)}, u32[]{:S(2)}) collective-permute-start(f32[1,7040]{1,0:T(1,128)} %stats.1), channel_id=1, source_target_pairs={{0,1},{1,0},{2,3},{3,2},{4,5},{5,4},{6,7},{7,6},{8,9},{9,8},{10,11... | collective-permute-start | bytes 84488 | tf_op jit(solution)/shard_map/ppermute | solution.py:950
  340.2 5.0 %collective-permute-start.35 = (f32[1,7040]{1,0:T(1,128)}, f32[1,7040]{1,0:T(1,128)S(1)}, u32[]{:S(2)}, u32[]{:S(2)}) collective-permute-start(f32[1,7040]{1,0:T(1,128)} %stats.1), channel_id=1, source_target_pairs={{0,2},{1,3},{2,0},{3,1},{4,6},{5,7},{6,4},{7,5},{8,10},{9,11},{10,... | collective-permute-start | bytes 84488 | tf_op jit(solution)/shard_map/ppermute | solution.py:950
  341.7 3.6 collective-permute-start.36
  345.3 5.8 %collective-permute-start.37 = (f32[1,7040]{1,0:T(1,128)S(1)}, f32[1,7040]{1,0:T(1,128)S(1)}, u32[]{:S(2)}, u32[]{:S(2)}) collective-permute-start(f32[1,7040]{1,0:T(1,128)S(1)} %add_add_fusion.1), channel_id=1, source_target_pairs={{0,4},{4,0},{8,12},{12,8},{16,20},{20,16},{24,28},{28,24},{1,5},{5... | collective-permute-start | bytes 84488 | tf_op jit(solution)/shard_map/ppermute | solution.py:950
  345.9 5.2 %collective-permute-start.38 = (f32[1,7040]{1,0:T(1,128)S(1)}, f32[1,7040]{1,0:T(1,128)S(1)}, u32[]{:S(2)}, u32[]{:S(2)}) collective-permute-start(f32[1,7040]{1,0:T(1,128)S(1)} %add_add_fusion.1), channel_id=1, source_target_pairs={{0,8},{4,12},{8,0},{12,4},{16,24},{20,28},{24,16},{28,20},{1,9},{5... | collective-permute-start | bytes 84488 | tf_op jit(solution)/shard_map/ppermute | solution.py:950
  346.3 4.8 %collective-permute-start.39 = (f32[1,7040]{1,0:T(1,128)S(1)}, f32[1,7040]{1,0:T(1,128)S(1)}, u32[]{:S(2)}, u32[]{:S(2)}) collective-permute-start(f32[1,7040]{1,0:T(1,128)S(1)} %add_add_fusion.1), channel_id=1, source_target_pairs={{0,12},{4,8},{8,4},{12,0},{16,28},{20,24},{24,20},{28,16},{1,13},{... | collective-permute-start | bytes 84488 | tf_op jit(solution)/shard_map/ppermute | solution.py:950
  351.3 4.9 %collective-permute-start.40 = (f32[1,7040]{1,0:T(1,128)S(1)}, f32[1,7040]{1,0:T(1,128)S(1)}, u32[]{:S(2)}, u32[]{:S(2)}) collective-permute-start(f32[1,7040]{1,0:T(1,128)S(1)} %add_add_fusion), channel_id=1, source_target_pairs={{0,16},{4,20},{8,24},{12,28},{16,0},{20,4},{24,8},{28,12},{1,17},{... | collective-permute-start | bytes 84488 | tf_op jit(solution)/shard_map/ppermute | solution.py:950
  (3 other events, 3.2 us)
Sparse Core Ops, SparseCore 0:
  11.0 117.1 all-gather.1
where the time goes:
time: 373 us; the launch traced here: 367 us
  Pallas kernels  144 us (39%)
  waiting for transfers between devices  96.1 us (26%)
  starting transfers between devices  46.3 us (12%)
  matrix products  24.7 us (7%)
  other arithmetic  22.7 us (6%)
  local copies, waits for them, and re-layouts  18.9 us (5%)
  between operations  15.1 us (4%)
    ppermute x27, waiting for transfers between devices, swap(): return lax.ppermute(value, axis, [(i, i ^ 1 << bit) for i in range(size)])  86.7 us
    pallas_call x1, Pallas kernels, feed(): pl.pallas_call(feed_kernel, grid=(rows // block,), in_specs=[row_block(wi...  48.2 us
    pallas_call x3, Pallas kernels, per_seq(): pl.pallas_call(body, grid=(seqs,), in_specs=[pl.BlockSpec(memory_space=pl...  32.3 us
    pallas_call x2, Pallas kernels, back(): pl.pallas_call(functools.partial(back_kernel, which), grid=(1,), in_specs...  30 us
    ppermute x27, starting transfers between devices, swap(): return lax.ppermute(value, axis, [(i, i ^ 1 << bit) for i in range(size)])  28.3 us
    pallas_call x2, Pallas kernels, pool_back(): pl.pallas_call(functools.partial(pool_back_kernel, first, last), grid=(1,...  20.3 us
    dot_general x3, matrix products, outer(): lax.dot_general(left, right, (((0,), (0,)), ((), ())), preferred_element_...  17 us
    pallas_call x4, Pallas kernels, whole_call(): pl.pallas_call(body, out_shape=[jax.ShapeDtypeStruct(shape, dtype) for sh...  12.9 us
  transfers between devices with their start and end apart: 42, of which 18 were waited for; matrix products, arithmetic and copies ran while one was open for 11% of the time, Pallas kernels for 24%

commit v1 on v0

--- a/solution.py
+++ b/solution.py
@@ -46,6 +46,7 @@
 BF16 = jnp.bfloat16
 CUT = 1280
 TOGETHER = 3
+BUFFERS = 4
 BACK_TOGETHER = 2
 VMEM_LIMIT = 60 * 1024 * 1024
 
@@ -553,7 +554,7 @@
     sums = rest.pop(0) if last else None
     full_grad = rest.pop(0)
     outs = [rest.pop(0), rest.pop(0)]
-    held, spread, window, taps_grad = rest
+    held_all, spread_all, window_all, taps_grad = rest
     piece = full_grad.shape[1]
     pools = piece // 4
     even = (info[0] // piece) % 2 == 0
@@ -578,6 +579,7 @@
     for group in range(2 * GROUPS):
         if group % 4 == 0:
             product(group // 4)
+        held, spread, window = [entry.at[group % BUFFERS] for entry in (held_all, spread_all, window_all)]
         part = group // GROUPS
         cols = lanes_of(group % GROUPS)
         source = key if part == 0 else value
@@ -640,9 +642,9 @@
         out_shape=[jax.ShapeDtypeStruct((1, piece, 3 * width), BF16)]
         + [jax.ShapeDtypeStruct(shape, dtype) for shape, dtype in outs],
         scratch_shapes=[
-            pltpu.VMEM((pools + 16, LANES), F32),
-            pltpu.VMEM((piece, LANES), F32),
-            pltpu.VMEM((piece + 32, LANES), F32),
+            pltpu.VMEM((BUFFERS, pools + 16, LANES), F32),
+            pltpu.VMEM((BUFFERS, piece, LANES), F32),
+            pltpu.VMEM((BUFFERS, piece + 32, LANES), F32),
             pltpu.VMEM((16, width), F32),
         ],
         compiler_params=params(),
@@ -720,7 +722,8 @@
     out[:, 9 * D :] = tail
 
 
-def stats_kernel(early, base, out):
+def stats_kernel(own, one, two, three, base, out, early):
+    early[...] = sum(entry[...].astype(F32) for entry in (own, one, two, three))
     out[:, : 3 * D] = squares(early[:, : 3 * D])
     out[:, 3 * D : 9 * D] = base[:, 3 * D : 9 * D]
     lane = lax.broadcasted_iota(jnp.int32, (1, LANES), 1)
@@ -885,6 +888,11 @@
     return (value, [other for other in left if other not in gone], steps[1:], lead)
 
 
+def scatter_blocks(state):
+    value, left, ((axis, bit, count),), lead = state
+    return (halves if count == 1 else quarters)(value, axis, bit, lead)
+
+
 def scatter_end(state, gate=None):
     while state[2]:
         state = scatter_step(state, gate)
@@ -1027,15 +1035,16 @@
         block_out, first_grad, hidden_low, active, up_grad, branch_grad, mixed_grad, att_grad, sums,
     ) = feed(flat, att_flat, cot, packed, vectors)
 
+    merge_local = outer(att_flat, mixed_grad).astype(BF16).reshape(1, devices, rows, D)
+    merge_chain = scatter_step(scatter_begin(merge_local, late_steps(True), 1))
+    merge_local, branch_grad = lax.optimization_barrier((merge_local, branch_grad))
     shrink_local = outer(active, branch_grad).astype(BF16).reshape(chunks, devices, rows, D)
-    merge_local = outer(att_flat, mixed_grad).astype(BF16).reshape(1, devices, rows, D)
-    shrink_local, merge_local, up_grad = lax.optimization_barrier((shrink_local, merge_local, up_grad))
     shrink_chain = scatter_step(scatter_begin(shrink_local, late_steps(True), 1))
-    merge_chain = scatter_step(scatter_begin(merge_local, late_steps(True), 1))
+    (merge_chain,), (shrink_local, up_grad) = after([merge_chain], (shrink_local, up_grad))
+    expand_local = outer(hidden_low, up_grad).astype(BF16).reshape(devices, rows, FF)
+    expand_chain = scatter_step(scatter_begin(expand_local, late_steps(False)))
     late_chain = (jnp.concatenate([shrink_chain[0], merge_chain[0]], axis=0),) + shrink_chain[1:]
-    expand_local = outer(hidden_low, up_grad).astype(BF16).reshape(devices, rows, FF)
-    expand_chain = scatter_begin(expand_local, late_steps(False))
-    chains = [late_chain, scatter_step(expand_chain)]
+    chains = [late_chain, expand_chain]
 
     def seq_rows(value, which):
         return value[which * piece : (which + 1) * piece]
@@ -1075,12 +1084,25 @@
         for entry, first in zip(before, ("seq", "grp"))
     ]
     for _ in range(bits_of("grp")):
+        early_gate = early_chains[0][0]
         early_chains = [scatter_step(state) for state in early_chains]
     early_chain = (
         jnp.concatenate([state[0] for state in early_chains], axis=-1),
     ) + early_chains[0][1:]
-    late_sum = scatter_end(late_chain, early_chain[0])
-    early_sum = scatter_end(early_chain)
+    late_sum = scatter_end(late_chain, early_gate)
+    base, expand_sum, shrink_sum = whole_call(
+        late_kernel,
+        [((1, 9 * D + LANES), F32), ((rows, FF), F32), ((ff_rows, D), F32)],
+        (late_sum,) + tuple(old_rows),
+        "late_stats",
+        3,
+        [pltpu.VMEM((GROUPS, ff_rows, LANES), F32)],
+    )
+    (early_chain,), base = after([early_chain], base)
+    while len(early_chain[2]) > 1:
+        early_chain = scatter_step(early_chain)
+    early_blocks = scatter_blocks(early_chain)
+    early_blocks += [jnp.zeros_like(early_blocks[0])] * (4 - len(early_blocks))
     full_parts, _ = lax.optimization_barrier((full_parts, early_chain[0]))
     input_grad = jnp.stack(
         [
@@ -1092,17 +1114,13 @@
     )
 
     masters = (qkv_weight, merge_weight, expand_weight, shrink_weight)
-    base, expand_sum, shrink_sum = whole_call(
-        late_kernel,
-        [((1, 9 * D + LANES), F32), ((rows, FF), F32), ((ff_rows, D), F32)],
-        (late_sum,) + tuple(old_rows),
-        "late_stats",
-        3,
-        [pltpu.VMEM((GROUPS, ff_rows, LANES), F32)],
-    )
-    payload = whole_call(
-        stats_kernel, [((1, 9 * D + LANES), F32)], (early_sum, base), "stats", 1
-    )[0]
+    payload, early_sum = whole_call(
+        stats_kernel,
+        [((1, 9 * D + LANES), F32), (early_blocks[0].shape, F32)],
+        (*early_blocks, base),
+        "stats",
+        1,
+    )
     payload = summed_all(payload)
     outs = [((1, 1), F32)]
     for master in masters:

time: 373 us -> 368 us (0.987)
    ppermute x27, waiting for transfers between devices: 86.7 us -> 81.5 us  [swap(): return lax.ppermute(value, axis, [(i, i ^ 1 << bit) for i in range(size)])]
  transfers between devices with their start and end apart: 42 -> 42, of which waited for: 18 -> 21; matrix products, arithmetic and copies ran while one was open for 11% -> 14% of each run, Pallas kernels for 24% -> 24%
where the time goes in v1:
time: 368 us; the launch traced here: 362 us
  Pallas kernels  143 us (39%)
  waiting for transfers between devices  93.4 us (25%)
  starting transfers between devices  43.4 us (12%)
  matrix products  24.5 us (7%)
  local copies, waits for them, and re-layouts  22 us (6%)
  other arithmetic  20.2 us (5%)
  between operations  15.1 us (4%)
    ppermute x27, waiting for transfers between devices, swap(): return lax.ppermute(value, axis, [(i, i ^ 1 << bit) for i in range(size)])  81.5 us
    pallas_call x1, Pallas kernels, feed(): pl.pallas_call(feed_kernel, grid=(rows // block,), in_specs=[row_block(wi...  48.2 us
    pallas_call x3, Pallas kernels, per_seq(): pl.pallas_call(body, grid=(seqs,), in_specs=[pl.BlockSpec(memory_space=pl...  32.4 us
    pallas_call x2, Pallas kernels, back(): pl.pallas_call(functools.partial(back_kernel, which), grid=(1,), in_specs...  30 us
    ppermute x27, starting transfers between devices, swap(): return lax.ppermute(value, axis, [(i, i ^ 1 << bit) for i in range(size)])  27.8 us
    pallas_call x2, Pallas kernels, pool_back(): pl.pallas_call(functools.partial(pool_back_kernel, first, last), grid=(1,...  20 us
    dot_general x3, matrix products, outer(): lax.dot_general(left, right, (((0,), (0,)), ((), ())), preferred_element_...  13.9 us
    pallas_call x4, Pallas kernels, whole_call(): pl.pallas_call(body, out_shape=[jax.ShapeDtypeStruct(shape, dtype) for sh...  12.8 us
  transfers between devices with their start and end apart: 42, of which 21 were waited for; matrix products, arithmetic and copies ran while one was open for 14% of the time, Pallas kernels for 24%

profile of v1, /device:TPU:0, one launch (start us, length us, event | category | flops | bytes accessed | tf_op | source)
XLA Modules:
  0.0 361.9 jit_solution(8534344282400173374)
XLA Ops:
  7.3 2.6 pack.1
  11.7 4.0 %collective-permute-start.2 = (bf16[24,2432]{1,0:T(8,128)(2,1)}, bf16[24,2432]{1,0:T(8,128)(2,1)S(1)}, u32[]{:S(2)}, u32[]{:S(2)}) collective-permute-start(bf16[24,2432]{1,0:T(8,128)(2,1)} %get-tuple-element.277), channel_id=1, source_target_pairs={{0,16},{4,20},{8,24},{12,28},{16,0},{20,4},{24,8},{28,12},{1,17},{... | collective-permute-start | bytes 350216 | tf_op jit(solution)/shard_map/ppermute | solution.py:814
  16.6 1.5 collective-permute-start
  18.0 1.3 collective-permute-start.1
  19.4 1.4 broadcast_multiply_fusion
  20.8 1.7 copy.73
  24.9 2.6 collective-permute-start.3
  27.6 10.6 %collective-permute-done.3 = bf16[2,24,2432]{2,1,0:T(8,128)(2,1)S(1)} collective-permute-done((bf16[2,24,2432]{2,1,0:T(8,128)(2,1)S(1)}, bf16[2,24,2432]{2,1,0:T(8,128)(2,1)S(1)}, u32[]{:S(2)}, u32[]{:S(2)}) %collective-permute-start.3) | collective-permute-done | bytes 233504 | tf_op jit(solution)/shard_map/ppermute | solution.py:814
  38.4 1.8 collective-permute-start.7
  40.2 1.6 collective-permute-start.4
  41.8 3.3 collective-permute-done.7
  45.2 1.5 collective-permute-start.8
  46.9 5.5 %collective-permute-done.4 = bf16[2,2,24,1280]{3,2,0,1:T(8,128)(2,1)S(1)} collective-permute-done((bf16[2,2,24,1280]{3,2,0,1:T(8,128)(2,1)S(1)}, bf16[2,2,24,1280]{3,2,0,1:T(8,128)(2,1)S(1)}, u32[]{:S(2)}, u32[]{:S(2)}) %collective-permute-start.4) | collective-permute-done | bytes 245792 | tf_op jit(solution)/shard_map/ppermute | solution.py:814
  52.6 8.2 %collective-permute-done.8 = bf16[2,2,2,24,1152]{4,3,0,1,2:T(8,128)(2,1)S(1)} collective-permute-done((bf16[2,2,2,24,1152]{4,3,0,1,2:T(8,128)(2,1)S(1)}, bf16[2,2,2,24,1152]{4,3,0,1,2:T(8,128)(2,1)S(1)}, u32[]{:S(2)}, u32[]{:S(2)}) %collective-permute-start.8) | collective-permute-done | bytes 442400 | tf_op jit(solution)/shard_map/ppermute | solution.py:814
  61.0 4.6 %collective-permute-done.5 = bf16[2,2,2,24,1280]{4,3,0,1,2:T(8,128)(2,1)S(1)} collective-permute-done((bf16[2,2,2,24,1280]{4,3,0,1,2:T(8,128)(2,1)S(1)}, bf16[2,2,2,24,1280]{4,3,0,1,2:T(8,128)(2,1)S(1)}, u32[]{:S(2)}, u32[]{:S(2)}) %collective-permute-start.5) | collective-permute-done | bytes 491552 | tf_op jit(solution)/shard_map/ppermute | solution.py:814
  66.5 1.3 copy.65
  68.7 1.5 copy.64
  70.2 10.0 %project.1 = (bf16[2,512,768]{2,1,0:T(8,128)(2,1)}, bf16[2,640,768]{2,1,0:T(8,128)(2,1)}, bf16[2,640,768]{2,1,0:T(8,128)(2,1)}, bf16[2,2,128,768]{3,2,1,0:T(8,12...) custom-call(s32[4]{0:T(128)} %pad_add_fusion.info, ...), custom_call_target="tpu_custom_call" | custom-call | flops 8000000000 | tf_op jit(solution)/shard_map/project/pallas_call | solution.py:241
  81.8 11.5 %near.1 = (f32[2,512,768]{2,1,0:T(8,128)}, f32[2,4,8,256]{3,2,1,0:T(8,128)}) custom-call(s32[4]{0:T(128)} %pad_add_fusion.info, bf16[2,512,768]{2,1,0:T(8,128)(2,1)} %get-tuple-element.138.query, bf16[2,640,768]{2,1,0:T(8,128)(2,1)} %get-tuple-element.142.key, bf16[2,640,768]{2,1,0:T(8,128)(2,1)} %get-tuple-element.143.value), custom_call_target="tpu_custom_call" | custom-call | flops 24000000000 | tf_op jit(solution)/shard_map/near/pallas_call | solution.py:241
  93.3 13.9 %collective-permute-done.10.beside = bf16[2,2,64,768]{3,2,1,0:T(8,128)(2,1)S(1)} collective-permute-done((bf16[2,2,64,768]{3,2,1,0:T(8,128)(2,1)}, bf16[2,2,64,768]{3,2,1,0:T(8,128)(2,1)S(1)}, u32[]{:S(2)}, u32[]{:S(2)}) %collective-permute-start.10) | collective-permute-done | bytes 393248 | tf_op jit(solution)/shard_map/ppermute | solution.py:814
  108.2 10.8 %far.1 = (bf16[2,512,768]{2,1,0:T(8,128)(2,1)}, bf16[2,256,768]{2,1,0:T(8,128)(2,1)}, bf16[2,256,768]{2,1,0:T(8,128)(2,1)}, f32[2,4,8,256]{3,2,1,0:T(8,128)}) custom-call(s32[4]{0:T(128)} %pad_add_fusion.info, bf16[2,512,768]{2,1,0:T(8,128)(2,1)} %get-tuple-element.138.query, bf16[2,2,128,768]{3,2,1,0:T(8,128)(2,1)} %get-tuple-element.139.pool, ...), custom_call_target="tpu_custom_call" | custom-call | flops 9600000000 | tf_op jit(solution)/shard_map/far/pallas_call | solution.py:241
  119.0 6.8 %all-gather.2.cloned.1.call-done.packed = bf16[768,6912]{1,0:T(8,128)(2,1)} async-done(((bf16[24,6912]{1,0:T(8,128)(2,1)}), bf16[768,6912]{1,0:T(8,128)(2,1)}) %all-gather.2.cloned.1.call-update) | async-done | bytes 10616848 | tf_op jit(solution)/shard_map/all_gather | solution.py:1008
  125.7 48.2 %feed.1 = (bf16[1024,768]{1,0:T(8,128)(2,1)}, f32[1024,768]{1,0:T(8,128)}, bf16[1024,768]{1,0:T(8,128)(2,1)}, bf16[1024,3072]{1,0:T(8,128)(2,1)}, bf16[1024,3072...) custom-call(bf16[1024,768]{1,0:T(8,128)(2,1)} %bitcast.182, ...), custom_call_target="tpu_custom_call" | custom-call | flops 38400000000 | tf_op jit(solution)/shard_map/feed/pallas_call | solution.py:415
  174.0 3.0 convolution_convert_fusion.2
  178.4 5.5 %convolution_convert_fusion.1 = bf16[3072,768]{1,0:T(8,128)(2,1)S(1)} fusion(bf16[1024,3072]{1,0:T(8,128)(2,1)S(1)} %copy-done.25, bf16[1024,768]{1,0:T(8,128)(2,1)S(1)} %copy-done.26), kind=kOutput, calls=%fused_computation.1 | convolution fusion | flops 4834197504 | bytes 12582912 | tf_op jit(solution)/shard_map/dot_general | solution.py:63
  184.3 1.6 copy.91
  188.3 5.4 %convolution_convert_fusion = bf16[768,3072]{1,0:T(8,128)(2,1)S(1)} fusion(bf16[1024,768]{1,0:T(8,128)(2,1)S(1)} %copy-done.24, bf16[1024,3072]{1,0:T(8,128)(2,1)S(1)} %bitcast.243), kind=kOutput, calls=%fused_computation | convolution fusion | flops 4834197504 | bytes 12582912 | tf_op jit(solution)/shard_map/dot_general | solution.py:63
  193.7 1.8 constant_dynamic-slice_fusion.1
  195.5 1.7 copy.90
  197.4 2.3 fusion.1
  200.0 2.0 collective-permute-done.14
  202.0 2.6 fusion
  207.1 1.4 dynamic-slice_bitcast_fusion
  208.5 1.5 collective-permute-start.17
  210.0 14.9 %back.2 = (bf16[1,512,768]{2,1,0:T(8,128)(2,1)}, f32[1,2,640,768]{3,2,1,0:T(8,128)}, f32[1,2,256,768]{3,2,1,0:T(8,128)}, bf16[1,2,144,768]{3,2,1,0:T(8,128)(2,1)}, bf16[1,2,144,768]{3,2,1,0:T(8,128)(2,1)}) custom-call(s32[4]{0:T(128)} %pad_add_fusion.info, bf16[2,512,768]{2,1,0:T(8,128)(2,1)} %get-tuple-element.138.query, ...), custom_call_target="tpu_custom_call" | custom-call | flops 24000000000 | tf_op jit(solution)/shard_map/back/pallas_call | solution.py:535
  225.6 15.0 %back.3 = (bf16[1,512,768]{2,1,0:T(8,128)(2,1)}, f32[1,2,640,768]{3,2,1,0:T(8,128)}, f32[1,2,256,768]{3,2,1,0:T(8,128)}, bf16[1,2,144,768]{3,2,1,0:T(8,128)(2,1)}, bf16[1,2,144,768]{3,2,1,0:T(8,128)(2,1)}) custom-call(s32[4]{0:T(128)} %pad_add_fusion.info, bf16[2,512,768]{2,1,0:T(8,128)(2,1)} %get-tuple-element.138.query, ...), custom_call_target="tpu_custom_call" | custom-call | flops 8000000 | tf_op jit(solution)/shard_map/back/pallas_call | solution.py:535
  240.6 3.7 %collective-permute-done.15.beside = bf16[1,2,144,768]{3,2,1,0:T(8,128)(2,1)S(1)} collective-permute-done((bf16[1,2,144,768]{3,2,1,0:T(8,128)(2,1)}, bf16[1,2,144,768]{3,2,1,0:T(8,128)(2,1)S(1)}, u32[]{:S(2)}, u32[]{:S(2)}) %collective-permute-start.15) | collective-permute-done | bytes 442400 | tf_op jit(solution)/shard_map/ppermute | solution.py:814
  244.3 2.4 collective-permute-start.19
  246.7 1.6 collective-permute-start.20
  248.3 1.7 add_convert_fusion.1
  250.0 1.7 add_convert_fusion
  252.6 2.0 collective-permute-start.21
  254.6 9.6 %pool_back.2 = (bf16[1,512,2304]{2,1,0:T(8,128)(2,1)}, f32[768,2304]{1,0:T(8,128)}, f32[16,768]{1,0:T(8,128)}) custom-call(s32[4]{0:T(128)} %pad_add_fusion.info, bf16[1,512,768]{2,1,0:T(8,128)(2,1)} %get-tuple-element.162.query_grad, f32[1,2,640,768]{3,2,1,0:T(8,128)} %get-tuple-element.166.near_grad, f32[1,2,256,768]{3,2,1,0:T(8,128)} %get-tuple-element.167.far_grad, ...), custom_call_target="tpu_custom_call" | custom-call | flops 24000000000 | tf_op jit(solution)/shard_map/pool_back/pallas_call | solution.py:633
  266.2 9.2 %collective-permute-done.21 = bf16[5,2,2,24,768]{4,3,2,1,0:T(8,128)(2,1)S(1)} collective-permute-done((bf16[5,2,2,24,768]{4,3,2,1,0:T(8,128)(2,1)S(1)}, bf16[5,2,2,24,768]{4,3,2,1,0:T(8,128)(2,1)S(1)}, u32[]{:S(2)}, u32[]{:S(2)}) %collective-permute-start.21) | collective-permute-done | bytes 737312 | tf_op jit(solution)/shard_map/ppermute | solution.py:814
  275.8 10.4 %pool_back.3 = (bf16[1,512,2304]{2,1,0:T(8,128)(2,1)}, bf16[768,1280]{1,0:T(8,128)(2,1)}, bf16[768,1152]{1,0:T(8,128)(2,1)}) custom-call(s32[4]{0:T(128)} %pad_add_fusion.info, bf16[1,512,768]{2,1,0:T(8,128)(2,1)} %get-tuple-element.164.query_grad, f32[1,2,640,768]{3,2,1,0:T(8,128)} %get-tuple-element.179.near_grad, ...), custom_call_target="tpu_custom_call" | custom-call | flops 8000000 | tf_op jit(solution)/shard_map/pool_back/pallas_call | solution.py:633
  286.2 4.6 %collective-permute-done.23 = bf16[2,24,6912]{2,1,0:T(8,128)(2,1)S(1)} collective-permute-done((bf16[2,24,6912]{2,1,0:T(8,128)(2,1)S(1)}, bf16[2,24,6912]{2,1,0:T(8,128)(2,1)S(1)}, u32[]{:S(2)}, u32[]{:S(2)}) %collective-permute-start.23) | collective-permute-done | bytes 663584 | tf_op jit(solution)/shard_map/ppermute | solution.py:814
  293.1 1.7 collective-permute-start.30
  296.8 10.5 %collective-permute-done.28 = bf16[2,2,2,24,1152]{4,3,2,1,0:T(8,128)(2,1)S(1)} collective-permute-done((bf16[2,2,2,24,1152]{4,3,2,1,0:T(8,128)(2,1)S(1)}, bf16[2,2,2,24,1152]{4,3,2,1,0:T(8,128)(2,1)S(1)}, u32[]{:S(2)}, u32[]{:S(2)}) %collective-permute-start.28) | collective-permute-done | bytes 442400 | tf_op jit(solution)/shard_map/ppermute | solution.py:814
  307.8 2.3 collective-permute-done.25
  310.3 1.5 collective-permute-start.26
  312.7 4.9 %late_stats.1 = (f32[1,7040]{1,0:T(1,128)}, f32[24,3072]{1,0:T(8,128)}, f32[96,768]{1,0:T(8,128)}) custom-call(f32[24,6912]{1,0:T(8,128)} %convert_add_fusion.8.late, f32[1,24]{1,0:T(1,128)} %bitcast.219, f32[1,24]{1,0:T(1,128)} %bitcast.221, f32[1,24]{1,0:T(1,128)} %bitcast.223, f32[1,96]{1,0:T(1,128)} %bitcast.225), custom_call_target="tpu_custom_call" | custom-call | flops 2400000000 | tf_op jit(solution)/shard_map/late_stats/pallas_call | solution.py:800
  318.9 1.6 collective-permute-start.32
  320.6 2.8 collective-permute-start.33
  323.3 2.7 fusion.15
  326.2 2.5 add_bitcast_fusion.1
  328.7 1.7 collective-permute-done.32.two
  331.0 1.9 stats.1
  334.7 3.2 fusion.13
  339.2 1.8 collective-permute-start.38
  341.6 2.3 add_bitcast_fusion
  343.9 1.9 collective-permute-done.39
  347.1 2.0 pad_maximum_fusion
  349.1 1.6 collective-permute-done.40
  351.3 3.5 update.1
  (176 shorter events, 34.9 us)
Async XLA Ops:
  7.2 3.8 %copy-start.11 = (f32[24,14]{0,1:T(8,128)S(1)}, f32[24,14]{0,1:T(8,128)}, u32[]{:S(2)}) copy-start(f32[24,14]{0,1:T(8,128)} %param.26) | copy-start | bytes 4036
  7.2 8.6 %copy-start.4 = (bf16[2,512,768]{2,1,0:T(8,128)(2,1)S(1)}, bf16[2,512,768]{2,1,0:T(8,128)(2,1)}, u32[]{:S(2)}) copy-start(bf16[2,512,768]{2,1,0:T(8,128)(2,1)} %own.1) | copy-start | bytes 4718596
  7.2 118.5 %all-gather.2.cloned.1.call-start = ((), (), s32[]{:S(2)}) async-start(), calls=%async_computation | async-start | bytes 10948608 | tf_op jit(solution)/shard_map/all_gather | solution.py:1008
  9.9 9.5 %copy-start.14 = (s32[2,512]{1,0:T(2,128)S(1)}, s32[2,512]{1,0:T(2,128)}, u32[]{:S(2)}) copy-start(s32[2,512]{1,0:T(2,128)} %param.20) | copy-start | bytes 12292
  9.9 9.5 %copy-start.8 = (bf16[2,512,768]{2,1,0:T(8,128)(2,1)S(1)}, bf16[2,512,768]{2,1,0:T(8,128)(2,1)}, u32[]{:S(2)}) copy-start(bf16[2,512,768]{2,1,0:T(8,128)(2,1)} %param.21) | copy-start | bytes 4718596
  11.7 13.1 %collective-permute-start.2 = (bf16[24,2432]{1,0:T(8,128)(2,1)}, bf16[24,2432]{1,0:T(8,128)(2,1)S(1)}, u32[]{:S(2)}, u32[]{:S(2)}) collective-permute-start(bf16[24,2432]{1,0:T(8,128)(2,1)} %get-tuple-element.277), channel_id=1, source_target_pairs={{0,16},{4,20},{8,24},{12,28},{16,0},{20,4},{24,8},{28,12},{1,17},{... | collective-permute-start | bytes 350216 | tf_op jit(solution)/shard_map/ppermute | solution.py:814
  16.6 53.7 %collective-permute-start = (bf16[2,64,768]{2,1,0:T(8,128)(2,1)}, bf16[2,64,768]{2,1,0:T(8,128)(2,1)}, u32[]{:S(2)}, u32[]{:S(2)}) collective-permute-start(bf16[2,64,768]{2,1,0:T(8,128)(2,1)} %get-tuple-element.256), channel_id=1, source_target_pairs={{0,4},{4,0},{8,12},{12,8},{16,20},{20,16},{24,28},{28,24},{1,5},{5... | collective-permute-start | bytes 589832 | tf_op jit(solution)/shard_map/ppermute | solution.py:814
  18.0 52.2 %collective-permute-start.1 = (bf16[2,64,768]{2,1,0:T(8,128)(2,1)}, bf16[2,64,768]{2,1,0:T(8,128)(2,1)}, u32[]{:S(2)}, u32[]{:S(2)}) collective-permute-start(bf16[2,64,768]{2,1,0:T(8,128)(2,1)} %get-tuple-element.255), channel_id=1, source_target_pairs={{4,8},{8,4},{12,16},{16,12},{20,24},{24,20},{5,9},{9,5},{13,17},{1... | collective-permute-start | bytes 589832 | tf_op jit(solution)/shard_map/ppermute | solution.py:931
  20.8 2.3 copy-start.12
  20.8 2.9 copy-start.13
  20.8 3.5 copy-start.15
  24.9 13.3 %collective-permute-start.3 = (bf16[2,24,2432]{2,1,0:T(8,128)(2,1)S(1)}, bf16[2,24,2432]{2,1,0:T(8,128)(2,1)S(1)}, u32[]{:S(2)}, u32[]{:S(2)}) collective-permute-start(bf16[2,24,2432]{2,1,0:T(8,128)(2,1)S(1)} %maximum_select_fusion.12), channel_id=1, source_target_pairs={{0,8},{4,12},{8,0},{12,4},{16,24},{20,28},{24,16},{28,20},{1,9},{5... | collective-permute-start | bytes 700424 | tf_op jit(solution)/shard_map/ppermute | solution.py:814
  38.4 6.7 %collective-permute-start.7 = (bf16[2,2,24,1152]{3,2,0,1:T(8,128)(2,1)S(1)}, bf16[2,2,24,1152]{3,2,0,1:T(8,128)(2,1)S(1)}, u32[]{:S(2)}, u32[]{:S(2)}) collective-permute-start(bf16[2,2,24,1152]{3,2,0,1:T(8,128)(2,1)S(1)} %get-tuple-element.271), channel_id=1, source_target_pairs={{0,4},{4,0},{8,12},{12,8},{16,20},{20,16},{24,28},{28,24},{1,5},{5... | collective-permute-start | bytes 663560 | tf_op jit(solution)/shard_map/ppermute | solution.py:814
  40.2 12.1 %collective-permute-start.4 = (bf16[2,2,24,1280]{3,2,0,1:T(8,128)(2,1)S(1)}, bf16[2,2,24,1280]{3,2,0,1:T(8,128)(2,1)S(1)}, u32[]{:S(2)}, u32[]{:S(2)}) collective-permute-start(bf16[2,2,24,1280]{3,2,0,1:T(8,128)(2,1)S(1)} %get-tuple-element.274), channel_id=1, source_target_pairs={{0,2},{1,3},{2,0},{3,1},{4,6},{5,7},{6,4},{7,5},{8,10},{9,11},{10,... | collective-permute-start | bytes 737288 | tf_op jit(solution)/shard_map/ppermute | solution.py:814
  45.2 15.6 %collective-permute-start.8 = (bf16[2,2,2,24,1152]{4,3,0,1,2:T(8,128)(2,1)S(1)}, bf16[2,2,2,24,1152]{4,3,0,1,2:T(8,128)(2,1)S(1)}, u32[]{:S(2)}, u32[]{:S(2)}) collective-permute-start(bf16[2,2,2,24,1152]{4,3,0,1,2:T(8,128)(2,1)S(1)} %maximum_select_fusion.10), channel_id=1, source_target_pairs={{0,2},{1,3},{2,0},{3,1},{4,6},{5,7},{6,4},{7,5},{8,10},{9,11},{10,... | collective-permute-start | bytes 1327112 | tf_op jit(solution)/shard_map/ppermute | solution.py:814
  52.4 13.1 %collective-permute-start.5 = (bf16[2,2,2,24,1280]{4,3,0,1,2:T(8,128)(2,1)S(1)}, bf16[2,2,2,24,1280]{4,3,0,1,2:T(8,128)(2,1)S(1)}, u32[]{:S(2)}, u32[]{:S(2)}) collective-permute-start(bf16[2,2,2,24,1280]{4,3,0,1,2:T(8,128)(2,1)S(1)} %maximum_select_fusion.7), channel_id=1, source_target_pairs={{0,4},{4,0},{8,12},{12,8},{16,20},{20,16},{24,28},{28,24},{1,5},{5... | collective-permute-start | bytes 1474568 | tf_op jit(solution)/shard_map/ppermute | solution.py:814
  60.9 5.3 %collective-permute-start.9 = (bf16[2,2,2,2,24,1152]{5,4,0,1,2,3:T(8,128)(2,1)S(1)}, bf16[2,2,2,2,24,1152]{5,4,0,1,2,3:T(8,128)(2,1)S(1)}, u32[]{:S(2)}, u32[]{:S(2)}) collective-permute-start(bf16[2,2,2,2,24,1152]{5,4,0,1,2,3:T(8,128)(2,1)S(1)} %maximum_select_fusion.5), channel_id=1, source_target_pairs={{0,1},{1,0},{2,3},{3,2},{4,5},{5,4},{6,7},{7,6},{8,9},{9,8},{10,11... | collective-permute-start | bytes 2654216 | tf_op jit(solution)/shard_map/ppermute | solution.py:814
  65.7 2.6 collective-permute-start.6
  80.2 27.0 %collective-permute-start.10 = (bf16[2,2,64,768]{3,2,1,0:T(8,128)(2,1)}, bf16[2,2,64,768]{3,2,1,0:T(8,128)(2,1)S(1)}, u32[]{:S(2)}, u32[]{:S(2)}) collective-permute-start(bf16[2,2,64,768]{3,2,1,0:T(8,128)(2,1)} %get-tuple-element.140), channel_id=1, source_target_pairs={{0,4},{4,0},{8,12},{12,8},{16,20},{20,16},{24,28},{28,24},{1,5},{5... | collective-permute-start | bytes 1179656 | tf_op jit(solution)/shard_map/ppermute | solution.py:814
  80.9 26.4 %collective-permute-start.11 = (bf16[2,2,64,768]{3,2,1,0:T(8,128)(2,1)}, bf16[2,2,64,768]{3,2,1,0:T(8,128)(2,1)S(1)}, u32[]{:S(2)}, u32[]{:S(2)}) collective-permute-start(bf16[2,2,64,768]{3,2,1,0:T(8,128)(2,1)} %get-tuple-element.141), channel_id=1, source_target_pairs={{4,8},{8,4},{12,16},{16,12},{20,24},{24,20},{5,9},{9,5},{13,17},{1... | collective-permute-start | bytes 1179656 | tf_op jit(solution)/shard_map/ppermute | solution.py:931
  125.7 48.2 %copy-start.23 = (bf16[2,512,768]{2,1,0:T(8,128)(2,1)S(1)}, bf16[2,512,768]{2,1,0:T(8,128)(2,1)}, u32[]{:S(2)}) copy-start(bf16[2,512,768]{2,1,0:T(8,128)(2,1)} %get-tuple-element.145) | copy-start | bytes 4718596
  173.9 3.5 copy-start.25
  177.1 9.1 %collective-permute-start.13 = (bf16[1,2,2,2,2,24,768]{6,5,3,2,1,0,4:T(8,128)(2,1)S(1)}, bf16[1,2,2,2,2,24,768]{6,5,3,2,1,0,4:T(8,128)(2,1)S(1)}, u32[]{:S(2)}, u32[]{:S(2)}) collective-permute-start(bf16[1,2,2,2,2,24,768]{6,5,3,2,1,0,4:T(8,128)(2,1)S(1)} %bitcast.208), channel_id=1, source_target_pairs={{0,1},{1,0},{2,3},{3,2},{4,5},{5,4},{6,7},{7,6},{8,9},{9,8},{10,11... | collective-permute-start | bytes 1769480 | tf_op jit(solution)/shard_map/ppermute | solution.py:814
  183.9 3.0 slice-start
  183.9 3.7 %slice-start.1 = ((s8[6291456]{0:T(1024)(128)(4,1)}), s8[2097152]{0:T(1024)(128)(4,1)S(1)}, s32[]{:S(2)}) async-start(s8[6291456]{0:T(1024)(128)(4,1)} %bitcast.242), calls=%async_computation.2 | async-start | bytes 4194304
  185.9 2.4 copy-start.24
  185.9 11.5 %collective-permute-start.12 = (bf16[4,2,2,2,2,24,768]{6,5,3,2,1,0,4:T(8,128)(2,1)}, bf16[4,2,2,2,2,24,768]{6,5,3,2,1,0,4:T(8,128)(2,1)}, u32[]{:S(2)}, u32[]{:S(2)}) collective-permute-start(bf16[4,2,2,2,2,24,768]{6,5,3,2,1,0,4:T(8,128)(2,1)} %bitcast.173), channel_id=1, source_target_pairs={{0,1},{1,0},{2,3},{3,2},{4,5},{5,4},{6,7},{7,6},{8,9},{9,8},{10,11... | collective-permute-start | bytes 7077896 | tf_op jit(solution)/shard_map/ppermute | solution.py:814
  197.1 4.9 %collective-permute-start.14 = (bf16[2,2,2,2,24,3072]{5,4,3,2,0,1:T(8,128)(2,1)}, bf16[2,2,2,2,24,3072]{5,4,3,2,0,1:T(8,128)(2,1)}, u32[]{:S(2)}, u32[]{:S(2)}) collective-permute-start(bf16[2,2,2,2,24,3072]{5,4,3,2,0,1:T(8,128)(2,1)} %bitcast.172), channel_id=1, source_target_pairs={{0,1},{1,0},{2,3},{3,2},{4,5},{5,4},{6,7},{7,6},{8,9},{9,8},{10,11... | collective-permute-start | bytes 7077896 | tf_op jit(solution)/shard_map/ppermute | solution.py:814
  199.7 2.3 copy-start.1
  205.8 42.5 %collective-permute-start.18 = (bf16[2,2,2,24,3072]{4,3,2,1,0:T(8,128)(2,1)}, bf16[2,2,2,24,3072]{4,3,2,1,0:T(8,128)(2,1)}, u32[]{:S(2)}, u32[]{:S(2)}) collective-permute-start(bf16[2,2,2,24,3072]{4,3,2,1,0:T(8,128)(2,1)} %get-tuple-element.253), channel_id=1, source_target_pairs={{0,8},{4,12},{8,0},{12,4},{16,24},{20,28},{24,16},{28,20},{1,9},{5... | collective-permute-start | bytes 3538952 | tf_op jit(solution)/shard_map/ppermute | solution.py:814
  208.5 41.5 %collective-permute-start.17 = (bf16[5,2,2,2,24,768]{5,4,3,2,1,0:T(8,128)(2,1)}, bf16[5,2,2,2,24,768]{5,4,3,2,1,0:T(8,128)(2,1)}, u32[]{:S(2)}, u32[]{:S(2)}) collective-permute-start(bf16[5,2,2,2,24,768]{5,4,3,2,1,0:T(8,128)(2,1)} %get-tuple-element.251), channel_id=1, source_target_pairs={{0,2},{1,3},{2,0},{3,1},{4,6},{5,7},{6,4},{7,5},{8,10},{9,11},{10,... | collective-permute-start | bytes 4423688 | tf_op jit(solution)/shard_map/ppermute | solution.py:814
  224.9 19.4 %collective-permute-start.15 = (bf16[1,2,144,768]{3,2,1,0:T(8,128)(2,1)}, bf16[1,2,144,768]{3,2,1,0:T(8,128)(2,1)S(1)}, u32[]{:S(2)}, u32[]{:S(2)}) collective-permute-start(bf16[1,2,144,768]{3,2,1,0:T(8,128)(2,1)} %get-tuple-element.168), channel_id=1, source_target_pairs={{0,4},{4,0},{8,12},{12,8},{16,20},{20,16},{24,28},{28,24},{1,5},{5... | collective-permute-start | bytes 1327112 | tf_op jit(solution)/shard_map/ppermute | solution.py:814
  224.9 19.4 %collective-permute-start.16 = (bf16[1,2,144,768]{3,2,1,0:T(8,128)(2,1)}, bf16[1,2,144,768]{3,2,1,0:T(8,128)(2,1)S(1)}, u32[]{:S(2)}, u32[]{:S(2)}) collective-permute-start(bf16[1,2,144,768]{3,2,1,0:T(8,128)(2,1)} %get-tuple-element.169), channel_id=1, source_target_pairs={{4,8},{8,4},{12,16},{16,12},{20,24},{24,20},{5,9},{9,5},{13,17},{1... | collective-permute-start | bytes 1327112 | tf_op jit(solution)/shard_map/ppermute | solution.py:931
  244.3 5.7 %copy-start.16 = (bf16[1,2,144,768]{3,2,1,0:T(8,128)(2,1)}, bf16[1,2,144,768]{3,2,1,0:T(8,128)(2,1)S(1)}, u32[]{:S(2)}) copy-start(bf16[1,2,144,768]{3,2,1,0:T(8,128)(2,1)S(1)} %collective-permute-done.15.beside) | copy-start | bytes 1327108
  244.3 5.7 %copy-start.17 = (bf16[1,2,144,768]{3,2,1,0:T(8,128)(2,1)}, bf16[1,2,144,768]{3,2,1,0:T(8,128)(2,1)S(1)}, u32[]{:S(2)}) copy-start(bf16[1,2,144,768]{3,2,1,0:T(8,128)(2,1)S(1)} %collective-permute-done.16.across) | copy-start | bytes 1327108
  244.3 20.9 %collective-permute-start.19 = (bf16[1,2,144,768]{3,2,1,0:T(8,128)(2,1)}, bf16[1,2,144,768]{3,2,1,0:T(8,128)(2,1)}, u32[]{:S(2)}, u32[]{:S(2)}) collective-permute-start(bf16[1,2,144,768]{3,2,1,0:T(8,128)(2,1)} %get-tuple-element.183), channel_id=1, source_target_pairs={{0,4},{4,0},{8,12},{12,8},{16,20},{20,16},{24,28},{28,24},{1,5},{5... | collective-permute-start | bytes 1327112 | tf_op jit(solution)/shard_map/ppermute | solution.py:814
  246.7 18.5 %collective-permute-start.20 = (bf16[1,2,144,768]{3,2,1,0:T(8,128)(2,1)}, bf16[1,2,144,768]{3,2,1,0:T(8,128)(2,1)}, u32[]{:S(2)}, u32[]{:S(2)}) collective-permute-start(bf16[1,2,144,768]{3,2,1,0:T(8,128)(2,1)} %get-tuple-element.184), channel_id=1, source_target_pairs={{4,8},{8,4},{12,16},{16,12},{20,24},{24,20},{5,9},{9,5},{13,17},{1... | collective-permute-start | bytes 1327112 | tf_op jit(solution)/shard_map/ppermute | solution.py:931
  251.9 14.1 %collective-permute-start.22 = (bf16[2,2,24,3072]{3,2,1,0:T(8,128)(2,1)S(1)}, bf16[2,2,24,3072]{3,2,1,0:T(8,128)(2,1)S(1)}, u32[]{:S(2)}, u32[]{:S(2)}) collective-permute-start(bf16[2,2,24,3072]{3,2,1,0:T(8,128)(2,1)S(1)} %get-tuple-element.259), channel_id=1, source_target_pairs={{0,2},{1,3},{2,0},{3,1},{4,6},{5,7},{6,4},{7,5},{8,10},{9,11},{10,... | collective-permute-start | bytes 1769480 | tf_op jit(solution)/shard_map/ppermute | solution.py:814
  252.6 22.7 %collective-permute-start.21 = (bf16[5,2,2,24,768]{4,3,2,1,0:T(8,128)(2,1)S(1)}, bf16[5,2,2,24,768]{4,3,2,1,0:T(8,128)(2,1)S(1)}, u32[]{:S(2)}, u32[]{:S(2)}) collective-permute-start(bf16[5,2,2,24,768]{4,3,2,1,0:T(8,128)(2,1)S(1)} %get-tuple-element.257), channel_id=1, source_target_pairs={{0,8},{4,12},{8,0},{12,4},{16,24},{20,28},{24,16},{28,20},{1,9},{5... | collective-permute-start | bytes 2211848 | tf_op jit(solution)/shard_map/ppermute | solution.py:814
  275.7 15.1 %collective-permute-start.23 = (bf16[2,24,6912]{2,1,0:T(8,128)(2,1)S(1)}, bf16[2,24,6912]{2,1,0:T(8,128)(2,1)S(1)}, u32[]{:S(2)}, u32[]{:S(2)}) collective-permute-start(bf16[2,24,6912]{2,1,0:T(8,128)(2,1)S(1)} %dynamic-slice_bitcast_fusion.8), channel_id=1, source_target_pairs={{0,4},{4,0},{8,12},{12,8},{16,20},{20,16},{24,28},{28,24},{1,5},{5... | collective-permute-start | bytes 1990664 | tf_op jit(solution)/shard_map/ppermute | solution.py:814
  286.2 6.1 %copy-start.6 = (bf16[768,1280]{1,0:T(8,128)(2,1)S(1)}, bf16[768,1280]{1,0:T(8,128)(2,1)}, u32[]{:S(2)}) copy-start(bf16[768,1280]{1,0:T(8,128)(2,1)} %get-tuple-element.200) | copy-start | bytes 5898244
  292.3 2.5 copy-start.7
  292.3 2.5 collective-permute-start.27
  292.4 3.7 %collective-permute-start.24 = (bf16[2,2,2,2,24,1280]{5,4,3,2,1,0:T(8,128)(2,1)S(1)}, bf16[2,2,2,2,24,1280]{5,4,3,2,1,0:T(8,128)(2,1)S(1)}, u32[]{:S(2)}, u32[]{:S(2)}) collective-permute-start(bf16[2,2,2,2,24,1280]{5,4,3,2,1,0:T(8,128)(2,1)S(1)} %dynamic-slice_bitcast_fusion.4), channel_id=1, source_target_pairs={{0,1},{1,0},{2,3},{3,2},{4,5},{5,4},{6,7},{7,6},{8,9},{9,8},{10,11... | collective-permute-start | bytes 2949128 | tf_op jit(solution)/shard_map/ppermute | solution.py:814
  293.1 17.2 %collective-permute-start.30 = (bf16[24,6912]{1,0:T(8,128)(2,1)S(1)}, bf16[24,6912]{1,0:T(8,128)(2,1)S(1)}, u32[]{:S(2)}, u32[]{:S(2)}) collective-permute-start(bf16[24,6912]{1,0:T(8,128)(2,1)S(1)} %get-tuple-element.263), channel_id=1, source_target_pairs={{0,16},{4,20},{8,24},{12,28},{16,0},{20,4},{24,8},{28,12},{1,17},{... | collective-permute-start | bytes 995336 | tf_op jit(solution)/shard_map/ppermute | solution.py:814
  295.1 12.3 %collective-permute-start.28 = (bf16[2,2,2,24,1152]{4,3,2,1,0:T(8,128)(2,1)S(1)}, bf16[2,2,2,24,1152]{4,3,2,1,0:T(8,128)(2,1)S(1)}, u32[]{:S(2)}, u32[]{:S(2)}) collective-permute-start(bf16[2,2,2,24,1152]{4,3,2,1,0:T(8,128)(2,1)S(1)} %dynamic-slice_bitcast_fusion.12), channel_id=1, source_target_pairs={{0,2},{1,3},{2,0},{3,1},{4,6},{5,7},{6,4},{7,5},{8,10},{9,11},{10,... | collective-permute-start | bytes 1327112 | tf_op jit(solution)/shard_map/ppermute | solution.py:814
  296.5 13.6 %collective-permute-start.25 = (bf16[2,2,2,24,1280]{4,3,2,1,0:T(8,128)(2,1)S(1)}, bf16[2,2,2,24,1280]{4,3,2,1,0:T(8,128)(2,1)S(1)}, u32[]{:S(2)}, u32[]{:S(2)}) collective-permute-start(bf16[2,2,2,24,1280]{4,3,2,1,0:T(8,128)(2,1)S(1)} %dynamic-slice_bitcast_fusion.11), channel_id=1, source_target_pairs={{0,4},{4,0},{8,12},{12,8},{16,20},{20,16},{24,28},{28,24},{1,5},{5... | collective-permute-start | bytes 1474568 | tf_op jit(solution)/shard_map/ppermute | solution.py:814
  307.5 10.0 %collective-permute-start.29 = (bf16[2,2,24,1152]{3,2,1,0:T(8,128)(2,1)S(1)}, bf16[2,2,24,1152]{3,2,1,0:T(8,128)(2,1)S(1)}, u32[]{:S(2)}, u32[]{:S(2)}) collective-permute-start(bf16[2,2,24,1152]{3,2,1,0:T(8,128)(2,1)S(1)} %dynamic-slice_bitcast_fusion.16), channel_id=1, source_target_pairs={{0,4},{4,0},{8,12},{12,8},{16,20},{20,16},{24,28},{28,24},{1,5},{5... | collective-permute-start | bytes 663560 | tf_op jit(solution)/shard_map/ppermute | solution.py:814
  310.3 7.9 %collective-permute-start.26 = (bf16[2,2,24,1280]{3,2,1,0:T(8,128)(2,1)S(1)}, bf16[2,2,24,1280]{3,2,1,0:T(8,128)(2,1)S(1)}, u32[]{:S(2)}, u32[]{:S(2)}) collective-permute-start(bf16[2,2,24,1280]{3,2,1,0:T(8,128)(2,1)S(1)} %dynamic-slice_bitcast_fusion.15), channel_id=1, source_target_pairs={{0,2},{1,3},{2,0},{3,1},{4,6},{5,7},{6,4},{7,5},{8,10},{9,11},{10,... | collective-permute-start | bytes 737288 | tf_op jit(solution)/shard_map/ppermute | solution.py:814
  317.5 5.8 %copy-start.5 = (bf16[2,2,2,2,2,24,1280]{6,5,4,3,2,1,0:T(8,128)(2,1)S(1)}, bf16[2,2,2,2,2,24,1280]{6,5,4,3,2,1,0:T(8,128)(2,1)}, u32[]{:S(2)}) copy-start(bf16[2,2,2,2,2,24,1280]{6,5,4,3,2,1,0:T(8,128)(2,1)} %copy.64) | copy-start | bytes 5898244
  318.9 9.7 %collective-permute-start.31 = (bf16[24,2432]{1,0:T(8,128)(2,1)S(1)}, bf16[24,2432]{1,0:T(8,128)(2,1)S(1)}, u32[]{:S(2)}, u32[]{:S(2)}) collective-permute-start(bf16[24,2432]{1,0:T(8,128)(2,1)S(1)} %get-tuple-element.267), channel_id=1, source_target_pairs={{0,8},{4,12},{8,0},{12,4},{16,24},{20,28},{24,16},{28,20},{1,9},{5... | collective-permute-start | bytes 350216 | tf_op jit(solution)/shard_map/ppermute | solution.py:846
  318.9 11.4 %collective-permute-start.32 = (bf16[24,2432]{1,0:T(8,128)(2,1)S(1)}, bf16[24,2432]{1,0:T(8,128)(2,1)S(1)}, u32[]{:S(2)}, u32[]{:S(2)}) collective-permute-start(bf16[24,2432]{1,0:T(8,128)(2,1)S(1)} %get-tuple-element.266), channel_id=1, source_target_pairs={{0,16},{4,20},{8,24},{12,28},{16,0},{20,4},{24,8},{28,12},{1,17},{... | collective-permute-start | bytes 350216 | tf_op jit(solution)/shard_map/ppermute | solution.py:846
  320.6 9.8 %collective-permute-start.33 = (bf16[24,2432]{1,0:T(8,128)(2,1)S(1)}, bf16[24,2432]{1,0:T(8,128)(2,1)S(1)}, u32[]{:S(2)}, u32[]{:S(2)}) collective-permute-start(bf16[24,2432]{1,0:T(8,128)(2,1)S(1)} %get-tuple-element.265), channel_id=1, source_target_pairs={{0,24},{4,28},{8,16},{12,20},{16,8},{20,12},{24,0},{28,4},{1,25},{... | collective-permute-start | bytes 350216 | tf_op jit(solution)/shard_map/ppermute | solution.py:846
  323.3 2.7 copy-start
  323.3 2.8 copy-start.2
  332.9 5.1 %copy-start.9 = (f32[1,7040]{1,0:T(1,128)S(1)}, f32[1,7040]{1,0:T(1,128)}, u32[]{:S(2)}) copy-start(f32[1,7040]{1,0:T(1,128)} %get-tuple-element.214) | copy-start | bytes 84484
  332.9 8.7 %copy-start.3 = (f32[1024,768]{1,0:T(8,128)S(1)}, f32[1024,768]{1,0:T(8,128)}, u32[]{:S(2)}) copy-start(f32[1024,768]{1,0:T(8,128)} %get-tuple-element.148) | copy-start | bytes 9437188
  332.9 5.0 %collective-permute-start.34 = (f32[1,7040]{1,0:T(1,128)}, f32[1,7040]{1,0:T(1,128)S(1)}, u32[]{:S(2)}, u32[]{:S(2)}) collective-permute-start(f32[1,7040]{1,0:T(1,128)} %get-tuple-element.214), channel_id=1, source_target_pairs={{0,1},{1,0},{2,3},{3,2},{4,5},{5,4},{6,7},{7,6},{8,9},{9,8},{10,11... | collective-permute-start | bytes 84488 | tf_op jit(solution)/shard_map/ppermute | solution.py:958
  332.9 5.0 %collective-permute-start.35 = (f32[1,7040]{1,0:T(1,128)}, f32[1,7040]{1,0:T(1,128)S(1)}, u32[]{:S(2)}, u32[]{:S(2)}) collective-permute-start(f32[1,7040]{1,0:T(1,128)} %get-tuple-element.214), channel_id=1, source_target_pairs={{0,2},{1,3},{2,0},{3,1},{4,6},{5,7},{6,4},{7,5},{8,10},{9,11},{10,... | collective-permute-start | bytes 84488 | tf_op jit(solution)/shard_map/ppermute | solution.py:958
  333.6 4.3 %collective-permute-start.36 = (f32[1,7040]{1,0:T(1,128)}, f32[1,7040]{1,0:T(1,128)S(1)}, u32[]{:S(2)}, u32[]{:S(2)}) collective-permute-start(f32[1,7040]{1,0:T(1,128)} %get-tuple-element.214), channel_id=1, source_target_pairs={{0,3},{1,2},{2,1},{3,0},{4,7},{5,6},{6,5},{7,4},{8,11},{9,10},{10,... | collective-permute-start | bytes 84488 | tf_op jit(solution)/shard_map/ppermute | solution.py:958
  338.0 5.8 %collective-permute-start.37 = (f32[1,7040]{1,0:T(1,128)S(1)}, f32[1,7040]{1,0:T(1,128)S(1)}, u32[]{:S(2)}, u32[]{:S(2)}) collective-permute-start(f32[1,7040]{1,0:T(1,128)S(1)} %add_add_fusion.1), channel_id=1, source_target_pairs={{0,4},{4,0},{8,12},{12,8},{16,20},{20,16},{24,28},{28,24},{1,5},{5... | collective-permute-start | bytes 84488 | tf_op jit(solution)/shard_map/ppermute | solution.py:958
  339.2 4.6 %collective-permute-start.38 = (f32[1,7040]{1,0:T(1,128)S(1)}, f32[1,7040]{1,0:T(1,128)S(1)}, u32[]{:S(2)}, u32[]{:S(2)}) collective-permute-start(f32[1,7040]{1,0:T(1,128)S(1)} %add_add_fusion.1), channel_id=1, source_target_pairs={{0,8},{4,12},{8,0},{12,4},{16,24},{20,28},{24,16},{28,20},{1,9},{5... | collective-permute-start | bytes 84488 | tf_op jit(solution)/shard_map/ppermute | solution.py:958
  341.0 4.8 %collective-permute-start.39 = (f32[1,7040]{1,0:T(1,128)S(1)}, f32[1,7040]{1,0:T(1,128)S(1)}, u32[]{:S(2)}, u32[]{:S(2)}) collective-permute-start(f32[1,7040]{1,0:T(1,128)S(1)} %add_add_fusion.1), channel_id=1, source_target_pairs={{0,12},{4,8},{8,4},{12,0},{16,28},{20,24},{24,20},{28,16},{1,13},{... | collective-permute-start | bytes 84488 | tf_op jit(solution)/shard_map/ppermute | solution.py:958
  345.8 4.8 %collective-permute-start.40 = (f32[1,7040]{1,0:T(1,128)S(1)}, f32[1,7040]{1,0:T(1,128)S(1)}, u32[]{:S(2)}, u32[]{:S(2)}) collective-permute-start(f32[1,7040]{1,0:T(1,128)S(1)} %add_add_fusion), channel_id=1, source_target_pairs={{0,16},{4,20},{8,24},{12,28},{16,0},{20,4},{24,8},{28,12},{1,17},{... | collective-permute-start | bytes 84488 | tf_op jit(solution)/shard_map/ppermute | solution.py:958
  (7 other events, 7.9 us)
Sparse Core Ops, SparseCore 0:
  11.0 114.7 all-gather.1

commit v2 on v1

--- a/solution.py
+++ b/solution.py
@@ -47,7 +47,7 @@
 CUT = 1280
 TOGETHER = 3
 BUFFERS = 4
-BACK_TOGETHER = 2
+BACK_TOGETHER = 3
 VMEM_LIMIT = 60 * 1024 * 1024
 
 
@@ -568,9 +568,9 @@
         cols = lanes_of(chunk, 256)
         total = nn(turned[...], full_grad[0, :, cols])
         if not first:
-            total = total + before[:, cols]
+            total = total + before[:, cols].astype(F32)
         if not last:
-            outs[0][:, cols] = total
+            outs[0][:, cols] = total.astype(BF16)
         elif chunk < CUT // 256:
             outs[0][:, cols] = total.astype(BF16)
         else:
@@ -629,7 +629,7 @@
     if last:
         outs = [((width, CUT), BF16), ((width, 3 * width + LANES - CUT), BF16)]
     else:
-        outs = [((width, 3 * width), F32), ((16, width), F32)]
+        outs = [((width, 3 * width), BF16), ((16, width), F32)]
     return pl.pallas_call(
         functools.partial(pool_back_kernel, first, last),
         grid=(1,),

time: 368 us -> 367 us (level)
  transfers between devices with their start and end apart: 42 -> 42, of which waited for: 21 -> 20; matrix products, arithmetic and copies ran while one was open for 14% -> 14% of each run, Pallas kernels for 24% -> 23%
where the time goes in v2:
time: 367 us; the launch traced here: 361 us
  Pallas kernels  140 us (38%)
  waiting for transfers between devices  95.5 us (26%)
  starting transfers between devices  44.3 us (12%)
  matrix products  24.5 us (7%)
  local copies, waits for them, and re-layouts  22 us (6%)
  other arithmetic  20.2 us (6%)
  between operations  15.1 us (4%)
    ppermute x27, waiting for transfers between devices, swap(): return lax.ppermute(value, axis, [(i, i ^ 1 << bit) for i in range(size)])  83.2 us
    pallas_call x1, Pallas kernels, feed(): pl.pallas_call(feed_kernel, grid=(rows // block,), in_specs=[row_block(wi...  48.2 us
    pallas_call x3, Pallas kernels, per_seq(): pl.pallas_call(body, grid=(seqs,), in_specs=[pl.BlockSpec(memory_space=pl...  32.4 us
    ppermute x27, starting transfers between devices, swap(): return lax.ppermute(value, axis, [(i, i ^ 1 << bit) for i in range(size)])  28.7 us
    pallas_call x2, Pallas kernels, back(): pl.pallas_call(functools.partial(back_kernel, which), grid=(1,), in_specs...  28.3 us
    pallas_call x2, Pallas kernels, pool_back(): pl.pallas_call(functools.partial(pool_back_kernel, first, last), grid=(1,...  17.8 us
    dot_general x3, matrix products, outer(): lax.dot_general(left, right, (((0,), (0,)), ((), ())), preferred_element_...  13.9 us
    pallas_call x4, Pallas kernels, whole_call(): pl.pallas_call(body, out_shape=[jax.ShapeDtypeStruct(shape, dtype) for sh...  12.9 us
  transfers between devices with their start and end apart: 42, of which 20 were waited for; matrix products, arithmetic and copies ran while one was open for 14% of the time, Pallas kernels for 23%

profile of v2, /device:TPU:0, one launch (start us, length us, event | category | flops | bytes accessed | tf_op | source)
XLA Modules:
  0.0 361.1 jit_solution(1071169922594227851)
XLA Ops:
  7.3 2.6 pack.1
  11.7 4.0 %collective-permute-start.2 = (bf16[24,2432]{1,0:T(8,128)(2,1)}, bf16[24,2432]{1,0:T(8,128)(2,1)S(1)}, u32[]{:S(2)}, u32[]{:S(2)}) collective-permute-start(bf16[24,2432]{1,0:T(8,128)(2,1)} %get-tuple-element.277), channel_id=1, source_target_pairs={{0,16},{4,20},{8,24},{12,28},{16,0},{20,4},{24,8},{28,12},{1,17},{... | collective-permute-start | bytes 350216 | tf_op jit(solution)/shard_map/ppermute | solution.py:814
  16.6 1.5 collective-permute-start
  19.4 1.4 broadcast_multiply_fusion
  20.8 1.7 copy.73
  24.9 2.6 collective-permute-start.3
  27.6 10.6 %collective-permute-done.3 = bf16[2,24,2432]{2,1,0:T(8,128)(2,1)S(1)} collective-permute-done((bf16[2,24,2432]{2,1,0:T(8,128)(2,1)S(1)}, bf16[2,24,2432]{2,1,0:T(8,128)(2,1)S(1)}, u32[]{:S(2)}, u32[]{:S(2)}) %collective-permute-start.3) | collective-permute-done | bytes 233504 | tf_op jit(solution)/shard_map/ppermute | solution.py:814
  38.4 1.8 collective-permute-start.7
  40.2 1.6 collective-permute-start.4
  41.8 3.3 collective-permute-done.7
  45.2 1.5 collective-permute-start.8
  46.9 5.5 %collective-permute-done.4 = bf16[2,2,24,1280]{3,2,0,1:T(8,128)(2,1)S(1)} collective-permute-done((bf16[2,2,24,1280]{3,2,0,1:T(8,128)(2,1)S(1)}, bf16[2,2,24,1280]{3,2,0,1:T(8,128)(2,1)S(1)}, u32[]{:S(2)}, u32[]{:S(2)}) %collective-permute-start.4) | collective-permute-done | bytes 245792 | tf_op jit(solution)/shard_map/ppermute | solution.py:814
  52.6 8.2 %collective-permute-done.8 = bf16[2,2,2,24,1152]{4,3,0,1,2:T(8,128)(2,1)S(1)} collective-permute-done((bf16[2,2,2,24,1152]{4,3,0,1,2:T(8,128)(2,1)S(1)}, bf16[2,2,2,24,1152]{4,3,0,1,2:T(8,128)(2,1)S(1)}, u32[]{:S(2)}, u32[]{:S(2)}) %collective-permute-start.8) | collective-permute-done | bytes 442400 | tf_op jit(solution)/shard_map/ppermute | solution.py:814
  61.0 4.6 %collective-permute-done.5 = bf16[2,2,2,24,1280]{4,3,0,1,2:T(8,128)(2,1)S(1)} collective-permute-done((bf16[2,2,2,24,1280]{4,3,0,1,2:T(8,128)(2,1)S(1)}, bf16[2,2,2,24,1280]{4,3,0,1,2:T(8,128)(2,1)S(1)}, u32[]{:S(2)}, u32[]{:S(2)}) %collective-permute-start.5) | collective-permute-done | bytes 491552 | tf_op jit(solution)/shard_map/ppermute | solution.py:814
  68.7 1.5 copy.64
  70.2 10.0 %project.1 = (bf16[2,512,768]{2,1,0:T(8,128)(2,1)}, bf16[2,640,768]{2,1,0:T(8,128)(2,1)}, bf16[2,640,768]{2,1,0:T(8,128)(2,1)}, bf16[2,2,128,768]{3,2,1,0:T(8,12...) custom-call(s32[4]{0:T(128)} %pad_add_fusion.info, ...), custom_call_target="tpu_custom_call" | custom-call | flops 8000000000 | tf_op jit(solution)/shard_map/project/pallas_call | solution.py:241
  81.8 11.5 %near.1 = (f32[2,512,768]{2,1,0:T(8,128)}, f32[2,4,8,256]{3,2,1,0:T(8,128)}) custom-call(s32[4]{0:T(128)} %pad_add_fusion.info, bf16[2,512,768]{2,1,0:T(8,128)(2,1)} %get-tuple-element.138.query, bf16[2,640,768]{2,1,0:T(8,128)(2,1)} %get-tuple-element.142.key, bf16[2,640,768]{2,1,0:T(8,128)(2,1)} %get-tuple-element.143.value), custom_call_target="tpu_custom_call" | custom-call | flops 24000000000 | tf_op jit(solution)/shard_map/near/pallas_call | solution.py:241
  93.3 13.9 %collective-permute-done.10.beside = bf16[2,2,64,768]{3,2,1,0:T(8,128)(2,1)S(1)} collective-permute-done((bf16[2,2,64,768]{3,2,1,0:T(8,128)(2,1)}, bf16[2,2,64,768]{3,2,1,0:T(8,128)(2,1)S(1)}, u32[]{:S(2)}, u32[]{:S(2)}) %collective-permute-start.10) | collective-permute-done | bytes 393248 | tf_op jit(solution)/shard_map/ppermute | solution.py:814
  108.2 10.8 %far.1 = (bf16[2,512,768]{2,1,0:T(8,128)(2,1)}, bf16[2,256,768]{2,1,0:T(8,128)(2,1)}, bf16[2,256,768]{2,1,0:T(8,128)(2,1)}, f32[2,4,8,256]{3,2,1,0:T(8,128)}) custom-call(s32[4]{0:T(128)} %pad_add_fusion.info, bf16[2,512,768]{2,1,0:T(8,128)(2,1)} %get-tuple-element.138.query, bf16[2,2,128,768]{3,2,1,0:T(8,128)(2,1)} %get-tuple-element.139.pool, ...), custom_call_target="tpu_custom_call" | custom-call | flops 9600000000 | tf_op jit(solution)/shard_map/far/pallas_call | solution.py:241
  119.0 6.8 %all-gather.2.cloned.1.call-done.packed = bf16[768,6912]{1,0:T(8,128)(2,1)} async-done(((bf16[24,6912]{1,0:T(8,128)(2,1)}), bf16[768,6912]{1,0:T(8,128)(2,1)}) %all-gather.2.cloned.1.call-update) | async-done | bytes 10616848 | tf_op jit(solution)/shard_map/all_gather | solution.py:1008
  125.7 48.2 %feed.1 = (bf16[1024,768]{1,0:T(8,128)(2,1)}, f32[1024,768]{1,0:T(8,128)}, bf16[1024,768]{1,0:T(8,128)(2,1)}, bf16[1024,3072]{1,0:T(8,128)(2,1)}, bf16[1024,3072...) custom-call(bf16[1024,768]{1,0:T(8,128)(2,1)} %bitcast.182, ...), custom_call_target="tpu_custom_call" | custom-call | flops 38400000000 | tf_op jit(solution)/shard_map/feed/pallas_call | solution.py:415
  174.0 3.0 convolution_convert_fusion.2
  178.4 5.5 %convolution_convert_fusion.1 = bf16[3072,768]{1,0:T(8,128)(2,1)S(1)} fusion(bf16[1024,3072]{1,0:T(8,128)(2,1)S(1)} %copy-done.25, bf16[1024,768]{1,0:T(8,128)(2,1)S(1)} %copy-done.26), kind=kOutput, calls=%fused_computation.1 | convolution fusion | flops 4834197504 | bytes 12582912 | tf_op jit(solution)/shard_map/dot_general | solution.py:63
  184.3 1.6 copy.91
  188.3 5.4 %convolution_convert_fusion = bf16[768,3072]{1,0:T(8,128)(2,1)S(1)} fusion(bf16[1024,768]{1,0:T(8,128)(2,1)S(1)} %copy-done.24, bf16[1024,3072]{1,0:T(8,128)(2,1)S(1)} %bitcast.243), kind=kOutput, calls=%fused_computation | convolution fusion | flops 4834197504 | bytes 12582912 | tf_op jit(solution)/shard_map/dot_general | solution.py:63
  193.7 1.8 constant_dynamic-slice_fusion.1
  195.5 1.7 copy.90
  197.4 2.3 fusion.1
  200.0 2.0 collective-permute-done.14
  202.0 2.6 fusion
  207.1 1.4 dynamic-slice_bitcast_fusion
  208.5 1.5 collective-permute-start.17
  210.0 14.1 %back.2 = (bf16[1,512,768]{2,1,0:T(8,128)(2,1)}, f32[1,2,640,768]{3,2,1,0:T(8,128)}, f32[1,2,256,768]{3,2,1,0:T(8,128)}, bf16[1,2,144,768]{3,2,1,0:T(8,128)(2,1)}, bf16[1,2,144,768]{3,2,1,0:T(8,128)(2,1)}) custom-call(s32[4]{0:T(128)} %pad_add_fusion.info, bf16[2,512,768]{2,1,0:T(8,128)(2,1)} %get-tuple-element.138.query, ...), custom_call_target="tpu_custom_call" | custom-call | flops 24000000000 | tf_op jit(solution)/shard_map/back/pallas_call | solution.py:535
  224.8 14.2 %back.3 = (bf16[1,512,768]{2,1,0:T(8,128)(2,1)}, f32[1,2,640,768]{3,2,1,0:T(8,128)}, f32[1,2,256,768]{3,2,1,0:T(8,128)}, bf16[1,2,144,768]{3,2,1,0:T(8,128)(2,1)}, bf16[1,2,144,768]{3,2,1,0:T(8,128)(2,1)}) custom-call(s32[4]{0:T(128)} %pad_add_fusion.info, bf16[2,512,768]{2,1,0:T(8,128)(2,1)} %get-tuple-element.138.query, ...), custom_call_target="tpu_custom_call" | custom-call | flops 8000000 | tf_op jit(solution)/shard_map/back/pallas_call | solution.py:535
  239.0 4.5 %collective-permute-done.15.beside = bf16[1,2,144,768]{3,2,1,0:T(8,128)(2,1)S(1)} collective-permute-done((bf16[1,2,144,768]{3,2,1,0:T(8,128)(2,1)}, bf16[1,2,144,768]{3,2,1,0:T(8,128)(2,1)S(1)}, u32[]{:S(2)}, u32[]{:S(2)}) %collective-permute-start.15) | collective-permute-done | bytes 442400 | tf_op jit(solution)/shard_map/ppermute | solution.py:814
  243.5 2.4 collective-permute-start.19
  245.9 1.6 collective-permute-start.20
  247.5 1.7 add_convert_fusion.1
  249.2 1.7 add_convert_fusion
  252.0 2.0 collective-permute-start.21
  254.0 8.4 %pool_back.2 = (bf16[1,512,2304]{2,1,0:T(8,128)(2,1)}, bf16[768,2304]{1,0:T(8,128)(2,1)}, f32[16,768]{1,0:T(8,128)}) custom-call(s32[4]{0:T(128)} %pad_add_fusion.info, bf16[1,512,768]{2,1,0:T(8,128)(2,1)} %get-tuple-element.162.query_grad, f32[1,2,640,768]{3,2,1,0:T(8,128)} %get-tuple-element.166.near_grad, f32[1,2,256,768]{3,2,1,0:T(8,128)} %get-tuple-element.167.far_grad, ...), custom_call_target="tpu_custom_call" | custom-call | flops 24000000000 | tf_op jit(solution)/shard_map/pool_back/pallas_call | solution.py:633
  262.4 1.7 collective-permute-done.19.beside
  265.0 9.1 %collective-permute-done.21 = bf16[5,2,2,24,768]{4,3,2,1,0:T(8,128)(2,1)S(1)} collective-permute-done((bf16[5,2,2,24,768]{4,3,2,1,0:T(8,128)(2,1)S(1)}, bf16[5,2,2,24,768]{4,3,2,1,0:T(8,128)(2,1)S(1)}, u32[]{:S(2)}, u32[]{:S(2)}) %collective-permute-start.21) | collective-permute-done | bytes 737312 | tf_op jit(solution)/shard_map/ppermute | solution.py:814
  274.7 9.4 %pool_back.3 = (bf16[1,512,2304]{2,1,0:T(8,128)(2,1)}, bf16[768,1280]{1,0:T(8,128)(2,1)}, bf16[768,1152]{1,0:T(8,128)(2,1)}) custom-call(s32[4]{0:T(128)} %pad_add_fusion.info, bf16[1,512,768]{2,1,0:T(8,128)(2,1)} %get-tuple-element.164.query_grad, f32[1,2,640,768]{3,2,1,0:T(8,128)} %get-tuple-element.179.near_grad, ...), custom_call_target="tpu_custom_call" | custom-call | flops 8000000 | tf_op jit(solution)/shard_map/pool_back/pallas_call | solution.py:633
  284.1 5.1 %collective-permute-done.23 = bf16[2,24,6912]{2,1,0:T(8,128)(2,1)S(1)} collective-permute-done((bf16[2,24,6912]{2,1,0:T(8,128)(2,1)S(1)}, bf16[2,24,6912]{2,1,0:T(8,128)(2,1)S(1)}, u32[]{:S(2)}, u32[]{:S(2)}) %collective-permute-start.23) | collective-permute-done | bytes 663584 | tf_op jit(solution)/shard_map/ppermute | solution.py:814
  291.4 2.5 collective-permute-start.30
  294.3 1.3 collective-permute-start.28
  296.3 9.9 %collective-permute-done.28 = bf16[2,2,2,24,1152]{4,3,2,1,0:T(8,128)(2,1)S(1)} collective-permute-done((bf16[2,2,2,24,1152]{4,3,2,1,0:T(8,128)(2,1)S(1)}, bf16[2,2,2,24,1152]{4,3,2,1,0:T(8,128)(2,1)S(1)}, u32[]{:S(2)}, u32[]{:S(2)}) %collective-permute-start.28) | collective-permute-done | bytes 442400 | tf_op jit(solution)/shard_map/ppermute | solution.py:814
  306.7 3.4 collective-permute-done.25
  311.7 4.9 %late_stats.1 = (f32[1,7040]{1,0:T(1,128)}, f32[24,3072]{1,0:T(8,128)}, f32[96,768]{1,0:T(8,128)}) custom-call(f32[24,6912]{1,0:T(8,128)} %convert_add_fusion.8.late, f32[1,24]{1,0:T(1,128)} %bitcast.219, f32[1,24]{1,0:T(1,128)} %bitcast.221, f32[1,24]{1,0:T(1,128)} %bitcast.223, f32[1,96]{1,0:T(1,128)} %bitcast.225), custom_call_target="tpu_custom_call" | custom-call | flops 2400000000 | tf_op jit(solution)/shard_map/late_stats/pallas_call | solution.py:800
  317.8 2.0 collective-permute-start.32
  319.7 2.4 collective-permute-start.33
  322.1 2.7 fusion.15
  325.0 2.5 add_bitcast_fusion.1
  327.5 1.6 collective-permute-done.32.two
  329.7 1.9 stats.1
  333.5 3.2 fusion.13
  336.8 1.7 collective-permute-start.37
  338.4 1.8 collective-permute-start.38
  340.3 2.3 add_bitcast_fusion
  342.6 2.4 collective-permute-done.39
  346.3 2.0 pad_maximum_fusion
  348.3 1.6 collective-permute-done.40
  350.5 3.5 update.1
  (176 shorter events, 34.5 us)
Async XLA Ops:
  7.2 3.8 %copy-start.11 = (f32[24,14]{0,1:T(8,128)S(1)}, f32[24,14]{0,1:T(8,128)}, u32[]{:S(2)}) copy-start(f32[24,14]{0,1:T(8,128)} %param.26) | copy-start | bytes 4036
  7.2 8.6 %copy-start.4 = (bf16[2,512,768]{2,1,0:T(8,128)(2,1)S(1)}, bf16[2,512,768]{2,1,0:T(8,128)(2,1)}, u32[]{:S(2)}) copy-start(bf16[2,512,768]{2,1,0:T(8,128)(2,1)} %own.1) | copy-start | bytes 4718596
  7.2 118.5 %all-gather.2.cloned.1.call-start = ((), (), s32[]{:S(2)}) async-start(), calls=%async_computation | async-start | bytes 10948608 | tf_op jit(solution)/shard_map/all_gather | solution.py:1008
  9.9 9.5 %copy-start.14 = (s32[2,512]{1,0:T(2,128)S(1)}, s32[2,512]{1,0:T(2,128)}, u32[]{:S(2)}) copy-start(s32[2,512]{1,0:T(2,128)} %param.20) | copy-start | bytes 12292
  9.9 9.5 %copy-start.8 = (bf16[2,512,768]{2,1,0:T(8,128)(2,1)S(1)}, bf16[2,512,768]{2,1,0:T(8,128)(2,1)}, u32[]{:S(2)}) copy-start(bf16[2,512,768]{2,1,0:T(8,128)(2,1)} %param.21) | copy-start | bytes 4718596
  11.7 13.1 %collective-permute-start.2 = (bf16[24,2432]{1,0:T(8,128)(2,1)}, bf16[24,2432]{1,0:T(8,128)(2,1)S(1)}, u32[]{:S(2)}, u32[]{:S(2)}) collective-permute-start(bf16[24,2432]{1,0:T(8,128)(2,1)} %get-tuple-element.277), channel_id=1, source_target_pairs={{0,16},{4,20},{8,24},{12,28},{16,0},{20,4},{24,8},{28,12},{1,17},{... | collective-permute-start | bytes 350216 | tf_op jit(solution)/shard_map/ppermute | solution.py:814
  16.6 53.7 %collective-permute-start = (bf16[2,64,768]{2,1,0:T(8,128)(2,1)}, bf16[2,64,768]{2,1,0:T(8,128)(2,1)}, u32[]{:S(2)}, u32[]{:S(2)}) collective-permute-start(bf16[2,64,768]{2,1,0:T(8,128)(2,1)} %get-tuple-element.256), channel_id=1, source_target_pairs={{0,4},{4,0},{8,12},{12,8},{16,20},{20,16},{24,28},{28,24},{1,5},{5... | collective-permute-start | bytes 589832 | tf_op jit(solution)/shard_map/ppermute | solution.py:814
  18.0 52.2 %collective-permute-start.1 = (bf16[2,64,768]{2,1,0:T(8,128)(2,1)}, bf16[2,64,768]{2,1,0:T(8,128)(2,1)}, u32[]{:S(2)}, u32[]{:S(2)}) collective-permute-start(bf16[2,64,768]{2,1,0:T(8,128)(2,1)} %get-tuple-element.255), channel_id=1, source_target_pairs={{4,8},{8,4},{12,16},{16,12},{20,24},{24,20},{5,9},{9,5},{13,17},{1... | collective-permute-start | bytes 589832 | tf_op jit(solution)/shard_map/ppermute | solution.py:931
  20.8 2.3 copy-start.12
  20.8 2.9 copy-start.13
  20.8 3.5 copy-start.15
  24.9 13.3 %collective-permute-start.3 = (bf16[2,24,2432]{2,1,0:T(8,128)(2,1)S(1)}, bf16[2,24,2432]{2,1,0:T(8,128)(2,1)S(1)}, u32[]{:S(2)}, u32[]{:S(2)}) collective-permute-start(bf16[2,24,2432]{2,1,0:T(8,128)(2,1)S(1)} %maximum_select_fusion.12), channel_id=1, source_target_pairs={{0,8},{4,12},{8,0},{12,4},{16,24},{20,28},{24,16},{28,20},{1,9},{5... | collective-permute-start | bytes 700424 | tf_op jit(solution)/shard_map/ppermute | solution.py:814
  38.4 6.7 %collective-permute-start.7 = (bf16[2,2,24,1152]{3,2,0,1:T(8,128)(2,1)S(1)}, bf16[2,2,24,1152]{3,2,0,1:T(8,128)(2,1)S(1)}, u32[]{:S(2)}, u32[]{:S(2)}) collective-permute-start(bf16[2,2,24,1152]{3,2,0,1:T(8,128)(2,1)S(1)} %get-tuple-element.271), channel_id=1, source_target_pairs={{0,4},{4,0},{8,12},{12,8},{16,20},{20,16},{24,28},{28,24},{1,5},{5... | collective-permute-start | bytes 663560 | tf_op jit(solution)/shard_map/ppermute | solution.py:814
  40.2 12.1 %collective-permute-start.4 = (bf16[2,2,24,1280]{3,2,0,1:T(8,128)(2,1)S(1)}, bf16[2,2,24,1280]{3,2,0,1:T(8,128)(2,1)S(1)}, u32[]{:S(2)}, u32[]{:S(2)}) collective-permute-start(bf16[2,2,24,1280]{3,2,0,1:T(8,128)(2,1)S(1)} %get-tuple-element.274), channel_id=1, source_target_pairs={{0,2},{1,3},{2,0},{3,1},{4,6},{5,7},{6,4},{7,5},{8,10},{9,11},{10,... | collective-permute-start | bytes 737288 | tf_op jit(solution)/shard_map/ppermute | solution.py:814
  45.2 15.6 %collective-permute-start.8 = (bf16[2,2,2,24,1152]{4,3,0,1,2:T(8,128)(2,1)S(1)}, bf16[2,2,2,24,1152]{4,3,0,1,2:T(8,128)(2,1)S(1)}, u32[]{:S(2)}, u32[]{:S(2)}) collective-permute-start(bf16[2,2,2,24,1152]{4,3,0,1,2:T(8,128)(2,1)S(1)} %maximum_select_fusion.10), channel_id=1, source_target_pairs={{0,2},{1,3},{2,0},{3,1},{4,6},{5,7},{6,4},{7,5},{8,10},{9,11},{10,... | collective-permute-start | bytes 1327112 | tf_op jit(solution)/shard_map/ppermute | solution.py:814
  52.4 13.1 %collective-permute-start.5 = (bf16[2,2,2,24,1280]{4,3,0,1,2:T(8,128)(2,1)S(1)}, bf16[2,2,2,24,1280]{4,3,0,1,2:T(8,128)(2,1)S(1)}, u32[]{:S(2)}, u32[]{:S(2)}) collective-permute-start(bf16[2,2,2,24,1280]{4,3,0,1,2:T(8,128)(2,1)S(1)} %maximum_select_fusion.7), channel_id=1, source_target_pairs={{0,4},{4,0},{8,12},{12,8},{16,20},{20,16},{24,28},{28,24},{1,5},{5... | collective-permute-start | bytes 1474568 | tf_op jit(solution)/shard_map/ppermute | solution.py:814
  60.9 5.3 %collective-permute-start.9 = (bf16[2,2,2,2,24,1152]{5,4,0,1,2,3:T(8,128)(2,1)S(1)}, bf16[2,2,2,2,24,1152]{5,4,0,1,2,3:T(8,128)(2,1)S(1)}, u32[]{:S(2)}, u32[]{:S(2)}) collective-permute-start(bf16[2,2,2,2,24,1152]{5,4,0,1,2,3:T(8,128)(2,1)S(1)} %maximum_select_fusion.5), channel_id=1, source_target_pairs={{0,1},{1,0},{2,3},{3,2},{4,5},{5,4},{6,7},{7,6},{8,9},{9,8},{10,11... | collective-permute-start | bytes 2654216 | tf_op jit(solution)/shard_map/ppermute | solution.py:814
  65.7 2.6 collective-permute-start.6
  80.2 27.0 %collective-permute-start.10 = (bf16[2,2,64,768]{3,2,1,0:T(8,128)(2,1)}, bf16[2,2,64,768]{3,2,1,0:T(8,128)(2,1)S(1)}, u32[]{:S(2)}, u32[]{:S(2)}) collective-permute-start(bf16[2,2,64,768]{3,2,1,0:T(8,128)(2,1)} %get-tuple-element.140), channel_id=1, source_target_pairs={{0,4},{4,0},{8,12},{12,8},{16,20},{20,16},{24,28},{28,24},{1,5},{5... | collective-permute-start | bytes 1179656 | tf_op jit(solution)/shard_map/ppermute | solution.py:814
  80.9 26.4 %collective-permute-start.11 = (bf16[2,2,64,768]{3,2,1,0:T(8,128)(2,1)}, bf16[2,2,64,768]{3,2,1,0:T(8,128)(2,1)S(1)}, u32[]{:S(2)}, u32[]{:S(2)}) collective-permute-start(bf16[2,2,64,768]{3,2,1,0:T(8,128)(2,1)} %get-tuple-element.141), channel_id=1, source_target_pairs={{4,8},{8,4},{12,16},{16,12},{20,24},{24,20},{5,9},{9,5},{13,17},{1... | collective-permute-start | bytes 1179656 | tf_op jit(solution)/shard_map/ppermute | solution.py:931
  125.7 48.2 %copy-start.23 = (bf16[2,512,768]{2,1,0:T(8,128)(2,1)S(1)}, bf16[2,512,768]{2,1,0:T(8,128)(2,1)}, u32[]{:S(2)}) copy-start(bf16[2,512,768]{2,1,0:T(8,128)(2,1)} %get-tuple-element.145) | copy-start | bytes 4718596
  173.9 3.5 copy-start.25
  177.1 9.1 %collective-permute-start.13 = (bf16[1,2,2,2,2,24,768]{6,5,3,2,1,0,4:T(8,128)(2,1)S(1)}, bf16[1,2,2,2,2,24,768]{6,5,3,2,1,0,4:T(8,128)(2,1)S(1)}, u32[]{:S(2)}, u32[]{:S(2)}) collective-permute-start(bf16[1,2,2,2,2,24,768]{6,5,3,2,1,0,4:T(8,128)(2,1)S(1)} %bitcast.208), channel_id=1, source_target_pairs={{0,1},{1,0},{2,3},{3,2},{4,5},{5,4},{6,7},{7,6},{8,9},{9,8},{10,11... | collective-permute-start | bytes 1769480 | tf_op jit(solution)/shard_map/ppermute | solution.py:814
  183.9 3.0 slice-start
  183.9 3.7 %slice-start.1 = ((s8[6291456]{0:T(1024)(128)(4,1)}), s8[2097152]{0:T(1024)(128)(4,1)S(1)}, s32[]{:S(2)}) async-start(s8[6291456]{0:T(1024)(128)(4,1)} %bitcast.242), calls=%async_computation.2 | async-start | bytes 4194304
  185.9 2.4 copy-start.24
  185.9 11.5 %collective-permute-start.12 = (bf16[4,2,2,2,2,24,768]{6,5,3,2,1,0,4:T(8,128)(2,1)}, bf16[4,2,2,2,2,24,768]{6,5,3,2,1,0,4:T(8,128)(2,1)}, u32[]{:S(2)}, u32[]{:S(2)}) collective-permute-start(bf16[4,2,2,2,2,24,768]{6,5,3,2,1,0,4:T(8,128)(2,1)} %bitcast.173), channel_id=1, source_target_pairs={{0,1},{1,0},{2,3},{3,2},{4,5},{5,4},{6,7},{7,6},{8,9},{9,8},{10,11... | collective-permute-start | bytes 7077896 | tf_op jit(solution)/shard_map/ppermute | solution.py:814
  197.1 4.9 %collective-permute-start.14 = (bf16[2,2,2,2,24,3072]{5,4,3,2,0,1:T(8,128)(2,1)}, bf16[2,2,2,2,24,3072]{5,4,3,2,0,1:T(8,128)(2,1)}, u32[]{:S(2)}, u32[]{:S(2)}) collective-permute-start(bf16[2,2,2,2,24,3072]{5,4,3,2,0,1:T(8,128)(2,1)} %bitcast.172), channel_id=1, source_target_pairs={{0,1},{1,0},{2,3},{3,2},{4,5},{5,4},{6,7},{7,6},{8,9},{9,8},{10,11... | collective-permute-start | bytes 7077896 | tf_op jit(solution)/shard_map/ppermute | solution.py:814
  199.7 2.3 copy-start.1
  205.9 41.6 %collective-permute-start.18 = (bf16[2,2,2,24,3072]{4,3,2,1,0:T(8,128)(2,1)}, bf16[2,2,2,24,3072]{4,3,2,1,0:T(8,128)(2,1)}, u32[]{:S(2)}, u32[]{:S(2)}) collective-permute-start(bf16[2,2,2,24,3072]{4,3,2,1,0:T(8,128)(2,1)} %get-tuple-element.253), channel_id=1, source_target_pairs={{0,8},{4,12},{8,0},{12,4},{16,24},{20,28},{24,16},{28,20},{1,9},{5... | collective-permute-start | bytes 3538952 | tf_op jit(solution)/shard_map/ppermute | solution.py:814
  208.5 40.7 %collective-permute-start.17 = (bf16[5,2,2,2,24,768]{5,4,3,2,1,0:T(8,128)(2,1)}, bf16[5,2,2,2,24,768]{5,4,3,2,1,0:T(8,128)(2,1)}, u32[]{:S(2)}, u32[]{:S(2)}) collective-permute-start(bf16[5,2,2,2,24,768]{5,4,3,2,1,0:T(8,128)(2,1)} %get-tuple-element.251), channel_id=1, source_target_pairs={{0,2},{1,3},{2,0},{3,1},{4,6},{5,7},{6,4},{7,5},{8,10},{9,11},{10,... | collective-permute-start | bytes 4423688 | tf_op jit(solution)/shard_map/ppermute | solution.py:814
  224.1 19.4 %collective-permute-start.15 = (bf16[1,2,144,768]{3,2,1,0:T(8,128)(2,1)}, bf16[1,2,144,768]{3,2,1,0:T(8,128)(2,1)S(1)}, u32[]{:S(2)}, u32[]{:S(2)}) collective-permute-start(bf16[1,2,144,768]{3,2,1,0:T(8,128)(2,1)} %get-tuple-element.168), channel_id=1, source_target_pairs={{0,4},{4,0},{8,12},{12,8},{16,20},{20,16},{24,28},{28,24},{1,5},{5... | collective-permute-start | bytes 1327112 | tf_op jit(solution)/shard_map/ppermute | solution.py:814
  224.1 19.4 %collective-permute-start.16 = (bf16[1,2,144,768]{3,2,1,0:T(8,128)(2,1)}, bf16[1,2,144,768]{3,2,1,0:T(8,128)(2,1)S(1)}, u32[]{:S(2)}, u32[]{:S(2)}) collective-permute-start(bf16[1,2,144,768]{3,2,1,0:T(8,128)(2,1)} %get-tuple-element.169), channel_id=1, source_target_pairs={{4,8},{8,4},{12,16},{16,12},{20,24},{24,20},{5,9},{9,5},{13,17},{1... | collective-permute-start | bytes 1327112 | tf_op jit(solution)/shard_map/ppermute | solution.py:931
  243.5 5.7 %copy-start.16 = (bf16[1,2,144,768]{3,2,1,0:T(8,128)(2,1)}, bf16[1,2,144,768]{3,2,1,0:T(8,128)(2,1)S(1)}, u32[]{:S(2)}) copy-start(bf16[1,2,144,768]{3,2,1,0:T(8,128)(2,1)S(1)} %collective-permute-done.15.beside) | copy-start | bytes 1327108
  243.5 5.7 %copy-start.17 = (bf16[1,2,144,768]{3,2,1,0:T(8,128)(2,1)}, bf16[1,2,144,768]{3,2,1,0:T(8,128)(2,1)S(1)}, u32[]{:S(2)}) copy-start(bf16[1,2,144,768]{3,2,1,0:T(8,128)(2,1)S(1)} %collective-permute-done.16.across) | copy-start | bytes 1327108
  243.5 20.5 %collective-permute-start.19 = (bf16[1,2,144,768]{3,2,1,0:T(8,128)(2,1)}, bf16[1,2,144,768]{3,2,1,0:T(8,128)(2,1)}, u32[]{:S(2)}, u32[]{:S(2)}) collective-permute-start(bf16[1,2,144,768]{3,2,1,0:T(8,128)(2,1)} %get-tuple-element.183), channel_id=1, source_target_pairs={{0,4},{4,0},{8,12},{12,8},{16,20},{20,16},{24,28},{28,24},{1,5},{5... | collective-permute-start | bytes 1327112 | tf_op jit(solution)/shard_map/ppermute | solution.py:814
  245.9 18.1 %collective-permute-start.20 = (bf16[1,2,144,768]{3,2,1,0:T(8,128)(2,1)}, bf16[1,2,144,768]{3,2,1,0:T(8,128)(2,1)}, u32[]{:S(2)}, u32[]{:S(2)}) collective-permute-start(bf16[1,2,144,768]{3,2,1,0:T(8,128)(2,1)} %get-tuple-element.184), channel_id=1, source_target_pairs={{4,8},{8,4},{12,16},{16,12},{20,24},{24,20},{5,9},{9,5},{13,17},{1... | collective-permute-start | bytes 1327112 | tf_op jit(solution)/shard_map/ppermute | solution.py:931
  251.1 13.8 %collective-permute-start.22 = (bf16[2,2,24,3072]{3,2,1,0:T(8,128)(2,1)S(1)}, bf16[2,2,24,3072]{3,2,1,0:T(8,128)(2,1)S(1)}, u32[]{:S(2)}, u32[]{:S(2)}) collective-permute-start(bf16[2,2,24,3072]{3,2,1,0:T(8,128)(2,1)S(1)} %get-tuple-element.259), channel_id=1, source_target_pairs={{0,2},{1,3},{2,0},{3,1},{4,6},{5,7},{6,4},{7,5},{8,10},{9,11},{10,... | collective-permute-start | bytes 1769480 | tf_op jit(solution)/shard_map/ppermute | solution.py:814
  252.0 22.2 %collective-permute-start.21 = (bf16[5,2,2,24,768]{4,3,2,1,0:T(8,128)(2,1)S(1)}, bf16[5,2,2,24,768]{4,3,2,1,0:T(8,128)(2,1)S(1)}, u32[]{:S(2)}, u32[]{:S(2)}) collective-permute-start(bf16[5,2,2,24,768]{4,3,2,1,0:T(8,128)(2,1)S(1)} %get-tuple-element.257), channel_id=1, source_target_pairs={{0,8},{4,12},{8,0},{12,4},{16,24},{20,28},{24,16},{28,20},{1,9},{5... | collective-permute-start | bytes 2211848 | tf_op jit(solution)/shard_map/ppermute | solution.py:814
  274.5 14.7 %collective-permute-start.23 = (bf16[2,24,6912]{2,1,0:T(8,128)(2,1)S(1)}, bf16[2,24,6912]{2,1,0:T(8,128)(2,1)S(1)}, u32[]{:S(2)}, u32[]{:S(2)}) collective-permute-start(bf16[2,24,6912]{2,1,0:T(8,128)(2,1)S(1)} %dynamic-slice_bitcast_fusion.8), channel_id=1, source_target_pairs={{0,4},{4,0},{8,12},{12,8},{16,20},{20,16},{24,28},{28,24},{1,5},{5... | collective-permute-start | bytes 1990664 | tf_op jit(solution)/shard_map/ppermute | solution.py:814
  284.1 6.6 %copy-start.6 = (bf16[768,1280]{1,0:T(8,128)(2,1)S(1)}, bf16[768,1280]{1,0:T(8,128)(2,1)}, u32[]{:S(2)}) copy-start(bf16[768,1280]{1,0:T(8,128)(2,1)} %get-tuple-element.200) | copy-start | bytes 5898244
  290.6 3.4 copy-start.7
  290.6 3.3 collective-permute-start.27
  290.8 4.8 %collective-permute-start.24 = (bf16[2,2,2,2,24,1280]{5,4,3,2,1,0:T(8,128)(2,1)S(1)}, bf16[2,2,2,2,24,1280]{5,4,3,2,1,0:T(8,128)(2,1)S(1)}, u32[]{:S(2)}, u32[]{:S(2)}) collective-permute-start(bf16[2,2,2,2,24,1280]{5,4,3,2,1,0:T(8,128)(2,1)S(1)} %dynamic-slice_bitcast_fusion.4), channel_id=1, source_target_pairs={{0,1},{1,0},{2,3},{3,2},{4,5},{5,4},{6,7},{7,6},{8,9},{9,8},{10,11... | collective-permute-start | bytes 2949128 | tf_op jit(solution)/shard_map/ppermute | solution.py:814
  291.4 18.8 %collective-permute-start.30 = (bf16[24,6912]{1,0:T(8,128)(2,1)S(1)}, bf16[24,6912]{1,0:T(8,128)(2,1)S(1)}, u32[]{:S(2)}, u32[]{:S(2)}) collective-permute-start(bf16[24,6912]{1,0:T(8,128)(2,1)S(1)} %get-tuple-element.263), channel_id=1, source_target_pairs={{0,16},{4,20},{8,24},{12,28},{16,0},{20,4},{24,8},{28,12},{1,17},{... | collective-permute-start | bytes 995336 | tf_op jit(solution)/shard_map/ppermute | solution.py:814
  294.3 11.9 %collective-permute-start.28 = (bf16[2,2,2,24,1152]{4,3,2,1,0:T(8,128)(2,1)S(1)}, bf16[2,2,2,24,1152]{4,3,2,1,0:T(8,128)(2,1)S(1)}, u32[]{:S(2)}, u32[]{:S(2)}) collective-permute-start(bf16[2,2,2,24,1152]{4,3,2,1,0:T(8,128)(2,1)S(1)} %dynamic-slice_bitcast_fusion.12), channel_id=1, source_target_pairs={{0,2},{1,3},{2,0},{3,1},{4,6},{5,7},{6,4},{7,5},{8,10},{9,11},{10,... | collective-permute-start | bytes 1327112 | tf_op jit(solution)/shard_map/ppermute | solution.py:814
  295.9 14.1 %collective-permute-start.25 = (bf16[2,2,2,24,1280]{4,3,2,1,0:T(8,128)(2,1)S(1)}, bf16[2,2,2,24,1280]{4,3,2,1,0:T(8,128)(2,1)S(1)}, u32[]{:S(2)}, u32[]{:S(2)}) collective-permute-start(bf16[2,2,2,24,1280]{4,3,2,1,0:T(8,128)(2,1)S(1)} %dynamic-slice_bitcast_fusion.11), channel_id=1, source_target_pairs={{0,4},{4,0},{8,12},{12,8},{16,20},{20,16},{24,28},{28,24},{1,5},{5... | collective-permute-start | bytes 1474568 | tf_op jit(solution)/shard_map/ppermute | solution.py:814
  306.3 10.3 %collective-permute-start.29 = (bf16[2,2,24,1152]{3,2,1,0:T(8,128)(2,1)S(1)}, bf16[2,2,24,1152]{3,2,1,0:T(8,128)(2,1)S(1)}, u32[]{:S(2)}, u32[]{:S(2)}) collective-permute-start(bf16[2,2,24,1152]{3,2,1,0:T(8,128)(2,1)S(1)} %dynamic-slice_bitcast_fusion.16), channel_id=1, source_target_pairs={{0,4},{4,0},{8,12},{12,8},{16,20},{20,16},{24,28},{28,24},{1,5},{5... | collective-permute-start | bytes 663560 | tf_op jit(solution)/shard_map/ppermute | solution.py:814
  310.2 6.7 %collective-permute-start.26 = (bf16[2,2,24,1280]{3,2,1,0:T(8,128)(2,1)S(1)}, bf16[2,2,24,1280]{3,2,1,0:T(8,128)(2,1)S(1)}, u32[]{:S(2)}, u32[]{:S(2)}) collective-permute-start(bf16[2,2,24,1280]{3,2,1,0:T(8,128)(2,1)S(1)} %dynamic-slice_bitcast_fusion.15), channel_id=1, source_target_pairs={{0,2},{1,3},{2,0},{3,1},{4,6},{5,7},{6,4},{7,5},{8,10},{9,11},{10,... | collective-permute-start | bytes 737288 | tf_op jit(solution)/shard_map/ppermute | solution.py:814
  316.6 5.6 %copy-start.5 = (bf16[2,2,2,2,2,24,1280]{6,5,4,3,2,1,0:T(8,128)(2,1)S(1)}, bf16[2,2,2,2,2,24,1280]{6,5,4,3,2,1,0:T(8,128)(2,1)}, u32[]{:S(2)}) copy-start(bf16[2,2,2,2,2,24,1280]{6,5,4,3,2,1,0:T(8,128)(2,1)} %copy.64) | copy-start | bytes 5898244
  317.7 9.7 %collective-permute-start.31 = (bf16[24,2432]{1,0:T(8,128)(2,1)S(1)}, bf16[24,2432]{1,0:T(8,128)(2,1)S(1)}, u32[]{:S(2)}, u32[]{:S(2)}) collective-permute-start(bf16[24,2432]{1,0:T(8,128)(2,1)S(1)} %get-tuple-element.267), channel_id=1, source_target_pairs={{0,8},{4,12},{8,0},{12,4},{16,24},{20,28},{24,16},{28,20},{1,9},{5... | collective-permute-start | bytes 350216 | tf_op jit(solution)/shard_map/ppermute | solution.py:846
  317.8 11.3 %collective-permute-start.32 = (bf16[24,2432]{1,0:T(8,128)(2,1)S(1)}, bf16[24,2432]{1,0:T(8,128)(2,1)S(1)}, u32[]{:S(2)}, u32[]{:S(2)}) collective-permute-start(bf16[24,2432]{1,0:T(8,128)(2,1)S(1)} %get-tuple-element.266), channel_id=1, source_target_pairs={{0,16},{4,20},{8,24},{12,28},{16,0},{20,4},{24,8},{28,12},{1,17},{... | collective-permute-start | bytes 350216 | tf_op jit(solution)/shard_map/ppermute | solution.py:846
  319.7 9.3 %collective-permute-start.33 = (bf16[24,2432]{1,0:T(8,128)(2,1)S(1)}, bf16[24,2432]{1,0:T(8,128)(2,1)S(1)}, u32[]{:S(2)}, u32[]{:S(2)}) collective-permute-start(bf16[24,2432]{1,0:T(8,128)(2,1)S(1)} %get-tuple-element.265), channel_id=1, source_target_pairs={{0,24},{4,28},{8,16},{12,20},{16,8},{20,12},{24,0},{28,4},{1,25},{... | collective-permute-start | bytes 350216 | tf_op jit(solution)/shard_map/ppermute | solution.py:846
  322.1 2.7 copy-start
  322.1 2.8 copy-start.2
  331.6 5.1 %copy-start.9 = (f32[1,7040]{1,0:T(1,128)S(1)}, f32[1,7040]{1,0:T(1,128)}, u32[]{:S(2)}) copy-start(f32[1,7040]{1,0:T(1,128)} %get-tuple-element.214) | copy-start | bytes 84484
  331.6 8.7 %copy-start.3 = (f32[1024,768]{1,0:T(8,128)S(1)}, f32[1024,768]{1,0:T(8,128)}, u32[]{:S(2)}) copy-start(f32[1024,768]{1,0:T(8,128)} %get-tuple-element.148) | copy-start | bytes 9437188
  331.6 5.0 %collective-permute-start.34 = (f32[1,7040]{1,0:T(1,128)}, f32[1,7040]{1,0:T(1,128)S(1)}, u32[]{:S(2)}, u32[]{:S(2)}) collective-permute-start(f32[1,7040]{1,0:T(1,128)} %get-tuple-element.214), channel_id=1, source_target_pairs={{0,1},{1,0},{2,3},{3,2},{4,5},{5,4},{6,7},{7,6},{8,9},{9,8},{10,11... | collective-permute-start | bytes 84488 | tf_op jit(solution)/shard_map/ppermute | solution.py:958
  331.6 5.0 %collective-permute-start.35 = (f32[1,7040]{1,0:T(1,128)}, f32[1,7040]{1,0:T(1,128)S(1)}, u32[]{:S(2)}, u32[]{:S(2)}) collective-permute-start(f32[1,7040]{1,0:T(1,128)} %get-tuple-element.214), channel_id=1, source_target_pairs={{0,2},{1,3},{2,0},{3,1},{4,6},{5,7},{6,4},{7,5},{8,10},{9,11},{10,... | collective-permute-start | bytes 84488 | tf_op jit(solution)/shard_map/ppermute | solution.py:958
  332.6 4.1 %collective-permute-start.36 = (f32[1,7040]{1,0:T(1,128)}, f32[1,7040]{1,0:T(1,128)S(1)}, u32[]{:S(2)}, u32[]{:S(2)}) collective-permute-start(f32[1,7040]{1,0:T(1,128)} %get-tuple-element.214), channel_id=1, source_target_pairs={{0,3},{1,2},{2,1},{3,0},{4,7},{5,6},{6,5},{7,4},{8,11},{9,10},{10,... | collective-permute-start | bytes 84488 | tf_op jit(solution)/shard_map/ppermute | solution.py:958
  336.8 5.8 %collective-permute-start.37 = (f32[1,7040]{1,0:T(1,128)S(1)}, f32[1,7040]{1,0:T(1,128)S(1)}, u32[]{:S(2)}, u32[]{:S(2)}) collective-permute-start(f32[1,7040]{1,0:T(1,128)S(1)} %add_add_fusion.1), channel_id=1, source_target_pairs={{0,4},{4,0},{8,12},{12,8},{16,20},{20,16},{24,28},{28,24},{1,5},{5... | collective-permute-start | bytes 84488 | tf_op jit(solution)/shard_map/ppermute | solution.py:958
  338.4 4.2 %collective-permute-start.38 = (f32[1,7040]{1,0:T(1,128)S(1)}, f32[1,7040]{1,0:T(1,128)S(1)}, u32[]{:S(2)}, u32[]{:S(2)}) collective-permute-start(f32[1,7040]{1,0:T(1,128)S(1)} %add_add_fusion.1), channel_id=1, source_target_pairs={{0,8},{4,12},{8,0},{12,4},{16,24},{20,28},{24,16},{28,20},{1,9},{5... | collective-permute-start | bytes 84488 | tf_op jit(solution)/shard_map/ppermute | solution.py:958
  340.2 4.8 %collective-permute-start.39 = (f32[1,7040]{1,0:T(1,128)S(1)}, f32[1,7040]{1,0:T(1,128)S(1)}, u32[]{:S(2)}, u32[]{:S(2)}) collective-permute-start(f32[1,7040]{1,0:T(1,128)S(1)} %add_add_fusion.1), channel_id=1, source_target_pairs={{0,12},{4,8},{8,4},{12,0},{16,28},{20,24},{24,20},{28,16},{1,13},{... | collective-permute-start | bytes 84488 | tf_op jit(solution)/shard_map/ppermute | solution.py:958
  345.0 4.8 %collective-permute-start.40 = (f32[1,7040]{1,0:T(1,128)S(1)}, f32[1,7040]{1,0:T(1,128)S(1)}, u32[]{:S(2)}, u32[]{:S(2)}) collective-permute-start(f32[1,7040]{1,0:T(1,128)S(1)} %add_add_fusion), channel_id=1, source_target_pairs={{0,16},{4,20},{8,24},{12,28},{16,0},{20,4},{24,8},{28,12},{1,17},{... | collective-permute-start | bytes 84488 | tf_op jit(solution)/shard_map/ppermute | solution.py:958
  (7 other events, 7.8 us)
Sparse Core Ops, SparseCore 0:
  11.0 114.7 all-gather.1
